TPU v7x, 256 devices: a whole 4x4x8 slice. The times are simulated.
256 devices in a mesh: group: 2 (over core), seq: 16 (over y, x), expert: 8 (over z).
Axes of the slice: x: 4, y: 4, z: 8, core: 2. Of those that a mesh axis runs over, the one named last changes fastest.
Arguments:
- q_pre: bfloat16 [2, 2048, 36864], P('group', 'seq', 'expert'), may hold values from -48 to 48
- prefix_cache: bfloat16 [2, 576, 2048], P('group', None, 'seq'), may hold values from -6 to 6
- span_cache: bfloat16 [2, 576, 2048], P('group', None, 'seq'), may hold values from -6 to 6
- prefix_len: int32 [2], P('group'), may hold values from 1 to 2048, as said below
- q_dec: bfloat16 [256, 36864], P(('group', 'seq'), 'expert'), may hold values from -48 to 48
- dec_cache: bfloat16 [256, 576, 128], P(('group', 'seq')), may hold values from -6 to 6
- cache_len: int32 [256], P(('group', 'seq')), may hold values from 1 to 128, as said below
- requests: int32 [256], P(('group', 'seq')), may hold values from 0 to 2
- w_uv: bfloat16 [64, 512, 128], P('expert'), may hold values from -0.25 to 0.25
- w_out: bfloat16 [8192, 7168], P('expert', 'seq'), may hold values from -0.0625 to 0.0625
- x_dec: bfloat16 [256, 7168], P(('group', 'expert'), 'seq'), may hold values from -3 to 3
- norm_gain: float32 [7168], replicated, may hold values from 0.5 to 1.5
- expert_ids: int32 [256, 8], P(('group', 'expert')), may hold values from 0 to 15, all different within a row; in each aligned block of 16 rows (0 to 15, 16 to 31, ...) at most 12 rows name the same one
- expert_gates: float32 [256, 8], P(('group', 'expert')), may hold values from 0.1 to 1
- w_in: bfloat16 [16, 2, 7168, 2048], P(('group', 'expert'), None, None, 'seq'), may hold values from -0.0625 to 0.0625
- w_down: bfloat16 [16, 2048, 7168], P(('group', 'expert'), 'seq'), may hold values from -0.125 to 0.125
Outputs:
- o_pre: bfloat16 [2, 2048, 32768], P('group', 'seq', 'expert')
- h_out: bfloat16 [256, 7168], P(('group', 'expert'), 'seq')
Inputs may be any that keep to these rules, and one draw needn't show every extreme that they name: `prefix_len`: the first prompt has all 2048 earlier columns valid. `cache_len`: every eighth decode row has all 128 resident columns valid. `expert_ids`: A row names 8 different experts; among the 16 rows of one aligned block no expert is named more than 12 times.
All inputs are finite; a program needn't handle non-finite values.
Results may differ from a plain program's by a relative error of at most 0.029.
Values may be sent and summed in bfloat16 or wider, within the bound.
No kernel may reach another device: no remote copies, remote signals or barrier semaphores. Data moves between devices by JAX's collectives and lax.ppermute only.
A program may use at most 192 MiB of HBM per device.

v0:
```python
import jax
import jax.numpy as jnp
from jax import lax
from jax.sharding import PartitionSpec as P

LATENT = 512
VDIM = 128


score_scale = 192.0 ** (-0.5)
epsilon = 1e-06


def fresh_state(count):
    return (
        jnp.full((count, 1), -1e30, jnp.float32),
        jnp.zeros((count, 1), jnp.float32),
        jnp.zeros((count, LATENT), jnp.float32),
    )


def absorb(state, scores, valid, weigh):
    running, total, weighted = state
    scores = jnp.where(valid, scores * score_scale, -jnp.inf)
    newest = jnp.maximum(running, jnp.max(scores, axis=-1, keepdims=True))
    probs = jnp.where(valid, jnp.exp(scores - newest), 0.0)
    factor = jnp.exp(running - newest)
    total = total * factor + jnp.sum(probs, axis=-1, keepdims=True)
    weighted = weighted * factor + weigh(probs.astype(jnp.bfloat16))
    return (newest, total, weighted)


def attend_keys(state, queries, keys, valid):
    scores = jnp.dot(queries, keys, preferred_element_type=jnp.float32)

    def weigh(probs):
        return lax.dot_general(
            probs, keys[:LATENT], (((1,), (1,)), ((), ())), preferred_element_type=jnp.float32
        )

    return absorb(state, scores, valid, weigh)


def resident_state(q_dec, dec_cache, cache_len, heads_here):
    rows_here, width, context = dec_cache.shape
    grouped = q_dec.reshape(rows_here, heads_here, width)
    scores = lax.dot_general(
        grouped, dec_cache, (((2,), (1,)), ((0,), (0,))), preferred_element_type=jnp.float32
    )
    scores = scores.reshape(rows_here * heads_here, context)
    valid = (
        jnp.repeat(cache_len, heads_here)[:, None] > jnp.arange(context, dtype=jnp.int32)[None, :]
    )

    def weigh(probs):
        shaped = probs.reshape(rows_here, heads_here, context)
        result = lax.dot_general(
            shaped,
            dec_cache[:, :LATENT],
            (((2,), (2,)), ((0,), (0,))),
            preferred_element_type=jnp.float32,
        )
        return result.reshape(rows_here * heads_here, LATENT)

    return absorb(fresh_state(rows_here * heads_here), scores, valid, weigh)


def on_device(
    q_pre,
    prefix_cache,
    span_cache,
    prefix_len,
    q_dec,
    dec_cache,
    cache_len,
    requests,
    w_uv,
    w_out,
    x_dec,
    norm_gain,
    expert_ids,
    expert_gates,
    w_in,
    w_down,
):
    width = span_cache.shape[1]
    heads_here = w_uv.shape[0]
    tokens_here = q_pre.shape[1]
    prefix_here = prefix_cache.shape[2]
    span_len = tokens_here * lax.axis_size("seq")
    queries = q_pre.reshape(tokens_here * heads_here, width)
    positions = jnp.repeat(
        lax.axis_index("seq") * tokens_here + jnp.arange(tokens_here, dtype=jnp.int32), heads_here
    )[:, None]
    valid_prefix = prefix_len[0]
    rows_here = q_dec.shape[0]
    dec_queries = q_dec.reshape(rows_here * heads_here, width)
    wanted = jnp.repeat(requests, heads_here)[:, None]
    state = resident_state(q_dec, dec_cache, cache_len, heads_here)
    joined = jnp.concatenate([prefix_cache, span_cache], axis=2)
    stride = prefix_here + tokens_here
    piece = lax.all_gather(joined, "seq", axis=2, tiled=True)
    index = jnp.arange(piece.shape[2], dtype=jnp.int32)
    shard = index // stride
    within = index % stride
    earlier = within < prefix_here
    place = jnp.where(
        earlier, shard * prefix_here + within, shard * tokens_here + within - prefix_here
    )
    valid = jnp.where(earlier[None, :], place[None, :] < valid_prefix, place[None, :] <= positions)
    prompt_state = attend_keys(fresh_state(queries.shape[0]), queries, piece[0], valid)
    piece = lax.all_gather(span_cache, ("group", "seq"), axis=2, tiled=True)
    index = jnp.arange(piece.shape[2], dtype=jnp.int32)
    state = attend_keys(state, dec_queries, piece[0], wanted == index[None, :] // span_len)
    o_pre = (
        (prompt_state[2] / prompt_state[1])
        .astype(jnp.bfloat16)
        .reshape(1, tokens_here, heads_here * LATENT)
    )
    dec_lat = (state[2] / state[1]).astype(jnp.bfloat16).reshape(rows_here, heads_here, LATENT)
    per_head = lax.dot_general(
        dec_lat, w_uv, (((2,), (1,)), ((1,), (0,))), preferred_element_type=jnp.float32
    )
    dec_val = (
        jnp.transpose(per_head, (1, 0, 2))
        .astype(jnp.bfloat16)
        .reshape(rows_here, heads_here * VDIM)
    )
    group_rows = lax.all_gather(dec_val, "seq", axis=0, tiled=True)
    block = x_dec.shape[0]
    attention = lax.psum_scatter(
        jnp.dot(group_rows, w_out, preferred_element_type=jnp.float32).astype(jnp.bfloat16),
        "expert",
        scatter_dimension=0,
        tiled=True,
    ).astype(jnp.float32)
    hidden = (x_dec.astype(jnp.float32) + attention).astype(jnp.bfloat16)
    full_rows = lax.all_gather(hidden, "seq", axis=1, tiled=True)
    wide = full_rows.astype(jnp.float32)
    normed = (
        wide * lax.rsqrt(jnp.mean(wide * wide, axis=1, keepdims=True) + epsilon) * norm_gain
    ).astype(jnp.bfloat16)
    experts = lax.axis_size("group") * lax.axis_size("expert")
    top_count = expert_ids.shape[1]
    capacity = max(block * top_count // experts, block * 3 // 4)
    chosen_mask = expert_ids[:, :, None] == jnp.arange(experts, dtype=jnp.int32)[None, None, :]
    hits = jnp.sum(chosen_mask.astype(jnp.int32), axis=1)
    gates = jnp.sum(jnp.where(chosen_mask, expert_gates[:, :, None], 0.0), axis=1)
    slots = jnp.cumsum(hits, axis=0) - hits
    placed = (hits.T[:, None, :] > 0) & (
        slots.T[:, None, :] == jnp.arange(capacity, dtype=jnp.int32)[None, :, None]
    )
    assign = placed.astype(jnp.bfloat16).reshape(experts * capacity, block)
    features = normed.shape[1]
    outgoing = (
        jnp.dot(assign, normed, preferred_element_type=jnp.float32)
        .astype(jnp.bfloat16)
        .reshape(experts, capacity, features)
    )
    combine_weights = (placed.astype(jnp.float32) * gates.T[:, None, :]).reshape(
        experts * capacity, block
    )
    arrived = lax.all_to_all(outgoing, ("group", "expert"), split_axis=0, concat_axis=0, tiled=True)
    sources, slots_now, feature_count = arrived.shape
    flat = arrived.reshape(sources * slots_now, feature_count)
    gate = jnp.dot(flat, w_in[0, 0], preferred_element_type=jnp.float32)
    upper = jnp.dot(flat, w_in[0, 1], preferred_element_type=jnp.float32)
    act = (jax.nn.silu(gate) * upper).astype(jnp.bfloat16)
    partial_out = jnp.dot(act, w_down[0], preferred_element_type=jnp.float32).reshape(
        sources, slots_now, feature_count
    )
    returned_full = lax.all_to_all(
        partial_out.astype(jnp.bfloat16),
        ("group", "expert"),
        split_axis=0,
        concat_axis=0,
        tiled=True,
    ).astype(partial_out.dtype)
    result = lax.psum_scatter(
        returned_full.astype(jnp.bfloat16), "seq", scatter_dimension=2, tiled=True
    ).astype(jnp.float32)
    flat_back = result.reshape(experts * capacity, result.shape[2])
    moe = lax.dot_general(
        combine_weights,
        flat_back,
        (((0,), (0,)), ((), ())),
        precision=lax.Precision.HIGHEST,
        preferred_element_type=jnp.float32,
    )
    h_out = (hidden.astype(jnp.float32) + moe).astype(jnp.bfloat16)
    return (o_pre, h_out)


def solution(mesh):
    return jax.shard_map(
        on_device,
        mesh=mesh,
        in_specs=(
            P("group", "seq", "expert"),
            P("group", None, "seq"),
            P("group", None, "seq"),
            P("group"),
            P(("group", "seq"), "expert"),
            P(("group", "seq"), None, None),
            P(("group", "seq")),
            P(("group", "seq")),
            P("expert", None, None),
            P("expert", "seq"),
            P(("group", "expert"), "seq"),
            P(),
            P(("group", "expert"), None),
            P(("group", "expert"), None),
            P(("group", "expert"), None, None, "seq"),
            P(("group", "expert"), "seq", None),
        ),
        out_specs=(P("group", "seq", "expert"), P(("group", "expert"), "seq")),
        check_vma=False,
    )
```

profile of v0, /device:TPU:1, one launch (start us, length us, event | category | flops | bytes accessed | tf_op | source)
XLA Modules:
  0.0 508.7 jit_solution(10435192290711156490)
XLA Ops:
  11.6 1.6 fusion.86
  15.2 55.9 %all-gather.6.cloned.1.call-done = bf16[1,576,4096]{2,1,0:T(8,128)(2,1)} async-done(((bf16[1,576,128]{2,1,0:T(8,128)(2,1)}), bf16[1,576,4096]{2,1,0:T(8,128)(2,1)}) %all-gather.6.cloned.1.call-update) | async-done | bytes 4718608 | tf_op jit(solution)/shard_map/all_gather | solution.py:112
  71.1 3.6 fusion.87
  77.3 17.6 %all_gather.14 = bf16[128,1024]{1,0:T(8,128)(2,1)S(1)} all-gather(bf16[8,1024]{1,0:T(8,128)(2,1)S(1)} %fusion.47), channel_id=1, replica_groups=mesh['group'=2,'seq'=16,'expert'=8] {'seq'}, dimensions={0}, use_global_device_ids=true | all-gather | bytes 278528 | tf_op jit(solution)/shard_map/all_gather | solution.py:129
  96.5 34.2 %reduce-scatter.5.cloned.1.call-done = bf16[16,448]{1,0:T(8,128)(2,1)} async-done(((bf16[128,448]{1,0:T(8,128)(2,1)}), bf16[16,448]{1,0:T(8,128)(2,1)}) %reduce-scatter.5.cloned.1.call-update) | async-done | bytes 14352 | tf_op jit(solution)/shard_map/reduce_scatter | solution.py:131
  131.5 18.5 %all-gather = bf16[16,448,16]{1,2,0:T(8,128)(2,1)S(1)} all-gather(bf16[1,448,16]{1,2,0:T(8,128)(2,1)S(1)} %fusion.81), channel_id=1, replica_groups=mesh['group'=2,'seq'=16,'expert'=8] {'seq'}, dimensions={0}, use_global_device_ids=true | all-gather | bytes 243712 | tf_op jit(solution)/shard_map/all_gather | solution.py:138
  150.6 2.5 convolution_convert_fusion.1
  153.0 4.4 reshape.245
  157.5 15.9 %all-to-all-start = ((bf16[16,12,7168]{2,1,0:T(8,128)(2,1)}), bf16[16,12,7168]{2,1,0:T(8,128)(2,1)}, u32[]{:S(2)}, u32[]{:S(2)}) async-start(bf16[16,12,7168]{2,1,0:T(8,128)(2,1)} %reshape.245), calls=%async_computation.1 | async-start | bytes 7340032 | tf_op jit(solution)/shard_map/all_to_all | solution.py:163
  174.3 81.0 %all-to-all-done = bf16[16,12,7168]{2,1,0:T(8,128)(2,1)} async-done(((bf16[16,12,7168]{2,1,0:T(8,128)(2,1)}), bf16[16,12,7168]{2,1,0:T(8,128)(2,1)}, u32[]{:S(2)}, u32[]{:S(2)}) %all-to-all-start) | async-done | bytes 2752544 | tf_op jit(solution)/shard_map/all_to_all | solution.py:163
  255.3 4.5 reshape.246
  259.7 3.4 fusion.17
  263.1 2.4 fusion.33
  266.4 3.4 copy.39
  269.8 6.2 %all-to-all-start.1 = ((bf16[16,12,7168]{2,1,0:T(8,128)(2,1)}), bf16[16,12,7168]{2,1,0:T(8,128)(2,1)}, u32[]{:S(2)}, u32[]{:S(2)}) async-start(bf16[16,12,7168]{2,1,0:T(8,128)(2,1)} %copy.39), calls=%async_computation.2 | async-start | bytes 7340032 | tf_op jit(solution)/shard_map/all_to_all | solution.py:172
  278.7 79.1 %all-to-all-done.1 = bf16[16,12,7168]{2,1,0:T(8,128)(2,1)} async-done(((bf16[16,12,7168]{2,1,0:T(8,128)(2,1)}), bf16[16,12,7168]{2,1,0:T(8,128)(2,1)}, u32[]{:S(2)}, u32[]{:S(2)}) %all-to-all-start.1) | async-done | bytes 2752544 | tf_op jit(solution)/shard_map/all_to_all | solution.py:172
  357.8 26.4 %copy.42 = bf16[16,12,7168]{0,1,2:T(8,128)(2,1)} copy(bf16[16,12,7168]{2,1,0:T(8,128)(2,1)} %all-to-all-done.1) | data formatting | bytes 5505024
  384.1 33.0 %reshape.252 = bf16[7168,192]{1,0:T(8,128)(2,1)} reshape(bf16[7168,12,16]{2,1,0:T(8,128)(2,1)} %bitcast.100) | data formatting | bytes 5505024
  417.2 11.5 %fusion = (f32[1024]{0:T(1024)S(1)}, f32[4096,1024]{1,0:T(8,128)S(1)}) fusion(s32[1024]{0:T(1024)S(1)} %le.16, s32[4096]{0:T(1024)S(1)} %add_select_fusion.1, pred[4096]{0:T(1024)(128)(4,1)S(1)} %get-tuple-element.16, pred[4096]{0:T(1024)(128)(4,1)S(1)} %get-tuple-element.15, bf16[1024,576]{1,0:T(8,128)(2,1)S(1)} %reshape.238, ...), kind=kOutput, calls=%fused_computation.3 | convolution fusion | flops 4852808704 | bytes 22708224 | tf_op jit(solution)/shard_map/dot_general | solution.py:34
  428.8 7.9 %fusion.85 = (f32[1024]{0:T(1024)S(1)}, bf16[1024,4096]{0,1:T(8,128)(2,1)S(1)}) fusion(f32[1024]{0:T(1024)S(1)} %broadcast_maximum_fusion.1, f32[4096,1024]{1,0:T(8,128)S(1)} %get-tuple-element.10, s32[1024]{0:T(1024)S(1)} %le.16, s32[4096]{0:T(1024)S(1)} %add_select_fusion.1, pred[4096]{0:T(1024)(128)(4,1)S(1)} %get-tuple-element.16, ...), kind=kLoop, calls=%fused_computation.110 | loop fusion | flops 33553408 | bytes 25202688 | tf_op jit(solution)/shard_map/reduce_sum | solution.py:28
  436.8 4.7 divide_convert_fusion
  442.8 52.0 %reduce-scatter.7.cloned.1.call-done = bf16[448,192]{1,0:T(8,128)(2,1)} async-done(((bf16[7168,192]{1,0:T(8,128)(2,1)}), bf16[448,192]{1,0:T(8,128)(2,1)}) %reduce-scatter.7.cloned.1.call-update) | async-done | bytes 172048
  494.8 3.2 reshape.253
  498.0 3.3 fusion.44
  (89 shorter events, 16.0 us)
Async XLA Ops:
  8.0 257.5 %copy-start = (bf16[1,128,7168]{2,1,0:T(8,128)(2,1)S(1)}, bf16[1,128,7168]{2,1,0:T(8,128)(2,1)}, u32[]{:S(2)}) copy-start(bf16[1,128,7168]{2,1,0:T(8,128)(2,1)} %param.31) | copy-start | bytes 5505028
  8.0 63.1 %all-gather.6.cloned.1.call-start = ((), (), s32[]{:S(2)}) async-start(), calls=%async_computation.5 | async-start | bytes 4866048 | tf_op jit(solution)/shard_map/all_gather | solution.py:112
  8.7 122.0 %reduce-scatter.5.cloned.1.call-start = ((), (), s32[]{:S(2)}) async-start(), calls=%async_computation.6 | async-start | bytes 147456 | tf_op jit(solution)/shard_map/reduce_scatter | solution.py:131
  71.1 4.0 copy-start.2
  74.7 1.9 copy-start.4
  74.7 1.9 copy-start.14
  75.1 1.9 copy-start.6
  75.1 19.7 %copy-start.7 = (bf16[1024,448]{0,1:T(8,128)(2,1)S(1)}, bf16[1024,448]{0,1:T(8,128)(2,1)}, u32[]{:S(2)}) copy-start(bf16[1024,448]{0,1:T(8,128)(2,1)} %param.25) | copy-start | bytes 2752516
  75.1 55.6 %copy-start.10 = (bf16[16,448]{1,0:T(8,128)(2,1)S(1)}, bf16[16,448]{1,0:T(8,128)(2,1)}, u32[]{:S(2)}) copy-start(bf16[16,448]{1,0:T(8,128)(2,1)} %param.26) | copy-start | bytes 43012
  76.6 74.0 %copy-start.12 = (f32[7168]{0:T(1024)S(1)}, f32[7168]{0:T(1024)}, u32[]{:S(2)}) copy-start(f32[7168]{0:T(1024)} %param.27) | copy-start | bytes 86020
  157.5 16.0 %copy-start.8 = (bf16[1,576,128]{2,1,0:T(8,128)(2,1)S(1)}, bf16[1,576,128]{2,1,0:T(8,128)(2,1)}, u32[]{:S(2)}) copy-start(bf16[1,576,128]{2,1,0:T(8,128)(2,1)} %param.18) | copy-start | bytes 442372
  157.5 16.0 %copy-start.9 = (bf16[1,576,128]{2,1,0:T(8,128)(2,1)S(1)}, bf16[1,576,128]{2,1,0:T(8,128)(2,1)}, u32[]{:S(2)}) copy-start(bf16[1,576,128]{2,1,0:T(8,128)(2,1)} %param.17) | copy-start | bytes 442372
  157.5 97.8 %all-to-all-start = ((bf16[16,12,7168]{2,1,0:T(8,128)(2,1)}), bf16[16,12,7168]{2,1,0:T(8,128)(2,1)}, u32[]{:S(2)}, u32[]{:S(2)}) async-start(bf16[16,12,7168]{2,1,0:T(8,128)(2,1)} %reshape.245), calls=%async_computation.1 | async-start | bytes 7340032 | tf_op jit(solution)/shard_map/all_to_all | solution.py:163
  173.4 243.8 %all-gather.4.cloned.1.call-start = ((), (), s32[]{:S(2)}) async-start(), calls=%async_computation.4 | async-start | bytes 5013504 | tf_op jit(solution)/shard_map/all_gather | solution.py:102
  259.7 3.4 copy-start.3
  269.8 6.4 %copy-start.13 = (f32[16,8]{0,1:T(8,128)S(1)}, f32[16,8]{0,1:T(8,128)}, u32[]{:S(2)}) copy-start(f32[16,8]{0,1:T(8,128)} %param.29) | copy-start | bytes 1540
  269.8 7.8 %copy-start.5 = (bf16[1,128,4608]{2,1,0:T(8,128)(2,1)S(1)}, bf16[1,128,4608]{2,1,0:T(8,128)(2,1)}, u32[]{:S(2)}) copy-start(bf16[1,128,4608]{2,1,0:T(8,128)(2,1)} %param.16) | copy-start | bytes 3538948
  269.8 88.0 %all-to-all-start.1 = ((bf16[16,12,7168]{2,1,0:T(8,128)(2,1)}), bf16[16,12,7168]{2,1,0:T(8,128)(2,1)}, u32[]{:S(2)}, u32[]{:S(2)}) async-start(bf16[16,12,7168]{2,1,0:T(8,128)(2,1)} %copy.39), calls=%async_computation.2 | async-start | bytes 7340032 | tf_op jit(solution)/shard_map/all_to_all | solution.py:172
  276.0 218.8 %reduce-scatter.7.cloned.1.call-start = ((), (), s32[]{:S(2)}) async-start(), calls=%async_computation.7 | async-start | bytes 3899392
  428.8 7.9 %copy-start.15 = (bf16[1,576,4096]{2,1,0:T(8,128)(2,1)S(1)}, bf16[1,576,4096]{2,1,0:T(8,128)(2,1)}, u32[]{:S(2)}) copy-start(bf16[1,576,4096]{2,1,0:T(8,128)(2,1)} %all-gather.4.cloned.1.call-done) | copy-start | bytes 14155780
  436.7 61.2 %copy-start.11 = (bf16[16,448]{1,0:T(8,128)(2,1)S(1)}, bf16[16,448]{1,0:T(8,128)(2,1)}, u32[]{:S(2)}) copy-start(bf16[16,448]{1,0:T(8,128)(2,1)} %reduce-scatter.5.cloned.1.call-done) | copy-start | bytes 43012
  436.7 64.5 %copy-start.1 = (bf16[1,128,7168]{2,1,0:T(8,128)(2,1)S(1)}, bf16[1,128,7168]{2,1,0:T(8,128)(2,1)}, u32[]{:S(2)}) copy-start(bf16[1,128,7168]{2,1,0:T(8,128)(2,1)} %param.31) | copy-start | bytes 5505028
Sparse Core Ops, SparseCore 0:
  11.3 59.7 all-gather.5
  96.1 34.6 reduce-scatter.4
Sparse Core Ops, SparseCore 1:
  176.9 62.4 all-gather.3
  417.3 77.4 reduce-scatter.6
where the time goes:
time: 511 us; the launch traced here: 509 us
  waiting for transfers between devices  303 us (59%)
  local copies, waits for them, and re-layouts  82.4 us (16%)
  matrix products  37 us (7%)
  blocking collectives  36.1 us (7%)
  starting transfers between devices  22.5 us (4%)
  between operations  16.6 us (3%)
  other arithmetic  11.2 us (2%)
    all_to_all x1, waiting for transfers between devices, on_device(): lax.all_to_all(outgoing, ('group', 'expert'), split_axis=0, concat_axis=0...  81 us
    all_to_all x1, waiting for transfers between devices, on_device(): lax.all_to_all(partial_out.astype(jnp.bfloat16), ('group', 'expert'), spl...  79.1 us
    unnamed x37, local copies, waits for them, and re-layouts  63.5 us
    all_gather x1, waiting for transfers between devices, on_device(): piece = lax.all_gather(span_cache, ('group', 'seq'), axis=2, tiled=True)  55.9 us
    unnamed x5, waiting for transfers between devices  52.8 us
    reduce_scatter x1, waiting for transfers between devices, on_device(): lax.psum_scatter(jnp.dot(group_rows, w_out, preferred_element_type=jnp.fl...  34.2 us
    all_gather x1, blocking collectives, on_device(): full_rows = lax.all_gather(hidden, 'seq', axis=1, tiled=True)  18.5 us
    all_gather x1, blocking collectives, on_device(): group_rows = lax.all_gather(dec_val, 'seq', axis=0, tiled=True)  17.6 us
  transfers between devices with their start and end apart: 6, of which 5 were waited for; matrix products, arithmetic and copies ran while one was open for 21% of the time, Pallas kernels for 0%

commit v1 on v0

v1 whole, which is shorter than its diff:
```python
import functools

import jax
import jax.numpy as jnp
from jax import lax
from jax.experimental import pallas as pl
from jax.experimental.pallas import tpu as pltpu
from jax.sharding import PartitionSpec as P

LATENT = 512
VDIM = 128
SIDE = 4
CAP = 12

bf16 = jnp.bfloat16
f32 = jnp.float32
score_scale = 192.0 ** (-0.5)
epsilon = 1e-06
LOW = -1e30

VMEM = pl.BlockSpec(memory_space=pltpu.VMEM)
SMEM = pl.BlockSpec(memory_space=pltpu.SMEM)


def call(kernel, out_shape, ins, scratch=(), cost=None, limit=48 << 20):
    multi = isinstance(out_shape, (tuple, list))
    return pl.pallas_call(
        kernel,
        out_shape=out_shape,
        in_specs=[SMEM] + [VMEM] * (len(ins) - 1),
        out_specs=[VMEM] * len(out_shape) if multi else VMEM,
        scratch_shapes=list(scratch),
        compiler_params=pltpu.CompilerParams(vmem_limit_bytes=limit),
        cost_estimate=cost,
    )(*ins)


def nn(a, b):
    return jnp.dot(a, b, preferred_element_type=f32)


def nt(a, b):
    return lax.dot_general(a, b, (((1,), (1,)), ((), ())), preferred_element_type=f32)


def tn(a, b):
    return lax.dot_general(a, b, (((0,), (0,)), ((), ())), preferred_element_type=f32)


def split3(v):
    high = v.astype(bf16).astype(f32)
    rest = v - high
    mid = rest.astype(bf16).astype(f32)
    return high, mid, (rest - mid).astype(bf16).astype(f32)


def along_x(array):
    return [array] + [
        lax.ppermute(
            array,
            "seq",
            [(y * SIDE + x, y * SIDE + (x + d) % SIDE) for y in range(SIDE) for x in range(SIDE)],
        )
        for d in range(1, SIDE)
    ]


def along_y(array):
    return [array] + [
        lax.ppermute(
            array,
            "seq",
            [(y * SIDE + x, (y + d) % SIDE * SIDE + x) for y in range(SIDE) for x in range(SIDE)],
        )
        for d in range(1, SIDE)
    ]


def other_core(array):
    return lax.ppermute(array, "group", [(0, 1), (1, 0)])


def everyone(array, axis, count):
    return lax.all_to_all(
        jnp.broadcast_to(array[None], (count,) + array.shape), axis, 0, 0, tiled=True
    )


def resident_kernel(lens, q_ref, cache_ref, m_ref, l_ref, w_ref):
    count = cache_ref.shape[0]
    queries = q_ref[:, :576]
    row = lax.rem(lax.broadcasted_iota(jnp.int32, (queries.shape[0], 128), 0), count)
    column = lax.broadcasted_iota(jnp.int32, (queries.shape[0], 128), 1)
    scores = []
    for r in range(count):
        s = nn(queries, cache_ref[r]) * score_scale
        scores.append(jnp.where((row == r) & (column < lens[r]), s, LOW))
    top = scores[0]
    for s in scores[1:]:
        top = jnp.maximum(top, s)
    m = jnp.max(top, axis=1, keepdims=True)
    total = jnp.zeros_like(top)
    weighted = jnp.zeros((queries.shape[0], LATENT), f32)
    for r in range(count):
        p = jnp.where((row == r) & (column < lens[r]), jnp.exp(scores[r] - m), 0.0)
        total += p
        weighted += nt(p.astype(bf16), cache_ref[r, :LATENT])
    m_ref[...] = m
    l_ref[...] = jnp.sum(total, axis=1, keepdims=True)
    w_ref[...] = weighted


def span_kernel(
    info, q0, q1, q2, q3, k0, k1, k2, k3, kp, w_uv, rm, rl, rw, out_ref, scr
):
    group = info[0].astype(f32)
    y = info[1]
    packed = jnp.concatenate([q0[...], q1[...], q2[...], q3[...]], axis=0)
    queries = packed[:, :576]
    wanted = packed[:, 576:577].astype(f32)
    own_keys = jnp.concatenate([k0[...], k1[...], k2[...], k3[...]], axis=1)
    far_keys = jnp.concatenate([kp[0], kp[1], kp[2], kp[3]], axis=1)
    own = wanted == group
    valid = wanted < 1.5
    s = jnp.where(own, nn(queries, own_keys), nn(queries, far_keys)) * score_scale
    m = jnp.where(valid, jnp.max(s, axis=1, keepdims=True), LOW)
    p = jnp.where(valid, jnp.exp(s - m), 0.0)
    total = jnp.sum(p, axis=1, keepdims=True)
    weighted = nt(jnp.where(own, p, 0.0).astype(bf16), own_keys[:LATENT]) + nt(
        jnp.where(own, 0.0, p).astype(bf16), far_keys[:LATENT]
    )
    here = q0.shape[0]
    newest = jnp.maximum(m[:here], rm[...])
    a = jnp.exp(m[:here] - newest)
    b = jnp.exp(rm[...] - newest)
    m = jnp.concatenate([newest, m[here:]], axis=0)
    total = jnp.concatenate([total[:here] * a + rl[...] * b, total[here:]], axis=0)
    weighted = jnp.concatenate([weighted[:here] * a + rw[...] * b, weighted[here:]], axis=0)
    some = total > 0.0
    safe = jnp.where(some, total, 1.0)
    latent = (weighted / safe).reshape(SIDE, 8, 8, LATENT)
    level = jnp.where(some, m + jnp.log(safe), LOW).reshape(SIDE, 8, 8, 1)
    lane = lax.broadcasted_iota(jnp.int32, (SIDE, 8, 128), 2)
    tail = jnp.zeros((SIDE, 8, 128), f32)
    places = [lax.rem(y - d + SIDE, SIDE) for d in range(SIDE)]
    for h in range(8):
        rows = latent[:, h].reshape(SIDE * 8, LATENT).astype(bf16)
        value = nn(rows, w_uv[h])
        for d in range(SIDE):
            scr[places[d], :, h * VDIM : (h + 1) * VDIM] = value[d * 8 : (d + 1) * 8]
        for part, v in enumerate(split3(level[:, h])):
            tail = jnp.where(lane == part * 8 + h, v, tail)
    for d in range(SIDE):
        scr[places[d], :, 8 * VDIM :] = tail[d]
    out_ref[...] = scr[...].reshape(SIDE * 8, 9 * VDIM).astype(bf16)


def merge_kernel(info, p0, p1, p2, p3, out_ref):
    parts = [p0, p1, p2, p3]
    levels = []
    for p in parts:
        tail = p[:, 8 * VDIM :].astype(f32)
        levels.append(tail[:, 0:8] + tail[:, 8:16] + tail[:, 16:24])
    top = functools.reduce(jnp.maximum, levels)
    weights = [jnp.exp(v - top) for v in levels]
    total = functools.reduce(jnp.add, weights)
    weights = [w / total for w in weights]
    for h in range(8):
        cut = slice(h * VDIM, (h + 1) * VDIM)
        value = sum(p[:, cut].astype(f32) * w[:, h : h + 1] for p, w in zip(parts, weights))
        out_ref[:, cut] = value.astype(bf16)


def project_kernel(info, x0, x1, x2, x3, w_out, out_ref, scr):
    x = info[2]
    rows = jnp.concatenate([x0[...], x1[...], x2[...], x3[...]], axis=0)
    product = nn(rows, w_out[...])
    for d in range(SIDE):
        place = lax.rem(x - d + SIDE, SIDE)
        for y in range(SIDE):
            at = (d * SIDE + y) * 8
            scr[y, place] = product[at : at + 8]
    out_ref[...] = scr[...].reshape(out_ref.shape).astype(bf16)


def dispatch_kernel(info, rows_ref, gain_ref, out_ref, place_ref, gate_ref, scr):
    expert = info[3].astype(f32)
    count, block = rows_ref.shape[0], 16
    features = gain_ref.shape[1]
    hidden = rows_ref[:, :features].astype(f32)
    extra = rows_ref[:, features:].astype(f32)
    hit = extra[:, 0:8] == expert
    mask = jnp.sum(jnp.where(hit, 1.0, 0.0), axis=1, keepdims=True)
    gates = extra[:, 8:16] + extra[:, 16:24] + extra[:, 24:32]
    gate_ref[...] = jnp.sum(jnp.where(hit, gates, 0.0), axis=1, keepdims=True)
    j = lax.broadcasted_iota(jnp.int32, (count, count), 0)
    k = lax.broadcasted_iota(jnp.int32, (count, count), 1)
    before = jnp.where((k < j) & (k // block == j // block), 1.0, 0.0).astype(bf16)
    slot = nn(before, jnp.broadcast_to(mask, (count, 128)).astype(bf16))[:, 0:1]
    j = lax.broadcasted_iota(jnp.int32, (count, out_ref.shape[0]), 0)
    i = lax.broadcasted_iota(jnp.int32, (count, out_ref.shape[0]), 1)
    target = slot.astype(jnp.int32) + CAP * (j // block)
    place = jnp.where((mask > 0.5) & (target == i), 1.0, 0.0).astype(bf16)
    place_ref[...] = place
    scr[:, :features] = (hidden * gain_ref[...]).astype(bf16)
    squares = jnp.sum(hidden * hidden, axis=1, keepdims=True)
    lane = lax.broadcasted_iota(jnp.int32, extra.shape, 1)
    tail = jnp.zeros(extra.shape, f32)
    for part, v in enumerate(split3(squares)):
        tail = jnp.where(lane == part, v, tail)
    scr[:, features:] = tail.astype(bf16)
    out_ref[...] = tn(place, scr[...]).astype(bf16)


def expert_kernel(info, x_ref, w_ref, act_ref):
    shards, rows, _ = x_ref.shape
    features = w_ref.shape[2]
    gate = jnp.zeros((rows, 128), f32)
    upper = jnp.zeros((rows, 128), f32)
    squares = jnp.zeros((rows, 1), f32)
    for s in range(shards):
        x = x_ref[s, :, :features]
        gate += nn(x, w_ref[0, s])
        upper += nn(x, w_ref[1, s])
        tail = x_ref[s, :, features:].astype(f32)
        squares += tail[:, 0:1] + tail[:, 1:2] + tail[:, 2:3]
    factor = lax.rsqrt(squares * (1.0 / (shards * features)) + epsilon)
    gate = gate * factor
    act_ref[...] = (gate * (1.0 / (1.0 + jnp.exp(-gate))) * (upper * factor)).astype(bf16)


def down_kernel(info, act_ref, w_ref, place_ref, gate_ref, near_ref, far_ref):
    shards, rows, _ = act_ref.shape
    total = jnp.zeros((rows, w_ref.shape[2]), f32)
    for s in range(shards):
        total += nn(act_ref[s], w_ref[s])
    high = total.astype(bf16)
    low = (total - high.astype(f32)).astype(bf16)
    place = place_ref[...]
    share = (nn(place, high) + nn(place, low)) * gate_ref[...]
    share = share.reshape(8, 2, 16, share.shape[1])
    near_ref[...] = share[:, 0].reshape(near_ref.shape)
    far_ref[...] = share[:, 1].reshape(far_ref.shape).astype(bf16)


def prompt_kernel(info, q_ref, keys_ref, out_ref, scores, probs):
    pieces = keys_ref.shape[0]
    tokens = q_ref.shape[0]
    me, prefix_len = info[4], info[5]
    queries = jnp.concatenate([q_ref[:, :576], q_ref[:, 576:1152]], axis=0)
    rows = queries.shape[0]
    lane = lax.broadcasted_iota(jnp.int32, (rows, 128), 1)
    token = lax.rem(lax.broadcasted_iota(jnp.int32, (rows, 128), 0), tokens)

    def score(j, top):
        early = nn(queries, keys_ref[j, 0])
        late = nn(queries, keys_ref[j, 1])
        early = jnp.where(lane < prefix_len - j * 128, early, LOW)
        late = jnp.where(lane - token <= (me - j) * tokens, late, LOW)
        scores[j, :, :128] = early
        scores[j, :, 128:] = late
        return jnp.maximum(top, jnp.maximum(early, late))

    top = lax.fori_loop(0, pieces, score, jnp.full((rows, 128), LOW, f32))
    top = jnp.max(top, axis=1, keepdims=True)

    def weigh(j, carry):
        total, weighted = carry
        p = jnp.exp((scores[j] - top) * score_scale)
        keys = jnp.concatenate([keys_ref[j, 0, :LATENT], keys_ref[j, 1, :LATENT]], axis=1)
        return total + (p[:, :128] + p[:, 128:]), weighted + nt(p.astype(bf16), keys)

    total, weighted = lax.fori_loop(
        0, pieces, weigh, (jnp.zeros((rows, 128), f32), jnp.zeros((rows, LATENT), f32))
    )
    result = (weighted / jnp.sum(total, axis=1, keepdims=True)).astype(bf16)
    out_ref[:, :LATENT] = result[:tokens]
    out_ref[:, LATENT:] = result[tokens:]


def prompt_attention(info, queries, keys):
    tokens, width = queries.shape
    pairs = width // 1152
    return pl.pallas_call(
        prompt_kernel,
        out_shape=jax.ShapeDtypeStruct((tokens, pairs * 2 * LATENT), bf16),
        grid=(pairs,),
        in_specs=[
            SMEM,
            pl.BlockSpec((tokens, 1152), lambda i: (0, i)),
            pl.BlockSpec(keys.shape, lambda i: (0, 0, 0, 0)),
        ],
        out_specs=pl.BlockSpec((tokens, 2 * LATENT), lambda i: (0, i)),
        scratch_shapes=[
            pltpu.VMEM((keys.shape[0], 2 * tokens, 256), f32),
            pltpu.VMEM((8, 128), f32),
        ],
        compiler_params=pltpu.CompilerParams(vmem_limit_bytes=48 << 20),
        cost_estimate=pl.CostEstimate(
            flops=2 * 8 * tokens * 4096 * 1088, bytes_accessed=8 << 20, transcendentals=8 * tokens * 4096
        ),
    )(info, queries, keys)


def on_device(
    q_pre,
    prefix_cache,
    span_cache,
    prefix_len,
    q_dec,
    dec_cache,
    cache_len,
    requests,
    w_uv,
    w_out,
    x_dec,
    norm_gain,
    expert_ids,
    expert_gates,
    w_in,
    w_down,
):
    group = lax.axis_index("group")
    seq = lax.axis_index("seq")
    z = lax.axis_index("expert")
    shards = lax.axis_size("seq")
    depth = lax.axis_size("expert")
    info = jnp.stack(
        [group, seq // SIDE, seq % SIDE, group * depth + z, seq, prefix_len[0], z, z]
    ).astype(jnp.int32)
    features = x_dec.shape[1]

    keys = lax.all_gather(jnp.concatenate([prefix_cache, span_cache], axis=0), "seq", axis=0)

    span = span_cache[0]
    q64 = jnp.transpose(q_dec.reshape(8, 8, 576), (1, 0, 2)).reshape(64, 576)
    wanted = jnp.tile(requests.astype(bf16), 8)[:, None]
    packet = jnp.concatenate([q64, jnp.broadcast_to(wanted, (64, 64))], axis=1)
    packets = along_y(packet)
    pieces = along_x(span)
    far = other_core(jnp.stack(pieces))
    rm, rl, rw = call(
        resident_kernel,
        [
            jax.ShapeDtypeStruct((64, 1), f32),
            jax.ShapeDtypeStruct((64, 1), f32),
            jax.ShapeDtypeStruct((64, LATENT), f32),
        ],
        [cache_len, packet, dec_cache],
    )
    part = call(
        span_kernel,
        jax.ShapeDtypeStruct((32, 9 * VDIM), bf16),
        [info, *packets, *pieces, far, w_uv, rm, rl, rw],
        [pltpu.VMEM((SIDE, 8, 9 * VDIM), f32)],
    )
    dec_val = call(
        merge_kernel, jax.ShapeDtypeStruct((32, 8 * VDIM), bf16), [info, *along_y(part)]
    )
    product = call(
        project_kernel,
        jax.ShapeDtypeStruct((128, features), bf16),
        [info, *along_x(dec_val), w_out],
        [pltpu.VMEM((SIDE, SIDE, 8, features), f32)],
    )
    terms = lax.all_to_all(product.reshape(depth, 16, features), "expert", 0, 0, tiled=True)
    hidden = (x_dec.astype(f32) + jnp.sum(terms.astype(f32), axis=0)).astype(bf16)

    g_high = lax.reduce_precision(expert_gates, 8, 7)
    g_mid = lax.reduce_precision(expert_gates - g_high, 8, 7)
    g_low = lax.reduce_precision(expert_gates - g_high - g_mid, 8, 7)
    packed = jnp.concatenate(
        [hidden]
        + [v.astype(bf16) for v in (expert_ids, g_high, g_mid, g_low)]
        + [jnp.zeros((16, 32), bf16)],
        axis=1,
    )
    both = jnp.stack([packed, other_core(packed)])
    rows = everyone(both, "expert", depth).reshape(256, features + 64)
    gain = lax.dynamic_slice(norm_gain, (seq * features,), (features,))[None]
    chosen, place, gate = call(
        dispatch_kernel,
        [
            jax.ShapeDtypeStruct((16 * CAP, features + 64), bf16),
            jax.ShapeDtypeStruct((256, 16 * CAP), bf16),
            jax.ShapeDtypeStruct((256, 1), f32),
        ],
        [info, rows, gain],
        [pltpu.VMEM((256, features + 64), bf16)],
    )
    arrived = everyone(chosen, "seq", shards)
    act = call(
        expert_kernel,
        jax.ShapeDtypeStruct((16 * CAP, 128), bf16),
        [info, arrived, w_in[0].reshape(2, shards, features, 128)],
    )
    w_back = lax.all_to_all(
        jnp.transpose(w_down[0].reshape(128, shards, features), (1, 0, 2)), "seq", 0, 0, tiled=True
    )
    acts = everyone(act, "seq", shards)
    near, far_share = call(
        down_kernel,
        [
            jax.ShapeDtypeStruct((128, features), f32),
            jax.ShapeDtypeStruct((128, features), bf16),
        ],
        [info, acts, w_back, place, gate],
    )
    share = (near + other_core(far_share).astype(f32)).astype(bf16)
    shares = lax.all_to_all(share.reshape(depth, 16, features), "expert", 0, 0, tiled=True)
    h_out = (hidden.astype(f32) + jnp.sum(shares.astype(f32), axis=0)).astype(bf16)

    o_pre = prompt_attention(info, q_pre[0], keys)[None]
    return (o_pre, h_out)


def solution(mesh):
    return jax.shard_map(
        on_device,
        mesh=mesh,
        in_specs=(
            P("group", "seq", "expert"),
            P("group", None, "seq"),
            P("group", None, "seq"),
            P("group"),
            P(("group", "seq"), "expert"),
            P(("group", "seq"), None, None),
            P(("group", "seq")),
            P(("group", "seq")),
            P("expert", None, None),
            P("expert", "seq"),
            P(("group", "expert"), "seq"),
            P(),
            P(("group", "expert"), None),
            P(("group", "expert"), None),
            P(("group", "expert"), None, None, "seq"),
            P(("group", "expert"), "seq", None),
        ),
        out_specs=(P("group", "seq", "expert"), P(("group", "expert"), "seq")),
        check_vma=False,
    )
```

time: 511 us -> 275 us (0.54)
  waiting for transfers between devices: 303 us -> 108 us
  local copies, waits for them, and re-layouts: 82.4 us -> 20.9 us
  Pallas kernels: 0 us -> 58 us
  matrix products: 37 us -> 0 us
  starting transfers between devices: 22.5 us -> 56.1 us
  blocking collectives: 36.1 us -> 10.8 us
  other arithmetic: 11.2 us -> 5.39 us
    all_to_all x2 -> x5, waiting for transfers between devices: 160 us -> 92.5 us  [the longest x3 64.8 us: everyone(): lax.all_to_all(jnp.broadcast_to(array[None], (count,) + array.shape), axi...]
    pallas_call x0 -> x8, Pallas kernels: none -> 58 us  [the longest x1 44.6 us: prompt_attention(): pl.pallas_call(prompt_kernel, out_shape=jax.ShapeDtypeStruct((tokens, pai...]
    all_gather x2 -> x1, waiting for transfers between devices: 55.9 us -> 0.01 us  [on_device(): lax.all_gather(jnp.concatenate([prefix_cache, span_cache], axis=0), 'seq'...]
    unnamed x5 -> x1, waiting for transfers between devices: 52.8 us -> 0.02 us
    unnamed x37 -> x30, local copies, waits for them, and re-layouts: 63.5 us -> 11.2 us
    dot_general x13 -> x0, matrix products: 37 us -> none  [the longest x2 15.1 us: attend_keys(): scores = jnp.dot(queries, keys, preferred_element_type=jnp.float32)]
    all_gather x2 -> x0, blocking collectives: 36.1 us -> none  [the longest x1 18.5 us: on_device(): full_rows = lax.all_gather(hidden, 'seq', axis=1, tiled=True)]
    reduce_scatter x1 -> x0, waiting for transfers between devices: 34.2 us -> none  [on_device(): lax.psum_scatter(jnp.dot(group_rows, w_out, preferred_element_type=jnp.fl...]
  transfers between devices with their start and end apart: 6 -> 21, of which waited for: 5 -> 13; matrix products, arithmetic and copies ran while one was open for 21% -> 7% of each run, Pallas kernels for 0% -> 5%
where the time goes in v1:
time: 275 us; the launch traced here: 274 us
  waiting for transfers between devices  108 us (39%)
  Pallas kernels  58 us (21%)
  starting transfers between devices  56.1 us (20%)
  local copies, waits for them, and re-layouts  20.9 us (8%)
  between operations  15 us (5%)
  blocking collectives  10.8 us (4%)
  other arithmetic  5.39 us (2%)
    all_to_all x3, waiting for transfers between devices, everyone(): lax.all_to_all(jnp.broadcast_to(array[None], (count,) + array.shape), axi...  64.8 us
    pallas_call x1, Pallas kernels, prompt_attention(): pl.pallas_call(prompt_kernel, out_shape=jax.ShapeDtypeStruct((tokens, pai...  44.6 us
    all_to_all x1, waiting for transfers between devices, on_device(): lax.all_to_all(jnp.transpose(w_down[0].reshape(128, shards, features), (1...  20 us
    all_to_all x3, starting transfers between devices, everyone(): lax.all_to_all(jnp.broadcast_to(array[None], (count,) + array.shape), axi...  15.5 us
    pallas_call x7, Pallas kernels, call(): pl.pallas_call(kernel, out_shape=out_shape, in_specs=[SMEM] + [VMEM] * (l...  13.4 us
    unnamed x30, local copies, waits for them, and re-layouts  11.2 us
    ppermute x6, starting transfers between devices, along_x(): lax.ppermute(array, 'seq', [(y * SIDE + x, y * SIDE + (x + d) % SIDE) for...  11.1 us
    all_to_all x1, blocking collectives, on_device(): lax.all_to_all(share.reshape(depth, 16, features), 'expert', 0, 0, tiled=...  10.8 us
  transfers between devices with their start and end apart: 21, of which 13 were waited for; matrix products, arithmetic and copies ran while one was open for 7% of the time, Pallas kernels for 5%

profile of v1, /device:TPU:1, one launch (start us, length us, event | category | flops | bytes accessed | tf_op | source)
XLA Modules:
  0.0 273.7 jit_solution(3035568140821934612)
XLA Ops:
  11.3 2.5 collective-permute-start.4
  15.3 5.1 %collective-permute-done.4.k2 = bf16[576,128]{1,0:T(8,128)(2,1)S(1)} collective-permute-done((bf16[576,128]{1,0:T(8,128)(2,1)}, bf16[576,128]{1,0:T(8,128)(2,1)S(1)}, u32[]{:S(2)}, u32[]{:S(2)}) %collective-permute-start.4) | collective-permute-done | bytes 147488 | tf_op jit(solution)/shard_map/ppermute | solution.py:59
  27.8 2.6 collective-permute-start.1
  35.0 2.4 collective-permute-done.1.q2
  38.3 2.4 shard_map.169.p0
  43.5 3.1 %collective-permute-done.7.p1 = bf16[32,1152]{1,0:T(8,128)(2,1)S(1)} collective-permute-done((bf16[32,1152]{1,0:T(8,128)(2,1)S(1)}, bf16[32,1152]{1,0:T(8,128)(2,1)S(1)}, u32[]{:S(2)}, u32[]{:S(2)}) %collective-permute-start.7) | collective-permute-done | bytes 73760 | tf_op jit(solution)/shard_map/ppermute | solution.py:70
  58.2 8.5 %all-to-all-start = ((bf16[8,16,448]{2,1,0:T(8,128)(2,1)}), bf16[8,16,448]{2,1,0:T(8,128)(2,1)S(1)}, u32[]{:S(2)}, u32[]{:S(2)}) async-start(bf16[8,16,448]{2,1,0:T(8,128)(2,1)} %bitcast.15), calls=%async_computation | async-start | bytes 262144 | tf_op jit(solution)/shard_map/all_to_all | solution.py:366
  67.1 7.7 %all-to-all-done = bf16[8,16,448]{2,1,0:T(8,128)(2,1)S(1)} async-done(((bf16[8,16,448]{2,1,0:T(8,128)(2,1)}), bf16[8,16,448]{2,1,0:T(8,128)(2,1)S(1)}, u32[]{:S(2)}, u32[]{:S(2)}) %all-to-all-start) | async-done | bytes 114720 | tf_op jit(solution)/shard_map/all_to_all | solution.py:366
  74.9 4.6 %collective-permute-start.13 = (bf16[16,512]{1,0:T(8,128)(2,1)S(1)}, bf16[16,512]{1,0:T(8,128)(2,1)S(1)}, u32[]{:S(2)}, u32[]{:S(2)}) collective-permute-start(bf16[16,512]{1,0:T(8,128)(2,1)S(1)} %concatenate.11), channel_id=1, source_target_pairs={{0,128},{128,0},{1,129},{129,1},{2,130},{130,2},{3,131},{131,3},{4... | collective-permute-start | bytes 49160 | tf_op jit(solution)/shard_map/ppermute | solution.py:80
  81.0 3.4 %all-to-all-start.1 = ((bf16[8,2,16,512]{3,2,1,0:T(8,128)(2,1)}), bf16[8,2,16,512]{3,2,1,0:T(8,128)(2,1)S(1)}, u32[]{:S(2)}, u32[]{:S(2)}) async-start(bf16[8,2,16,512]{3,2,1,0:T(8,128)(2,1)} %broadcast_in_dim.38), calls=%async_computation.1 | async-start | bytes 524288 | tf_op jit(solution)/shard_map/all_to_all | solution.py:84
  85.3 11.5 %all-to-all-done.1 = bf16[8,2,16,512]{3,2,1,0:T(8,128)(2,1)S(1)} async-done(((bf16[8,2,16,512]{3,2,1,0:T(8,128)(2,1)}), bf16[8,2,16,512]{3,2,1,0:T(8,128)(2,1)S(1)}, u32[]{:S(2)}, u32[]{:S(2)}) %all-to-all-start.1) | async-done | bytes 262176 | tf_op jit(solution)/shard_map/all_to_all | solution.py:84
  100.0 5.7 %all-to-all-start.2 = ((bf16[16,192,512]{2,1,0:T(8,128)(2,1)}), bf16[16,192,512]{2,1,0:T(8,128)(2,1)S(1)}, u32[]{:S(2)}, u32[]{:S(2)}) async-start(bf16[16,192,512]{2,1,0:T(8,128)(2,1)} %broadcast_in_dim.40), calls=%async_computation.2 | async-start | bytes 6291456 | tf_op jit(solution)/shard_map/all_to_all | solution.py:84
  105.7 3.9 %copy.43 = bf16[1,128,7168]{1,2,0:T(8,128)(2,1)} copy(bf16[1,128,7168]{2,1,0:T(8,128)(2,1)} %param.31) | data formatting | bytes 3670016 | tf_op args[15]
  109.6 43.4 %all-to-all-done.2.x_ref = bf16[16,192,512]{2,1,0:T(8,128)(2,1)S(1)} async-done(((bf16[16,192,512]{2,1,0:T(8,128)(2,1)}), bf16[16,192,512]{2,1,0:T(8,128)(2,1)S(1)}, u32[]{:S(2)}, u32[]{:S(2)}) %all-to-all-start.2) | async-done | bytes 3145760 | tf_op jit(solution)/shard_map/all_to_all | solution.py:84
  153.0 4.4 %all-to-all-start.4 = ((bf16[16,128,448]{1,2,0:T(8,128)(2,1)}), bf16[16,128,448]{1,2,0:T(8,128)(2,1)}, u32[]{:S(2)}, u32[]{:S(2)}) async-start(bf16[16,128,448]{1,2,0:T(8,128)(2,1)} %bitcast.39), calls=%async_computation.4 | async-start | bytes 3670016 | tf_op jit(solution)/shard_map/all_to_all | solution.py:397
  157.4 4.1 %shard_map.173 = bf16[192,128]{1,0:T(8,128)(2,1)S(1)} custom-call(s32[8]{0:T(128)S(1)} %copy-done.6, bf16[16,192,512]{2,1,0:T(8,128)(2,1)S(1)} %all-to-all-done.2.x_ref, bf16[2,16,448,128]{3,2,1,0:T(8,128)(2,1)} %bitcast.40), custom_call_target="tpu_custom_call" | custom-call | tf_op jit(solution)/shard_map/pallas_call | solution.py:27
  161.5 20.0 %all-to-all-done.4 = bf16[16,128,448]{1,2,0:T(8,128)(2,1)} async-done(((bf16[16,128,448]{1,2,0:T(8,128)(2,1)}), bf16[16,128,448]{1,2,0:T(8,128)(2,1)}, u32[]{:S(2)}, u32[]{:S(2)}) %all-to-all-start.4) | async-done | bytes 1835040 | tf_op jit(solution)/shard_map/all_to_all | solution.py:397
  182.6 6.4 %all-to-all-start.3 = ((bf16[16,192,128]{2,1,0:T(8,128)(2,1)}), bf16[16,192,128]{2,1,0:T(8,128)(2,1)S(1)}, u32[]{:S(2)}, u32[]{:S(2)}) async-start(bf16[16,192,128]{2,1,0:T(8,128)(2,1)} %broadcast_in_dim.41), calls=%async_computation.3 | async-start | bytes 1572864 | tf_op jit(solution)/shard_map/all_to_all | solution.py:84
  189.0 2.8 %copy.44.w_ref = bf16[16,128,448]{2,1,0:T(8,128)(2,1)S(1)} copy(bf16[16,128,448]{1,2,0:T(8,128)(2,1)} %all-to-all-done.4) | data formatting | bytes 3670016 | tf_op jit(solution)/shard_map/all_to_all | solution.py:397
  191.8 9.9 %all-to-all-done.3.act_ref = bf16[16,192,128]{2,1,0:T(8,128)(2,1)S(1)} async-done(((bf16[16,192,128]{2,1,0:T(8,128)(2,1)}), bf16[16,192,128]{2,1,0:T(8,128)(2,1)S(1)}, u32[]{:S(2)}, u32[]{:S(2)}) %all-to-all-start.3) | async-done | bytes 786464 | tf_op jit(solution)/shard_map/all_to_all | solution.py:84
  203.5 2.7 collective-permute-start.14
  207.1 10.8 %all_to_all.30 = bf16[8,16,448]{2,1,0:T(8,128)(2,1)S(1)} all-to-all(bf16[8,16,448]{2,1,0:T(8,128)(2,1)S(1)} %bitcast.41), channel_id=1, replica_groups=mesh['group'=2,'seq'=16,'expert'=8] {'expert'}, dimensions={0} | all-to-all | bytes 229376 | tf_op jit(solution)/shard_map/all_to_all | solution.py:410
  218.6 2.3 copy-done.8
  222.2 44.6 %shard_map.167 = bf16[128,4096]{1,0:T(8,128)(2,1)} custom-call(s32[8]{0:T(128)S(1)} %copy-done.6, bf16[128,4608]{1,0:T(8,128)(2,1)S(1)} %bitcast.38, bf16[16,2,576,128]{3,2,1,0:T(8,128)(2,1)S(1)} %bitcast.37), custom_call_target="tpu_custom_call" | custom-call | flops 9126805504 | bytes 8388608 | tf_op jit(solution)/shard_map/pallas_call | solution.py:284
  (87 shorter events, 44.0 us)
Async XLA Ops:
  7.2 211.4 %all-gather.3.cloned.1.call-start = ((), (), s32[]{:S(2)}) async-start(), calls=%async_computation.6 | async-start | bytes 5013504 | tf_op jit(solution)/shard_map/all_gather | solution.py:333
  9.2 6.1 %collective-permute-start.3 = (bf16[576,128]{1,0:T(8,128)(2,1)}, bf16[576,128]{1,0:T(8,128)(2,1)S(1)}, u32[]{:S(2)}, u32[]{:S(2)}) collective-permute-start(bf16[576,128]{1,0:T(8,128)(2,1)} %bitcast.28), channel_id=1, source_target_pairs={{0,8},{8,16},{16,24},{24,0},{32,40},{40,48},{48,56},{56,32},{64,72... | collective-permute-start | bytes 442376 | tf_op jit(solution)/shard_map/ppermute | solution.py:59
  11.3 9.1 %collective-permute-start.4 = (bf16[576,128]{1,0:T(8,128)(2,1)}, bf16[576,128]{1,0:T(8,128)(2,1)S(1)}, u32[]{:S(2)}, u32[]{:S(2)}) collective-permute-start(bf16[576,128]{1,0:T(8,128)(2,1)} %bitcast.29), channel_id=1, source_target_pairs={{0,16},{8,24},{16,0},{24,8},{32,48},{40,56},{48,32},{56,40},{64,80... | collective-permute-start | bytes 442376 | tf_op jit(solution)/shard_map/ppermute | solution.py:59
  13.7 6.6 %collective-permute-start.5 = (bf16[576,128]{1,0:T(8,128)(2,1)}, bf16[576,128]{1,0:T(8,128)(2,1)S(1)}, u32[]{:S(2)}, u32[]{:S(2)}) collective-permute-start(bf16[576,128]{1,0:T(8,128)(2,1)} %bitcast.30), channel_id=1, source_target_pairs={{0,24},{8,0},{16,8},{24,16},{32,56},{40,32},{48,40},{56,48},{64,88... | collective-permute-start | bytes 442376 | tf_op jit(solution)/shard_map/ppermute | solution.py:59
  22.2 15.2 %collective-permute-start.6 = (bf16[4,576,128]{2,1,0:T(8,128)(2,1)}, bf16[4,576,128]{2,1,0:T(8,128)(2,1)S(1)}, u32[]{:S(2)}, u32[]{:S(2)}) collective-permute-start(bf16[4,576,128]{2,1,0:T(8,128)(2,1)} %pad_maximum_fusion), channel_id=1, source_target_pairs={{0,128},{128,0},{1,129},{129,1},{2,130},{130,2},{3,131},{131,3},{4... | collective-permute-start | bytes 1769480 | tf_op jit(solution)/shard_map/ppermute | solution.py:80
  26.8 8.2 %collective-permute-start = (bf16[64,640]{1,0:T(8,128)(2,1)S(1)}, bf16[64,640]{1,0:T(8,128)(2,1)}, u32[]{:S(2)}, u32[]{:S(2)}) collective-permute-start(bf16[64,640]{1,0:T(8,128)(2,1)S(1)} %pad_maximum_fusion.2.q_ref.q0), channel_id=1, source_target_pairs={{0,32},{8,40},{16,48},{24,56},{32,64},{40,72},{48,80},{56,88},{64,... | collective-permute-start | bytes 245768 | tf_op jit(solution)/shard_map/ppermute | solution.py:70
  27.8 9.6 %collective-permute-start.1 = (bf16[64,640]{1,0:T(8,128)(2,1)S(1)}, bf16[64,640]{1,0:T(8,128)(2,1)}, u32[]{:S(2)}, u32[]{:S(2)}) collective-permute-start(bf16[64,640]{1,0:T(8,128)(2,1)S(1)} %pad_maximum_fusion.2.q_ref.q0), channel_id=1, source_target_pairs={{0,64},{8,72},{16,80},{24,88},{32,96},{40,104},{48,112},{56,120},{... | collective-permute-start | bytes 245768 | tf_op jit(solution)/shard_map/ppermute | solution.py:70
  30.5 6.9 %collective-permute-start.2 = (bf16[64,640]{1,0:T(8,128)(2,1)S(1)}, bf16[64,640]{1,0:T(8,128)(2,1)}, u32[]{:S(2)}, u32[]{:S(2)}) collective-permute-start(bf16[64,640]{1,0:T(8,128)(2,1)S(1)} %pad_maximum_fusion.2.q_ref.q0), channel_id=1, source_target_pairs={{0,96},{8,104},{16,112},{24,120},{32,0},{40,8},{48,16},{56,24},{64... | collective-permute-start | bytes 245768 | tf_op jit(solution)/shard_map/ppermute | solution.py:70
  35.0 61.7 %copy-start.5 = (s32[8]{0:T(128)}, s32[8]{0:T(128)S(1)}, u32[]{:S(2)}) copy-start(s32[8]{0:T(128)S(1)} %stack.49.info) | copy-start | bytes 100
  40.8 34.0 %copy-start.10 = (bf16[16,448]{1,0:T(8,128)(2,1)S(1)}, bf16[16,448]{1,0:T(8,128)(2,1)}, u32[]{:S(2)}) copy-start(bf16[16,448]{1,0:T(8,128)(2,1)} %param.26) | copy-start | bytes 43012
  40.8 5.9 %collective-permute-start.7 = (bf16[32,1152]{1,0:T(8,128)(2,1)S(1)}, bf16[32,1152]{1,0:T(8,128)(2,1)S(1)}, u32[]{:S(2)}, u32[]{:S(2)}) collective-permute-start(bf16[32,1152]{1,0:T(8,128)(2,1)S(1)} %shard_map.169.p0), channel_id=1, source_target_pairs={{0,32},{8,40},{16,48},{24,56},{32,64},{40,72},{48,80},{56,88},{64,... | collective-permute-start | bytes 221192 | tf_op jit(solution)/shard_map/ppermute | solution.py:70
  40.9 5.8 %collective-permute-start.8 = (bf16[32,1152]{1,0:T(8,128)(2,1)S(1)}, bf16[32,1152]{1,0:T(8,128)(2,1)S(1)}, u32[]{:S(2)}, u32[]{:S(2)}) collective-permute-start(bf16[32,1152]{1,0:T(8,128)(2,1)S(1)} %shard_map.169.p0), channel_id=1, source_target_pairs={{0,64},{8,72},{16,80},{24,88},{32,96},{40,104},{48,112},{56,120},{... | collective-permute-start | bytes 221192 | tf_op jit(solution)/shard_map/ppermute | solution.py:70
  42.8 4.5 %collective-permute-start.9 = (bf16[32,1152]{1,0:T(8,128)(2,1)S(1)}, bf16[32,1152]{1,0:T(8,128)(2,1)S(1)}, u32[]{:S(2)}, u32[]{:S(2)}) collective-permute-start(bf16[32,1152]{1,0:T(8,128)(2,1)S(1)} %shard_map.169.p0), channel_id=1, source_target_pairs={{0,96},{8,104},{16,112},{24,120},{32,0},{40,8},{48,16},{56,24},{64... | collective-permute-start | bytes 221192 | tf_op jit(solution)/shard_map/ppermute | solution.py:70
  48.1 6.9 %collective-permute-start.10 = (bf16[32,1024]{1,0:T(8,128)(2,1)S(1)}, bf16[32,1024]{1,0:T(8,128)(2,1)S(1)}, u32[]{:S(2)}, u32[]{:S(2)}) collective-permute-start(bf16[32,1024]{1,0:T(8,128)(2,1)S(1)} %shard_map.170.x0), channel_id=1, source_target_pairs={{0,8},{8,16},{16,24},{24,0},{32,40},{40,48},{48,56},{56,32},{64,72... | collective-permute-start | bytes 196616 | tf_op jit(solution)/shard_map/ppermute | solution.py:59
  50.2 4.8 %collective-permute-start.11 = (bf16[32,1024]{1,0:T(8,128)(2,1)S(1)}, bf16[32,1024]{1,0:T(8,128)(2,1)S(1)}, u32[]{:S(2)}, u32[]{:S(2)}) collective-permute-start(bf16[32,1024]{1,0:T(8,128)(2,1)S(1)} %shard_map.170.x0), channel_id=1, source_target_pairs={{0,16},{8,24},{16,0},{24,8},{32,48},{40,56},{48,32},{56,40},{64,80... | collective-permute-start | bytes 196616 | tf_op jit(solution)/shard_map/ppermute | solution.py:59
  51.9 4.7 %collective-permute-start.12 = (bf16[32,1024]{1,0:T(8,128)(2,1)S(1)}, bf16[32,1024]{1,0:T(8,128)(2,1)S(1)}, u32[]{:S(2)}, u32[]{:S(2)}) collective-permute-start(bf16[32,1024]{1,0:T(8,128)(2,1)S(1)} %shard_map.170.x0), channel_id=1, source_target_pairs={{0,24},{8,0},{16,8},{24,16},{32,56},{40,32},{48,40},{56,48},{64,88... | collective-permute-start | bytes 196616 | tf_op jit(solution)/shard_map/ppermute | solution.py:59
  58.2 16.5 %all-to-all-start = ((bf16[8,16,448]{2,1,0:T(8,128)(2,1)}), bf16[8,16,448]{2,1,0:T(8,128)(2,1)S(1)}, u32[]{:S(2)}, u32[]{:S(2)}) async-start(bf16[8,16,448]{2,1,0:T(8,128)(2,1)} %bitcast.15), calls=%async_computation | async-start | bytes 262144 | tf_op jit(solution)/shard_map/all_to_all | solution.py:366
  74.9 5.4 %collective-permute-start.13 = (bf16[16,512]{1,0:T(8,128)(2,1)S(1)}, bf16[16,512]{1,0:T(8,128)(2,1)S(1)}, u32[]{:S(2)}, u32[]{:S(2)}) collective-permute-start(bf16[16,512]{1,0:T(8,128)(2,1)S(1)} %concatenate.11), channel_id=1, source_target_pairs={{0,128},{128,0},{1,129},{129,1},{2,130},{130,2},{3,131},{131,3},{4... | collective-permute-start | bytes 49160 | tf_op jit(solution)/shard_map/ppermute | solution.py:80
  81.0 15.7 %all-to-all-start.1 = ((bf16[8,2,16,512]{3,2,1,0:T(8,128)(2,1)}), bf16[8,2,16,512]{3,2,1,0:T(8,128)(2,1)S(1)}, u32[]{:S(2)}, u32[]{:S(2)}) async-start(bf16[8,2,16,512]{3,2,1,0:T(8,128)(2,1)} %broadcast_in_dim.38), calls=%async_computation.1 | async-start | bytes 524288 | tf_op jit(solution)/shard_map/all_to_all | solution.py:84
  100.0 52.9 %all-to-all-start.2 = ((bf16[16,192,512]{2,1,0:T(8,128)(2,1)}), bf16[16,192,512]{2,1,0:T(8,128)(2,1)S(1)}, u32[]{:S(2)}, u32[]{:S(2)}) async-start(bf16[16,192,512]{2,1,0:T(8,128)(2,1)} %broadcast_in_dim.40), calls=%async_computation.2 | async-start | bytes 6291456 | tf_op jit(solution)/shard_map/all_to_all | solution.py:84
  109.6 47.8 %copy-start.6 = (s32[8]{0:T(128)S(1)}, s32[8]{0:T(128)}, u32[]{:S(2)}) copy-start(s32[8]{0:T(128)} %copy-done.5) | copy-start | bytes 100
  153.0 28.6 %all-to-all-start.4 = ((bf16[16,128,448]{1,2,0:T(8,128)(2,1)}), bf16[16,128,448]{1,2,0:T(8,128)(2,1)}, u32[]{:S(2)}, u32[]{:S(2)}) async-start(bf16[16,128,448]{1,2,0:T(8,128)(2,1)} %bitcast.39), calls=%async_computation.4 | async-start | bytes 3670016 | tf_op jit(solution)/shard_map/all_to_all | solution.py:397
  182.6 19.1 %all-to-all-start.3 = ((bf16[16,192,128]{2,1,0:T(8,128)(2,1)}), bf16[16,192,128]{2,1,0:T(8,128)(2,1)S(1)}, u32[]{:S(2)}, u32[]{:S(2)}) async-start(bf16[16,192,128]{2,1,0:T(8,128)(2,1)} %broadcast_in_dim.41), calls=%async_computation.3 | async-start | bytes 1572864 | tf_op jit(solution)/shard_map/all_to_all | solution.py:84
  203.5 3.7 %collective-permute-start.14 = (bf16[128,448]{1,0:T(8,128)(2,1)S(1)}, bf16[128,448]{1,0:T(8,128)(2,1)S(1)}, u32[]{:S(2)}, u32[]{:S(2)}) collective-permute-start(bf16[128,448]{1,0:T(8,128)(2,1)S(1)} %get-tuple-element.17), channel_id=1, source_target_pairs={{0,128},{128,0},{1,129},{129,1},{2,130},{130,2},{3,131},{131,3},{4... | collective-permute-start | bytes 344072 | tf_op jit(solution)/shard_map/ppermute | solution.py:80
  (11 other events, 162.0 us)
Sparse Core Ops, SparseCore 0:
  10.5 65.6 all-gather.2

commit v2 on v1

v2 whole, which is shorter than its diff:
```python
import functools

import jax
import jax.numpy as jnp
from jax import lax
from jax.experimental import pallas as pl
from jax.experimental.pallas import tpu as pltpu
from jax.sharding import PartitionSpec as P

LATENT = 512
VDIM = 128
SIDE = 4
CAP = 12

ROWS_X = [[y * SIDE + x for x in range(SIDE)] for y in range(SIDE)]
ROWS_Y = [[y * SIDE + x for y in range(SIDE)] for x in range(SIDE)]

bf16 = jnp.bfloat16
f32 = jnp.float32
score_scale = 192.0 ** (-0.5)
epsilon = 1e-06
LOW = -1e30

VMEM = pl.BlockSpec(memory_space=pltpu.VMEM)
SMEM = pl.BlockSpec(memory_space=pltpu.SMEM)


def call(kernel, out_shape, ins, scratch=(), fetch=(), cost=None, limit=48 << 20):
    multi = isinstance(out_shape, (tuple, list))

    def body(*refs):
        refs = list(refs)
        if fetch:
            held, sems = refs[-len(fetch) - 1 : -1], refs[-1]
            copies = [
                pltpu.make_async_copy(refs[at], to, sems.at[i])
                for i, (at, to) in enumerate(zip(fetch, held))
            ]
            for copy in copies:
                copy.start()
            for copy in copies:
                copy.wait()
            refs = refs[: -len(fetch) - 1]
            for at, to in zip(fetch, held):
                refs[at] = to
        kernel(*refs)

    held = [pltpu.VMEM(ins[at].shape, ins[at].dtype) for at in fetch]
    if fetch:
        held.append(pltpu.SemaphoreType.DMA((len(fetch),)))
    place = [SMEM] + [VMEM] * (len(ins) - 1)
    for at in fetch:
        place[at] = pl.BlockSpec(memory_space=pl.ANY)
    return pl.pallas_call(
        body,
        out_shape=out_shape,
        in_specs=place,
        out_specs=[VMEM] * len(out_shape) if multi else VMEM,
        scratch_shapes=list(scratch) + held,
        compiler_params=pltpu.CompilerParams(vmem_limit_bytes=limit),
        cost_estimate=cost,
    )(*ins)


def nn(a, b):
    return jnp.dot(a, b, preferred_element_type=f32)


def nt(a, b):
    return lax.dot_general(a, b, (((1,), (1,)), ((), ())), preferred_element_type=f32)


def tn(a, b):
    return lax.dot_general(a, b, (((0,), (0,)), ((), ())), preferred_element_type=f32)


def split3(v):
    high = v.astype(bf16).astype(f32)
    rest = v - high
    mid = rest.astype(bf16).astype(f32)
    return high, mid, (rest - mid).astype(bf16).astype(f32)


def to_x(array, d):
    return lax.ppermute(
        array,
        "seq",
        [(y * SIDE + x, y * SIDE + (x + d) % SIDE) for y in range(SIDE) for x in range(SIDE)],
    )


def to_y(array, d):
    return lax.ppermute(
        array,
        "seq",
        [(y * SIDE + x, (y + d) % SIDE * SIDE + x) for y in range(SIDE) for x in range(SIDE)],
    )


def along_x(array):
    return [array] + [to_x(array, d) for d in range(1, SIDE)]


def along_y(array):
    return [array] + [to_y(array, d) for d in range(1, SIDE)]


def other_core(array):
    return lax.ppermute(array, "group", [(0, 1), (1, 0)])


def everyone(array, axis, count, groups=None):
    return lax.all_to_all(
        jnp.broadcast_to(array[None], (count,) + array.shape),
        axis,
        0,
        0,
        tiled=True,
        axis_index_groups=groups,
    )


def head_rows(ref):
    raw = ref[...].astype(f32)
    heads = [raw[:, h * 576 : (h + 1) * 576] for h in range(8)]
    wanted = raw[:, 8 * 576 : 8 * 576 + 1]
    return jnp.concatenate(heads, axis=0).astype(bf16), jnp.concatenate([wanted] * 8, axis=0)


def resident_kernel(lens, q_ref, cache_ref, m_ref, l_ref, w_ref):
    count = cache_ref.shape[0]
    queries, _ = head_rows(q_ref)
    row = lax.rem(lax.broadcasted_iota(jnp.int32, (queries.shape[0], 128), 0), count)
    column = lax.broadcasted_iota(jnp.int32, (queries.shape[0], 128), 1)
    scores = []
    for r in range(count):
        s = nn(queries, cache_ref[r]) * score_scale
        scores.append(jnp.where((row == r) & (column < lens[r]), s, LOW))
    top = scores[0]
    for s in scores[1:]:
        top = jnp.maximum(top, s)
    m = jnp.max(top, axis=1, keepdims=True)
    total = jnp.zeros_like(top)
    weighted = jnp.zeros((queries.shape[0], LATENT), f32)
    for r in range(count):
        p = jnp.where((row == r) & (column < lens[r]), jnp.exp(scores[r] - m), 0.0)
        total += p
        weighted += nt(p.astype(bf16), cache_ref[r, :LATENT])
    m_ref[...] = m
    l_ref[...] = jnp.sum(total, axis=1, keepdims=True)
    w_ref[...] = weighted


def span_kernel(
    info, q0, q1, q2, q3, k0, k1, k2, k3, kp, w_uv, rm, rl, rw, out_ref, scr
):
    group = info[0].astype(f32)
    y = info[1]
    parts = [head_rows(q) for q in (q0, q1, q2, q3)]
    queries = jnp.concatenate([p[0] for p in parts], axis=0)
    wanted = jnp.concatenate([p[1] for p in parts], axis=0)
    own_keys = jnp.concatenate([k0[...], k1[...], k2[...], k3[...]], axis=1)
    far_keys = jnp.concatenate([kp[0], kp[1], kp[2], kp[3]], axis=1)
    own = wanted == group
    valid = wanted < 1.5
    s = jnp.where(own, nn(queries, own_keys), nn(queries, far_keys)) * score_scale
    m = jnp.where(valid, jnp.max(s, axis=1, keepdims=True), LOW)
    p = jnp.where(valid, jnp.exp(s - m), 0.0)
    total = jnp.sum(p, axis=1, keepdims=True)
    weighted = nt(jnp.where(own, p, 0.0).astype(bf16), own_keys[:LATENT]) + nt(
        jnp.where(own, 0.0, p).astype(bf16), far_keys[:LATENT]
    )
    here = rm.shape[0]
    newest = jnp.maximum(m[:here], rm[...])
    a = jnp.exp(m[:here] - newest)
    b = jnp.exp(rm[...] - newest)
    m = jnp.concatenate([newest, m[here:]], axis=0)
    total = jnp.concatenate([total[:here] * a + rl[...] * b, total[here:]], axis=0)
    weighted = jnp.concatenate([weighted[:here] * a + rw[...] * b, weighted[here:]], axis=0)
    some = total > 0.0
    safe = jnp.where(some, total, 1.0)
    latent = (weighted / safe).reshape(SIDE, 8, 8, LATENT)
    level = jnp.where(some, m + jnp.log(safe), LOW).reshape(SIDE, 8, 8, 1)
    lane = lax.broadcasted_iota(jnp.int32, (SIDE, 8, 128), 2)
    tail = jnp.zeros((SIDE, 8, 128), f32)
    places = [lax.rem(y - d + SIDE, SIDE) for d in range(SIDE)]
    for h in range(8):
        rows = latent[:, h].reshape(SIDE * 8, LATENT).astype(bf16)
        value = nn(rows, w_uv[h])
        for d in range(SIDE):
            scr[places[d], :, h * VDIM : (h + 1) * VDIM] = value[d * 8 : (d + 1) * 8]
        for part, v in enumerate(split3(level[:, h])):
            tail = jnp.where(lane == part * 8 + h, v, tail)
    for d in range(SIDE):
        scr[places[d], :, 8 * VDIM :] = tail[d]
    out_ref[...] = scr[...].reshape(SIDE * 8, 9 * VDIM).astype(bf16)


def merge_kernel(info, p0, p1, p2, p3, out_ref):
    parts = [p0, p1, p2, p3]
    levels = []
    for p in parts:
        tail = p[:, 8 * VDIM :].astype(f32)
        levels.append(tail[:, 0:8] + tail[:, 8:16] + tail[:, 16:24])
    top = functools.reduce(jnp.maximum, levels)
    weights = [jnp.exp(v - top) for v in levels]
    total = functools.reduce(jnp.add, weights)
    weights = [w / total for w in weights]
    for h in range(8):
        cut = slice(h * VDIM, (h + 1) * VDIM)
        value = sum(p[:, cut].astype(f32) * w[:, h : h + 1] for p, w in zip(parts, weights))
        out_ref[:, cut] = value.astype(bf16)


def project_kernel(info, x0, x1, x2, x3, w_out, out_ref, scr):
    x = info[2]
    rows = jnp.concatenate([x0[...], x1[...], x2[...], x3[...]], axis=0)
    product = nt(rows, w_out[...])
    for d in range(SIDE):
        place = lax.rem(x - d + SIDE, SIDE)
        for y in range(SIDE):
            at = (d * SIDE + y) * 8
            scr[y, place] = product[at : at + 8]
    out_ref[...] = scr[...].reshape(out_ref.shape).astype(bf16)


def hidden_kernel(info, terms_ref, x_ref, gain_ref, extra_ref, hidden_ref, packed_ref):
    attention = jnp.sum(terms_ref[...].astype(f32), axis=0)
    rounded = (x_ref[...].astype(f32) + attention).astype(bf16)
    hidden_ref[...] = rounded
    hidden = rounded.astype(f32)
    features = hidden.shape[1]
    packed_ref[:, :features] = (hidden * gain_ref[...]).astype(bf16)
    extra = extra_ref[...]
    lane = lax.broadcasted_iota(jnp.int32, extra.shape, 1)
    for part, v in enumerate(split3(jnp.sum(hidden * hidden, axis=1, keepdims=True))):
        extra = jnp.where(lane == 32 + part, v, extra)
    packed_ref[:, features:] = extra.astype(bf16)


def expert_kernel(info, near_ref, far_ref, w_ref, act_ref, place_ref, gate_ref):
    shards, half, _ = near_ref.shape
    features, block = w_ref.shape[2], 16
    rows, slots = 2 * half, act_ref.shape[0]
    both = jnp.zeros((rows, 256), f32)
    tails = jnp.zeros((rows, 64), f32)
    for s in range(shards):
        x = jnp.concatenate([near_ref[s], far_ref[s]], axis=0)
        both += nn(x[:, :features], jnp.concatenate([w_ref[0, s], w_ref[1, s]], axis=1))
        tails += x[:, features:].astype(f32)
    squares = tails[:, 32:33] + tails[:, 33:34] + tails[:, 34:35]
    factor = lax.rsqrt(squares * (1.0 / (shards * features)) + epsilon)
    gate = both[:, :128] * factor
    act = (gate * (1.0 / (1.0 + jnp.exp(-gate))) * (both[:, 128:] * factor)).astype(bf16)
    extra = jnp.concatenate([near_ref[0, :, features:], far_ref[0, :, features:]], axis=0).astype(f32)
    hit = extra[:, 0:8] == info[3].astype(f32)
    mask = jnp.sum(jnp.where(hit, 1.0, 0.0), axis=1, keepdims=True)
    gates = extra[:, 8:16] + extra[:, 16:24] + extra[:, 24:32]
    gate_ref[...] = jnp.sum(jnp.where(hit, gates, 0.0), axis=1, keepdims=True)
    j = lax.broadcasted_iota(jnp.int32, (rows, rows), 0)
    k = lax.broadcasted_iota(jnp.int32, (rows, rows), 1)
    before = jnp.where((k < j) & (k // block == j // block), 1.0, 0.0).astype(bf16)
    slot = nn(before, jnp.broadcast_to(mask, (rows, 128)).astype(bf16))[:, 0:1]
    j = lax.broadcasted_iota(jnp.int32, (rows, slots), 0)
    i = lax.broadcasted_iota(jnp.int32, (rows, slots), 1)
    target = slot.astype(jnp.int32) + CAP * (j // block)
    place = jnp.where((mask > 0.5) & (target == i), 1.0, 0.0).astype(bf16)
    place_ref[...] = place
    act_ref[...] = tn(place, act).astype(bf16)


def down_kernel(info, a0, a1, a2, a3, w0, w1, w2, w3, place_ref, gate_ref, near_ref, far_ref):
    y = info[1]
    place, gates = place_ref[...], gate_ref[...]
    half = near_ref.shape[1]
    for d in range(SIDE):
        to = lax.rem(y + d, SIDE)
        total = sum(nt(a[...], w[to]) for a, w in ((a0, w0), (a1, w1), (a2, w2), (a3, w3)))
        high = total.astype(bf16)
        low = (total - high.astype(f32)).astype(bf16)
        share = (nn(place, high) + nn(place, low)) * gates
        near_ref[d] = share[:half]
        far_ref[d] = share[half:].astype(bf16)


def prompt_kernel(info, q_ref, keys_ref, out_ref, scores, weighted):
    pieces, tokens = keys_ref.shape[0], q_ref.shape[0]
    heads = q_ref.shape[1] // 576
    me, prefix_len = info[4], info[5]
    queries = jnp.concatenate([q_ref[:, h * 576 : (h + 1) * 576] for h in range(heads)], axis=0)
    rows = queries.shape[0]
    lane = lax.broadcasted_iota(jnp.int32, (tokens, 128), 1)
    ahead = lane - lax.broadcasted_iota(jnp.int32, (tokens, 128), 0)
    unroll = 8

    def score(i, top):
        for u in range(unroll):
            j = i * unroll + u
            early = jnp.where(lane < prefix_len - j * 128, 0.0, LOW)
            late = jnp.where(ahead <= (me - j) * tokens, 0.0, LOW)
            masks = jnp.concatenate([jnp.concatenate([early, late], axis=1)] * heads, axis=0)
            s = nn(queries, keys_ref[j]) + masks
            scores[j] = s
            top = jnp.maximum(top, jnp.maximum(s[:, :128], s[:, 128:]))
        return top

    top = lax.fori_loop(0, pieces // unroll, score, jnp.full((rows, 128), LOW, f32))
    top = jnp.max(top, axis=1, keepdims=True) * score_scale
    weighted[...] = jnp.zeros_like(weighted)

    def weigh(i, total):
        sums = jnp.zeros(weighted.shape, f32)
        for u in range(unroll):
            j = i * unroll + u
            p = jnp.exp(scores[j] * score_scale - top)
            total = total + (p[:, :128] + p[:, 128:])
            sums = sums + nt(p.astype(bf16), keys_ref[j, :LATENT])
        weighted[...] += sums
        return total

    total = lax.fori_loop(0, pieces // unroll, weigh, jnp.zeros((rows, 128), f32))
    total = jnp.sum(total, axis=1, keepdims=True)
    result = (weighted[...] / total).astype(bf16)
    for h in range(heads):
        out_ref[:, h * LATENT : (h + 1) * LATENT] = result[h * tokens : (h + 1) * tokens]


def prompt_attention(info, queries, keys, heads=4):
    tokens, width = queries.shape
    steps = width // (576 * heads)
    pieces = keys.shape[0]
    return pl.pallas_call(
        prompt_kernel,
        out_shape=jax.ShapeDtypeStruct((tokens, steps * heads * LATENT), bf16),
        grid=(steps,),
        in_specs=[
            SMEM,
            pl.BlockSpec((tokens, heads * 576), lambda i: (0, i)),
            pl.BlockSpec(keys.shape, lambda i: (0, 0, 0)),
        ],
        out_specs=pl.BlockSpec((tokens, heads * LATENT), lambda i: (0, i)),
        scratch_shapes=[
            pltpu.VMEM((pieces, heads * tokens, 256), f32),
            pltpu.VMEM((heads * tokens, LATENT), f32),
        ],
        compiler_params=pltpu.CompilerParams(vmem_limit_bytes=48 << 20),
        cost_estimate=pl.CostEstimate(
            flops=2 * 8 * tokens * 4096 * 1088, bytes_accessed=8 << 20, transcendentals=8 * tokens * 4096
        ),
    )(info, queries, keys)


def on_device(
    q_pre,
    prefix_cache,
    span_cache,
    prefix_len,
    q_dec,
    dec_cache,
    cache_len,
    requests,
    w_uv,
    w_out,
    x_dec,
    norm_gain,
    expert_ids,
    expert_gates,
    w_in,
    w_down,
):
    group = lax.axis_index("group")
    seq = lax.axis_index("seq")
    z = lax.axis_index("expert")
    shards = lax.axis_size("seq")
    depth = lax.axis_size("expert")
    info = jnp.stack(
        [group, seq // SIDE, seq % SIDE, group * depth + z, seq, prefix_len[0], z, z]
    ).astype(jnp.int32)
    features = x_dec.shape[1]

    wanted = jnp.broadcast_to(requests.astype(bf16)[:, None], (8, 128))
    packet = jnp.concatenate([q_dec, wanted], axis=1)
    span, packet, prefix, columns = lax.optimization_barrier(
        (span_cache[0], packet, prefix_cache[0], span_cache[0])
    )
    keys = lax.all_gather(jnp.concatenate([prefix, columns], axis=1), "seq", axis=0)
    pieces, packets = along_x(span), along_y(packet)
    resident = call(
        resident_kernel,
        [
            jax.ShapeDtypeStruct((64, 1), f32),
            jax.ShapeDtypeStruct((64, 1), f32),
            jax.ShapeDtypeStruct((64, LATENT), f32),
        ],
        [cache_len, packet, dec_cache],
    )
    w_back = w_down[0].T.reshape(SIDE, SIDE, features, 128).transpose(1, 0, 2, 3)
    pieces, packets, resident, w_back = lax.optimization_barrier(
        (pieces, packets, resident, w_back)
    )
    far = other_core(jnp.stack(pieces))
    part = call(
        span_kernel,
        jax.ShapeDtypeStruct((32, 9 * VDIM), bf16),
        [info, *packets, *pieces, far, w_uv, *resident],
        [pltpu.VMEM((SIDE, 8, 9 * VDIM), f32)],
        fetch=(5, 6, 7, 8, 9),
    )

    dec_val = call(
        merge_kernel,
        jax.ShapeDtypeStruct((32, 8 * VDIM), bf16),
        [info, *along_y(part)],
        fetch=(1, 2, 3, 4),
    )
    product = call(
        project_kernel,
        jax.ShapeDtypeStruct((128, features), bf16),
        [info, *along_x(dec_val), w_out.T],
        [pltpu.VMEM((SIDE, SIDE, 8, features), f32)],
        fetch=(1, 2, 3, 4),
    )
    product, w_back = lax.optimization_barrier((product, w_back))
    x_here = seq % SIDE
    w_back = [
        lax.dynamic_index_in_dim(w_back, (x_here + d) % SIDE, 0, keepdims=False)
        for d in range(SIDE)
    ]
    w_back = [w_back[0]] + [to_x(w_back[d], d) for d in range(1, SIDE)]
    terms = lax.all_to_all(product.reshape(depth, 16, features), "expert", 0, 0, tiled=True)

    g_high = lax.reduce_precision(expert_gates, 8, 7)
    g_mid = lax.reduce_precision(expert_gates - g_high, 8, 7)
    g_low = lax.reduce_precision(expert_gates - g_high - g_mid, 8, 7)
    extra = jnp.concatenate(
        [expert_ids.astype(f32), g_high, g_mid, g_low, jnp.zeros((16, 32), f32)], axis=1
    )
    gain = lax.dynamic_slice(norm_gain, (seq * features,), (features,))[None]
    hidden, packed = call(
        hidden_kernel,
        [
            jax.ShapeDtypeStruct((16, features), bf16),
            jax.ShapeDtypeStruct((16, features + 64), bf16),
        ],
        [info, terms, x_dec, gain, extra],
    )
    rows = everyone(packed, "expert", depth).reshape(16 * depth, features + 64)
    rows, q_pre, keys, w_back = lax.optimization_barrier((rows, q_pre, keys, w_back))
    arrived = everyone(rows, "seq", shards)
    o_pre = prompt_attention(info, q_pre[0], keys)[None]
    arrived, o_pre = lax.optimization_barrier((arrived, o_pre))
    act, place, gate = call(
        expert_kernel,
        [
            jax.ShapeDtypeStruct((16 * CAP, 128), bf16),
            jax.ShapeDtypeStruct((256, 16 * CAP), bf16),
            jax.ShapeDtypeStruct((256, 1), f32),
        ],
        [info, arrived, other_core(arrived), w_in[0].reshape(2, shards, features, 128)],
    )
    shape = (SIDE, 16 * depth, features)
    near, far_share = call(
        down_kernel,
        [jax.ShapeDtypeStruct(shape, f32), jax.ShapeDtypeStruct(shape, bf16)],
        [info, *along_x(act), *w_back, place, gate],
    )
    share = (near + other_core(far_share).astype(f32)).astype(bf16)
    parts = [share[0]] + [to_y(share[d], d) for d in range(1, SIDE)]
    share = sum(v.astype(f32) for v in parts).astype(bf16)
    shares = lax.all_to_all(share.reshape(depth, 16, features), "expert", 0, 0, tiled=True)
    h_out = (hidden.astype(f32) + jnp.sum(shares.astype(f32), axis=0)).astype(bf16)

    return (o_pre, h_out)


def solution(mesh):
    return jax.shard_map(
        on_device,
        mesh=mesh,
        in_specs=(
            P("group", "seq", "expert"),
            P("group", None, "seq"),
            P("group", None, "seq"),
            P("group"),
            P(("group", "seq"), "expert"),
            P(("group", "seq"), None, None),
            P(("group", "seq")),
            P(("group", "seq")),
            P("expert", None, None),
            P("expert", "seq"),
            P(("group", "expert"), "seq"),
            P(),
            P(("group", "expert"), None),
            P(("group", "expert"), None),
            P(("group", "expert"), None, None, "seq"),
            P(("group", "expert"), "seq", None),
        ),
        out_specs=(P("group", "seq", "expert"), P(("group", "expert"), "seq")),
        check_vma=False,
    )
```

time: 275 us -> 186 us (0.68)
  waiting for transfers between devices: 108 us -> 39.5 us
  Pallas kernels: 58 us -> 29.8 us
  blocking collectives: 10.8 us -> 24.9 us
  starting transfers between devices: 56.1 us -> 51.5 us
  local copies, waits for them, and re-layouts: 20.9 us -> 18 us
    all_to_all x3 -> x1, waiting for transfers between devices: 64.8 us -> 5.53 us  [everyone(): lax.all_to_all(jnp.broadcast_to(array[None], (count,) + array.shape), axi...]
    pallas_call x8, Pallas kernels: 58 us -> 29.8 us  [the longest x1 15 us: prompt_attention(): pl.pallas_call(prompt_kernel, out_shape=jax.ShapeDtypeStruct((tokens, ste...]
    all_to_all x1 -> x0, waiting for transfers between devices: 20 us -> none  [on_device(): lax.all_to_all(jnp.transpose(w_down[0].reshape(128, shards, features), (1...]
    all_to_all x0 -> x1, blocking collectives: none -> 10.3 us  [everyone(): lax.all_to_all(jnp.broadcast_to(array[None], (count,) + array.shape), axi...]
    all_to_all x3 -> x1, starting transfers between devices: 15.5 us -> 6.35 us  [everyone(): lax.all_to_all(jnp.broadcast_to(array[None], (count,) + array.shape), axi...]
    ppermute x12 -> x21, waiting for transfers between devices: 13.2 us -> 19.6 us  [the longest x9 10 us: to_y(): lax.ppermute(array, 'seq', [(y * SIDE + x, (y + d) % SIDE * SIDE + x) for...]
    ppermute x12 -> x21, starting transfers between devices: 18.5 us -> 24.8 us  [the longest x12 13.2 us: to_x(): lax.ppermute(array, 'seq', [(y * SIDE + x, y * SIDE + (x + d) % SIDE) for...]
    ppermute x3, waiting for transfers between devices: 1.83 us -> 6.42 us  [other_core(): return lax.ppermute(array, 'group', [(0, 1), (1, 0)])]
  transfers between devices with their start and end apart: 21 -> 27, of which waited for: 13 -> 17; matrix products, arithmetic and copies ran while one was open for 7% -> 4% of each run, Pallas kernels for 5% -> 13%
where the time goes in v2:
time: 186 us; the launch traced here: 184 us
  starting transfers between devices  51.5 us (28%)
  waiting for transfers between devices  39.5 us (21%)
  Pallas kernels  29.8 us (16%)
  blocking collectives  24.9 us (13%)
  local copies, waits for them, and re-layouts  18 us (10%)
  between operations  14.9 us (8%)
  other arithmetic  5.11 us (3%)
    pallas_call x1, Pallas kernels, prompt_attention(): pl.pallas_call(prompt_kernel, out_shape=jax.ShapeDtypeStruct((tokens, ste...  15 us
    pallas_call x7, Pallas kernels, call(): pl.pallas_call(body, out_shape=out_shape, in_specs=place, out_specs=[VMEM...  14.8 us
    all_to_all x1, blocking collectives, on_device(): lax.all_to_all(share.reshape(depth, 16, features), 'expert', 0, 0, tiled=...  14.6 us
    unnamed x42, local copies, waits for them, and re-layouts  13.7 us
    ppermute x12, starting transfers between devices, to_x(): lax.ppermute(array, 'seq', [(y * SIDE + x, y * SIDE + (x + d) % SIDE) for...  13.2 us
    ppermute x3, starting transfers between devices, other_core(): return lax.ppermute(array, 'group', [(0, 1), (1, 0)])  11.8 us
    ppermute x9, starting transfers between devices, to_y(): lax.ppermute(array, 'seq', [(y * SIDE + x, (y + d) % SIDE * SIDE + x) for...  11.6 us
    all_to_all x1, blocking collectives, everyone(): lax.all_to_all(jnp.broadcast_to(array[None], (count,) + array.shape), axi...  10.3 us
  transfers between devices with their start and end apart: 27, of which 17 were waited for; matrix products, arithmetic and copies ran while one was open for 4% of the time, Pallas kernels for 13%

profile of v2, /device:TPU:1, one launch (start us, length us, event | category | flops | bytes accessed | tf_op | source)
XLA Modules:
  0.0 183.8 jit_solution(9712663561078818785)
XLA Ops:
  10.7 2.2 %collective-permute-start.3 = (bf16[8,4736]{1,0:T(8,128)(2,1)S(1)}, bf16[8,4736]{1,0:T(8,128)(2,1)S(1)}, u32[]{:S(2)}, u32[]{:S(2)}) collective-permute-start(bf16[8,4736]{1,0:T(8,128)(2,1)S(1)} %pad_maximum_fusion.2.refs_1_), channel_id=1, source_target_pairs={{0,32},{8,40},{16,48},{24,56},{32,64},{40,72},{48,80},{56,88},{64,... | collective-permute-start | bytes 227336 | tf_op jit(solution)/shard_map/ppermute | solution.py:93
  14.1 2.5 %collective-permute-start.1 = (bf16[576,128]{1,0:T(8,128)(2,1)}, bf16[576,128]{1,0:T(8,128)(2,1)S(1)}, u32[]{:S(2)}, u32[]{:S(2)}) collective-permute-start(bf16[576,128]{1,0:T(8,128)(2,1)} %bitcast.49), channel_id=1, source_target_pairs={{0,16},{8,24},{16,0},{24,8},{32,48},{40,56},{48,32},{56,40},{64,80... | collective-permute-start | bytes 442376 | tf_op jit(solution)/shard_map/ppermute | solution.py:85
  17.7 2.6 %collective-permute-start.4 = (bf16[8,4736]{1,0:T(8,128)(2,1)S(1)}, bf16[8,4736]{1,0:T(8,128)(2,1)S(1)}, u32[]{:S(2)}, u32[]{:S(2)}) collective-permute-start(bf16[8,4736]{1,0:T(8,128)(2,1)S(1)} %pad_maximum_fusion.2.refs_1_), channel_id=1, source_target_pairs={{0,64},{8,72},{16,80},{24,88},{32,96},{40,104},{48,112},{56,120},{... | collective-permute-start | bytes 227336 | tf_op jit(solution)/shard_map/ppermute | solution.py:93
  22.0 3.9 %copy.26 = bf16[1,128,7168]{1,2,0:T(8,128)(2,1)} copy(bf16[1,128,7168]{2,1,0:T(8,128)(2,1)} %param.31) | data formatting | bytes 3670016 | tf_op args[15]
  30.2 2.4 %collective-permute-start.6 = (bf16[4,576,128]{2,1,0:T(8,128)(2,1)}, bf16[4,576,128]{2,1,0:T(8,128)(2,1)S(1)}, u32[]{:S(2)}, u32[]{:S(2)}) collective-permute-start(bf16[4,576,128]{2,1,0:T(8,128)(2,1)} %pad_maximum_fusion), channel_id=1, source_target_pairs={{0,128},{128,0},{1,129},{129,1},{2,130},{130,2},{3,131},{131,3},{4... | collective-permute-start | bytes 1769480 | tf_op jit(solution)/shard_map/ppermute | solution.py:109
  38.0 2.9 %shard_map.168.refs_1_ = bf16[32,1152]{1,0:T(8,128)(2,1)S(1)} custom-call(s32[8]{0:T(128)S(1)} %stack.43.refs_0_.info, bf16[8,4736]{1,0:T(8,128)(2,1)S(1)} %pad_maximum_fusion.2.refs_1_, bf16[8,4736]{1,0:T(8,128)(2,1)S(1)} %copy-done.9, bf16[8,4736]{1,0:T(8,128)(2,1)S(1)} %copy-done.11, bf16[8,4736]{1,0:T(8,128)(2,1)S(1)} %copy-done.13, ...), custom_call_target="tpu_custom_call" | custom-call | tf_op jit(solution)/shard_map/pallas_call | solution.py:54
  54.1 4.0 %collective-permute-done.12.refs_4_ = bf16[32,1024]{1,0:T(8,128)(2,1)S(1)} collective-permute-done((bf16[32,1024]{1,0:T(8,128)(2,1)S(1)}, bf16[32,1024]{1,0:T(8,128)(2,1)S(1)}, u32[]{:S(2)}, u32[]{:S(2)}) %collective-permute-start.12) | collective-permute-done | bytes 65568 | tf_op jit(solution)/shard_map/ppermute | solution.py:85
  58.1 2.0 %shard_map.170 = bf16[128,448]{1,0:T(8,128)(2,1)} custom-call(s32[8]{0:T(128)S(1)} %stack.43.refs_0_.info, bf16[32,1024]{1,0:T(8,128)(2,1)S(1)} %shard_map.169.refs_1_, bf16[32,1024]{1,0:T(8,128)(2,1)S(1)} %collective-permute-done.10.refs_2_, bf16[32,1024]{1,0:T(8,128)(2,1)S(1)} %collective-permute-done.11.refs_3_, ...), custom_call_target="tpu_custom_call" | custom-call | tf_op jit(solution)/shard_map/pallas_call | solution.py:54
  65.5 8.6 %all-to-all-start = ((bf16[8,16,448]{2,1,0:T(8,128)(2,1)}), bf16[8,16,448]{2,1,0:T(8,128)(2,1)S(1)}, u32[]{:S(2)}, u32[]{:S(2)}) async-start(bf16[8,16,448]{2,1,0:T(8,128)(2,1)} %bitcast.17), calls=%async_computation | async-start | bytes 262144 | tf_op jit(solution)/shard_map/all_to_all | solution.py:430
  74.2 7.9 %all-to-all-done.refs_1_ = bf16[8,16,448]{2,1,0:T(8,128)(2,1)S(1)} async-done(((bf16[8,16,448]{2,1,0:T(8,128)(2,1)}), bf16[8,16,448]{2,1,0:T(8,128)(2,1)S(1)}, u32[]{:S(2)}, u32[]{:S(2)}) %all-to-all-start) | async-done | bytes 114720 | tf_op jit(solution)/shard_map/all_to_all | solution.py:430
  82.8 10.3 %all_to_all.20 = bf16[8,16,512]{2,1,0:T(8,128)(2,1)S(1)} all-to-all(bf16[8,16,512]{2,1,0:T(8,128)(2,1)S(1)} %broadcast_in_dim.30), channel_id=1, replica_groups=mesh['group'=2,'seq'=16,'expert'=8] {'expert'}, dimensions={0} | all-to-all | bytes 262144 | tf_op jit(solution)/shard_map/all_to_all | solution.py:113
  95.0 6.3 %all-to-all-start.2 = ((bf16[16,128,512]{2,1,0:T(8,128)(2,1)}), bf16[16,128,512]{2,1,0:T(8,128)(2,1)S(1)}, u32[]{:S(2)}, u32[]{:S(2)}) async-start(bf16[16,128,512]{2,1,0:T(8,128)(2,1)} %broadcast_in_dim.31), calls=%async_computation.2 | async-start | bytes 4194304 | tf_op jit(solution)/shard_map/all_to_all | solution.py:113
  101.4 2.3 %copy-done.16 = bf16[9216,256]{1,0:T(8,128)(2,1)S(1)} copy-done((bf16[9216,256]{1,0:T(8,128)(2,1)S(1)}, bf16[9216,256]{1,0:T(8,128)(2,1)}, u32[]{:S(2)}) %copy-start.16) | copy-done | bytes 4718616
  105.0 15.0 %shard_map.172 = bf16[128,4096]{1,0:T(8,128)(2,1)} custom-call(s32[8]{0:T(128)S(1)} %stack.43.refs_0_.info, bf16[128,4608]{1,0:T(8,128)(2,1)S(1)} %bitcast.58, bf16[16,576,256]{2,1,0:T(8,128)(2,1)S(1)} %bitcast.57), custom_call_target="tpu_custom_call" | custom-call | flops 9126805504 | bytes 8388608 | tf_op jit(solution)/shard_map/pallas_call | solution.py:332
  120.0 5.5 %all-to-all-done.2.refs_1_ = bf16[16,128,512]{2,1,0:T(8,128)(2,1)S(1)} async-done(((bf16[16,128,512]{2,1,0:T(8,128)(2,1)}), bf16[16,128,512]{2,1,0:T(8,128)(2,1)S(1)}, u32[]{:S(2)}, u32[]{:S(2)}) %all-to-all-start.2) | async-done | bytes 2097184 | tf_op jit(solution)/shard_map/all_to_all | solution.py:113
  125.5 7.6 %collective-permute-start.16 = (bf16[16,128,512]{2,1,0:T(8,128)(2,1)S(1)}, bf16[16,128,512]{2,1,0:T(8,128)(2,1)S(1)}, u32[]{:S(2)}, u32[]{:S(2)}) collective-permute-start(bf16[16,128,512]{2,1,0:T(8,128)(2,1)S(1)} %all-to-all-done.2.refs_1_), channel_id=1, source_target_pairs={{0,128},{128,0},{1,129},{129,1},{2,130},{130,2},{3,131},{131,3},{4... | collective-permute-start | bytes 6291464 | tf_op jit(solution)/shard_map/ppermute | solution.py:109
  133.1 3.8 %collective-permute-done.16.refs_2_ = bf16[16,128,512]{2,1,0:T(8,128)(2,1)S(1)} collective-permute-done((bf16[16,128,512]{2,1,0:T(8,128)(2,1)S(1)}, bf16[16,128,512]{2,1,0:T(8,128)(2,1)S(1)}, u32[]{:S(2)}, u32[]{:S(2)}) %collective-permute-start.16) | collective-permute-done | bytes 2097184 | tf_op jit(solution)/shard_map/ppermute | solution.py:109
  136.9 3.8 %shard_map.173 = (bf16[192,128]{1,0:T(8,128)(2,1)S(1)}, bf16[256,192]{1,0:T(8,128)(2,1)S(1)}, f32[256,1]{1,0:T(8,128)S(1)}) custom-call(s32[8]{0:T(128)S(1)} %stack.43.refs_0_.info, bf16[16,128,512]{2,1,0:T(8,128)(2,1)S(1)} %all-to-all-done.2.refs_1_, bf16[16,128,512]{2,1,0:T(8,128)(2,1)S(1)} %collective-permute-done.16.refs_2_, ...), custom_call_target="tpu_custom_call" | custom-call | tf_op jit(solution)/shard_map/pallas_call | solution.py:54
  140.9 2.6 %collective-permute-start.19 = (bf16[192,128]{1,0:T(8,128)(2,1)S(1)}, bf16[192,128]{1,0:T(8,128)(2,1)S(1)}, u32[]{:S(2)}, u32[]{:S(2)}) collective-permute-start(bf16[192,128]{1,0:T(8,128)(2,1)S(1)} %get-tuple-element.67.refs_1_), channel_id=1, source_target_pairs={{0,24},{8,0},{16,8},{24,16},{32,56},{40,32},{48,40},{56,48},{64,88... | collective-permute-start | bytes 147464 | tf_op jit(solution)/shard_map/ppermute | solution.py:85
  143.5 2.4 %collective-permute-done.17.refs_2_ = bf16[192,128]{1,0:T(8,128)(2,1)S(1)} collective-permute-done((bf16[192,128]{1,0:T(8,128)(2,1)S(1)}, bf16[192,128]{1,0:T(8,128)(2,1)S(1)}, u32[]{:S(2)}, u32[]{:S(2)}) %collective-permute-start.17) | collective-permute-done | bytes 49184 | tf_op jit(solution)/shard_map/ppermute | solution.py:85
  146.4 2.6 %shard_map.174 = (f32[4,128,448]{2,1,0:T(8,128)S(1)}, bf16[4,128,448]{2,1,0:T(8,128)(2,1)S(1)}) custom-call(s32[8]{0:T(128)S(1)} %stack.43.refs_0_.info, bf16[192,128]{1,0:T(8,128)(2,1)S(1)} %get-tuple-element.67.refs_1_, bf16[192,128]{1,0:T(8,128)(2,1)S(1)} %collective-permute-done.17.refs_2_, bf16[192,128]{1,0:T(8,128)(2,1)S(1)} %collective-permute-done.18.refs_3_, ...), custom_call_target="tpu_custom_call" | custom-call | tf_op jit(solution)/shard_map/pallas_call | solution.py:54
  152.6 2.1 %collective-permute-start.22 = (bf16[128,448]{1,0:T(8,128)(2,1)S(1)}, bf16[128,448]{1,0:T(8,128)(2,1)S(1)}, u32[]{:S(2)}, u32[]{:S(2)}) collective-permute-start(bf16[128,448]{1,0:T(8,128)(2,1)S(1)} %get-tuple-element.82), channel_id=1, source_target_pairs={{0,64},{8,72},{16,80},{24,88},{32,96},{40,104},{48,112},{56,120},{... | collective-permute-start | bytes 344072 | tf_op jit(solution)/shard_map/ppermute | solution.py:93
  155.3 3.8 %collective-permute-done.21 = bf16[128,448]{1,0:T(8,128)(2,1)S(1)} collective-permute-done((bf16[128,448]{1,0:T(8,128)(2,1)S(1)}, bf16[128,448]{1,0:T(8,128)(2,1)S(1)}, u32[]{:S(2)}, u32[]{:S(2)}) %collective-permute-start.21) | collective-permute-done | bytes 114720 | tf_op jit(solution)/shard_map/ppermute | solution.py:93
  161.7 14.6 %all_to_all.21 = bf16[8,16,448]{2,1,0:T(8,128)(2,1)S(1)} all-to-all(bf16[8,16,448]{2,1,0:T(8,128)(2,1)S(1)} %bitcast.62), channel_id=1, replica_groups=mesh['group'=2,'seq'=16,'expert'=8] {'expert'}, dimensions={0} | all-to-all | bytes 229376 | tf_op jit(solution)/shard_map/all_to_all | solution.py:470
  (105 shorter events, 47.3 us)
Async XLA Ops:
  7.2 86.3 %all-gather.3.cloned.1.call-start = ((), (), s32[]{:S(2)}) async-start(), calls=%async_computation.4 | async-start | bytes 5013504 | tf_op jit(solution)/shard_map/all_gather | solution.py:386
  10.7 9.6 %collective-permute-start.3 = (bf16[8,4736]{1,0:T(8,128)(2,1)S(1)}, bf16[8,4736]{1,0:T(8,128)(2,1)S(1)}, u32[]{:S(2)}, u32[]{:S(2)}) collective-permute-start(bf16[8,4736]{1,0:T(8,128)(2,1)S(1)} %pad_maximum_fusion.2.refs_1_), channel_id=1, source_target_pairs={{0,32},{8,40},{16,48},{24,56},{32,64},{40,72},{48,80},{56,88},{64,... | collective-permute-start | bytes 227336 | tf_op jit(solution)/shard_map/ppermute | solution.py:93
  12.9 16.4 %collective-permute-start = (bf16[576,128]{1,0:T(8,128)(2,1)}, bf16[576,128]{1,0:T(8,128)(2,1)S(1)}, u32[]{:S(2)}, u32[]{:S(2)}) collective-permute-start(bf16[576,128]{1,0:T(8,128)(2,1)} %bitcast.48), channel_id=1, source_target_pairs={{0,8},{8,16},{16,24},{24,0},{32,40},{40,48},{48,56},{56,32},{64,72... | collective-permute-start | bytes 442376 | tf_op jit(solution)/shard_map/ppermute | solution.py:85
  14.1 15.2 %collective-permute-start.1 = (bf16[576,128]{1,0:T(8,128)(2,1)}, bf16[576,128]{1,0:T(8,128)(2,1)S(1)}, u32[]{:S(2)}, u32[]{:S(2)}) collective-permute-start(bf16[576,128]{1,0:T(8,128)(2,1)} %bitcast.49), channel_id=1, source_target_pairs={{0,16},{8,24},{16,0},{24,8},{32,48},{40,56},{48,32},{56,40},{64,80... | collective-permute-start | bytes 442376 | tf_op jit(solution)/shard_map/ppermute | solution.py:85
  16.5 12.8 %collective-permute-start.2 = (bf16[576,128]{1,0:T(8,128)(2,1)}, bf16[576,128]{1,0:T(8,128)(2,1)S(1)}, u32[]{:S(2)}, u32[]{:S(2)}) collective-permute-start(bf16[576,128]{1,0:T(8,128)(2,1)} %bitcast.50), channel_id=1, source_target_pairs={{0,24},{8,0},{16,8},{24,16},{32,56},{40,32},{48,40},{56,48},{64,88... | collective-permute-start | bytes 442376 | tf_op jit(solution)/shard_map/ppermute | solution.py:85
  17.7 10.3 %collective-permute-start.4 = (bf16[8,4736]{1,0:T(8,128)(2,1)S(1)}, bf16[8,4736]{1,0:T(8,128)(2,1)S(1)}, u32[]{:S(2)}, u32[]{:S(2)}) collective-permute-start(bf16[8,4736]{1,0:T(8,128)(2,1)S(1)} %pad_maximum_fusion.2.refs_1_), channel_id=1, source_target_pairs={{0,64},{8,72},{16,80},{24,88},{32,96},{40,104},{48,112},{56,120},{... | collective-permute-start | bytes 227336 | tf_op jit(solution)/shard_map/ppermute | solution.py:93
  20.9 7.7 %collective-permute-start.5 = (bf16[8,4736]{1,0:T(8,128)(2,1)S(1)}, bf16[8,4736]{1,0:T(8,128)(2,1)S(1)}, u32[]{:S(2)}, u32[]{:S(2)}) collective-permute-start(bf16[8,4736]{1,0:T(8,128)(2,1)S(1)} %pad_maximum_fusion.2.refs_1_), channel_id=1, source_target_pairs={{0,96},{8,104},{16,112},{24,120},{32,0},{40,8},{48,16},{56,24},{64... | collective-permute-start | bytes 227336 | tf_op jit(solution)/shard_map/ppermute | solution.py:93
  40.9 4.5 %collective-permute-start.7 = (bf16[32,1152]{1,0:T(8,128)(2,1)S(1)}, bf16[32,1152]{1,0:T(8,128)(2,1)S(1)}, u32[]{:S(2)}, u32[]{:S(2)}) collective-permute-start(bf16[32,1152]{1,0:T(8,128)(2,1)S(1)} %shard_map.168.refs_1_), channel_id=1, source_target_pairs={{0,32},{8,40},{16,48},{24,56},{32,64},{40,72},{48,80},{56,88},{64,... | collective-permute-start | bytes 221192 | tf_op jit(solution)/shard_map/ppermute | solution.py:93
  41.4 4.8 %collective-permute-start.8 = (bf16[32,1152]{1,0:T(8,128)(2,1)S(1)}, bf16[32,1152]{1,0:T(8,128)(2,1)S(1)}, u32[]{:S(2)}, u32[]{:S(2)}) collective-permute-start(bf16[32,1152]{1,0:T(8,128)(2,1)S(1)} %shard_map.168.refs_1_), channel_id=1, source_target_pairs={{0,64},{8,72},{16,80},{24,88},{32,96},{40,104},{48,112},{56,120},{... | collective-permute-start | bytes 221192 | tf_op jit(solution)/shard_map/ppermute | solution.py:93
  41.9 5.6 %collective-permute-start.9 = (bf16[32,1152]{1,0:T(8,128)(2,1)S(1)}, bf16[32,1152]{1,0:T(8,128)(2,1)S(1)}, u32[]{:S(2)}, u32[]{:S(2)}) collective-permute-start(bf16[32,1152]{1,0:T(8,128)(2,1)S(1)} %shard_map.168.refs_1_), channel_id=1, source_target_pairs={{0,96},{8,104},{16,112},{24,120},{32,0},{40,8},{48,16},{56,24},{64... | collective-permute-start | bytes 221192 | tf_op jit(solution)/shard_map/ppermute | solution.py:93
  49.2 4.9 %collective-permute-start.11 = (bf16[32,1024]{1,0:T(8,128)(2,1)S(1)}, bf16[32,1024]{1,0:T(8,128)(2,1)S(1)}, u32[]{:S(2)}, u32[]{:S(2)}) collective-permute-start(bf16[32,1024]{1,0:T(8,128)(2,1)S(1)} %shard_map.169.refs_1_), channel_id=1, source_target_pairs={{0,16},{8,24},{16,0},{24,8},{32,48},{40,56},{48,32},{56,40},{64,80... | collective-permute-start | bytes 196616 | tf_op jit(solution)/shard_map/ppermute | solution.py:85
  49.8 8.3 %collective-permute-start.12 = (bf16[32,1024]{1,0:T(8,128)(2,1)S(1)}, bf16[32,1024]{1,0:T(8,128)(2,1)S(1)}, u32[]{:S(2)}, u32[]{:S(2)}) collective-permute-start(bf16[32,1024]{1,0:T(8,128)(2,1)S(1)} %shard_map.169.refs_1_), channel_id=1, source_target_pairs={{0,24},{8,0},{16,8},{24,16},{32,56},{40,32},{48,40},{56,48},{64,88... | collective-permute-start | bytes 196616 | tf_op jit(solution)/shard_map/ppermute | solution.py:85
  61.7 31.4 %collective-permute-start.13 = (bf16[4,448,128]{2,1,0:T(8,128)(2,1)S(1)}, bf16[4,448,128]{2,1,0:T(8,128)(2,1)S(1)}, u32[]{:S(2)}, u32[]{:S(2)}) collective-permute-start(bf16[4,448,128]{2,1,0:T(8,128)(2,1)S(1)} %get-tuple-element.78), channel_id=1, source_target_pairs={{0,8},{8,16},{16,24},{24,0},{32,40},{40,48},{48,56},{56,32},{64,72... | collective-permute-start | bytes 1376264 | tf_op jit(solution)/shard_map/ppermute | solution.py:85
  61.8 31.3 %collective-permute-start.14 = (bf16[4,448,128]{2,1,0:T(8,128)(2,1)S(1)}, bf16[4,448,128]{2,1,0:T(8,128)(2,1)S(1)}, u32[]{:S(2)}, u32[]{:S(2)}) collective-permute-start(bf16[4,448,128]{2,1,0:T(8,128)(2,1)S(1)} %get-tuple-element.77), channel_id=1, source_target_pairs={{0,16},{8,24},{16,0},{24,8},{32,48},{40,56},{48,32},{56,40},{64,80... | collective-permute-start | bytes 1376264 | tf_op jit(solution)/shard_map/ppermute | solution.py:85
  63.3 30.2 %collective-permute-start.15 = (bf16[4,448,128]{2,1,0:T(8,128)(2,1)S(1)}, bf16[4,448,128]{2,1,0:T(8,128)(2,1)S(1)}, u32[]{:S(2)}, u32[]{:S(2)}) collective-permute-start(bf16[4,448,128]{2,1,0:T(8,128)(2,1)S(1)} %get-tuple-element.76), channel_id=1, source_target_pairs={{0,24},{8,0},{16,8},{24,16},{32,56},{40,32},{48,40},{56,48},{64,88... | collective-permute-start | bytes 1376264 | tf_op jit(solution)/shard_map/ppermute | solution.py:85
  65.5 16.6 %all-to-all-start = ((bf16[8,16,448]{2,1,0:T(8,128)(2,1)}), bf16[8,16,448]{2,1,0:T(8,128)(2,1)S(1)}, u32[]{:S(2)}, u32[]{:S(2)}) async-start(bf16[8,16,448]{2,1,0:T(8,128)(2,1)} %bitcast.17), calls=%async_computation | async-start | bytes 262144 | tf_op jit(solution)/shard_map/all_to_all | solution.py:430
  95.0 30.5 %all-to-all-start.2 = ((bf16[16,128,512]{2,1,0:T(8,128)(2,1)}), bf16[16,128,512]{2,1,0:T(8,128)(2,1)S(1)}, u32[]{:S(2)}, u32[]{:S(2)}) async-start(bf16[16,128,512]{2,1,0:T(8,128)(2,1)} %broadcast_in_dim.31), calls=%async_computation.2 | async-start | bytes 4194304 | tf_op jit(solution)/shard_map/all_to_all | solution.py:113
  125.5 11.4 %collective-permute-start.16 = (bf16[16,128,512]{2,1,0:T(8,128)(2,1)S(1)}, bf16[16,128,512]{2,1,0:T(8,128)(2,1)S(1)}, u32[]{:S(2)}, u32[]{:S(2)}) collective-permute-start(bf16[16,128,512]{2,1,0:T(8,128)(2,1)S(1)} %all-to-all-done.2.refs_1_), channel_id=1, source_target_pairs={{0,128},{128,0},{1,129},{129,1},{2,130},{130,2},{3,131},{131,3},{4... | collective-permute-start | bytes 6291464 | tf_op jit(solution)/shard_map/ppermute | solution.py:109
  140.7 5.1 %collective-permute-start.17 = (bf16[192,128]{1,0:T(8,128)(2,1)S(1)}, bf16[192,128]{1,0:T(8,128)(2,1)S(1)}, u32[]{:S(2)}, u32[]{:S(2)}) collective-permute-start(bf16[192,128]{1,0:T(8,128)(2,1)S(1)} %get-tuple-element.67.refs_1_), channel_id=1, source_target_pairs={{0,8},{8,16},{16,24},{24,0},{32,40},{40,48},{48,56},{56,32},{64,72... | collective-permute-start | bytes 147464 | tf_op jit(solution)/shard_map/ppermute | solution.py:85
  140.9 5.0 %collective-permute-start.18 = (bf16[192,128]{1,0:T(8,128)(2,1)S(1)}, bf16[192,128]{1,0:T(8,128)(2,1)S(1)}, u32[]{:S(2)}, u32[]{:S(2)}) collective-permute-start(bf16[192,128]{1,0:T(8,128)(2,1)S(1)} %get-tuple-element.67.refs_1_), channel_id=1, source_target_pairs={{0,16},{8,24},{16,0},{24,8},{32,48},{40,56},{48,32},{56,40},{64,80... | collective-permute-start | bytes 147464 | tf_op jit(solution)/shard_map/ppermute | solution.py:85
  140.9 5.4 %collective-permute-start.19 = (bf16[192,128]{1,0:T(8,128)(2,1)S(1)}, bf16[192,128]{1,0:T(8,128)(2,1)S(1)}, u32[]{:S(2)}, u32[]{:S(2)}) collective-permute-start(bf16[192,128]{1,0:T(8,128)(2,1)S(1)} %get-tuple-element.67.refs_1_), channel_id=1, source_target_pairs={{0,24},{8,0},{16,8},{24,16},{32,56},{40,32},{48,40},{56,48},{64,88... | collective-permute-start | bytes 147464 | tf_op jit(solution)/shard_map/ppermute | solution.py:85
  152.5 6.5 %collective-permute-start.21 = (bf16[128,448]{1,0:T(8,128)(2,1)S(1)}, bf16[128,448]{1,0:T(8,128)(2,1)S(1)}, u32[]{:S(2)}, u32[]{:S(2)}) collective-permute-start(bf16[128,448]{1,0:T(8,128)(2,1)S(1)} %get-tuple-element.80), channel_id=1, source_target_pairs={{0,32},{8,40},{16,48},{24,56},{32,64},{40,72},{48,80},{56,88},{64,... | collective-permute-start | bytes 344072 | tf_op jit(solution)/shard_map/ppermute | solution.py:93
  152.6 8.2 %collective-permute-start.22 = (bf16[128,448]{1,0:T(8,128)(2,1)S(1)}, bf16[128,448]{1,0:T(8,128)(2,1)S(1)}, u32[]{:S(2)}, u32[]{:S(2)}) collective-permute-start(bf16[128,448]{1,0:T(8,128)(2,1)S(1)} %get-tuple-element.82), channel_id=1, source_target_pairs={{0,64},{8,72},{16,80},{24,88},{32,96},{40,104},{48,112},{56,120},{... | collective-permute-start | bytes 344072 | tf_op jit(solution)/shard_map/ppermute | solution.py:93
  154.7 6.9 %collective-permute-start.23 = (bf16[128,448]{1,0:T(8,128)(2,1)S(1)}, bf16[128,448]{1,0:T(8,128)(2,1)S(1)}, u32[]{:S(2)}, u32[]{:S(2)}) collective-permute-start(bf16[128,448]{1,0:T(8,128)(2,1)S(1)} %get-tuple-element.81), channel_id=1, source_target_pairs={{0,96},{8,104},{16,112},{24,120},{32,0},{40,8},{48,16},{56,24},{64... | collective-permute-start | bytes 344072 | tf_op jit(solution)/shard_map/ppermute | solution.py:93
  (23 other events, 150.0 us)
Sparse Core Ops, SparseCore 0:
  10.8 77.3 all-gather.2

commit v3 on v2

--- a/solution.py
+++ b/solution.py
@@ -25,7 +25,7 @@
 SMEM = pl.BlockSpec(memory_space=pltpu.SMEM)
 
 
-def call(kernel, out_shape, ins, scratch=(), fetch=(), cost=None, limit=48 << 20):
+def call(kernel, out_shape, ins, scratch=(), fetch=(), mib=8):
     multi = isinstance(out_shape, (tuple, list))
 
     def body(*refs):
@@ -50,16 +50,19 @@
         held.append(pltpu.SemaphoreType.DMA((len(fetch),)))
     place = [SMEM] + [VMEM] * (len(ins) - 1)
     for at in fetch:
-        place[at] = pl.BlockSpec(memory_space=pl.ANY)
+        place[at] = pl.BlockSpec(memory_space=pltpu.HBM)
     return pl.pallas_call(
         body,
         out_shape=out_shape,
         in_specs=place,
         out_specs=[VMEM] * len(out_shape) if multi else VMEM,
         scratch_shapes=list(scratch) + held,
-        compiler_params=pltpu.CompilerParams(vmem_limit_bytes=limit),
-        cost_estimate=cost,
-    )(*ins)
+        compiler_params=pltpu.CompilerParams(vmem_limit_bytes=mib << 20),
+    )(*[in_hbm(v) if i in fetch else v for i, v in enumerate(ins)])
+
+
+def in_hbm(array):
+    return pltpu.with_memory_space_constraint(array, pltpu.HBM)
 
 
 def nn(a, b):
@@ -95,6 +98,14 @@
         "seq",
         [(y * SIDE + x, (y + d) % SIDE * SIDE + x) for y in range(SIDE) for x in range(SIDE)],
     )
+
+
+NEIGHBOURS = (0, 1, SIDE, SIDE + 1)
+SQUARES = (0, 2, 2 * SIDE, 2 * SIDE + 2)
+
+
+def swap(array, mask):
+    return lax.ppermute(array, "seq", [(i, i ^ mask) for i in range(SIDE * SIDE)])
 
 
 def along_x(array):
@@ -122,14 +133,26 @@
 
 def head_rows(ref):
     raw = ref[...].astype(f32)
-    heads = [raw[:, h * 576 : (h + 1) * 576] for h in range(8)]
-    wanted = raw[:, 8 * 576 : 8 * 576 + 1]
+    heads = [raw[h // 4 * 8 : h // 4 * 8 + 8, h % 4 * 576 : h % 4 * 576 + 576] for h in range(8)]
+    wanted = raw[:8, 4 * 576 : 4 * 576 + 1]
     return jnp.concatenate(heads, axis=0).astype(bf16), jnp.concatenate([wanted] * 8, axis=0)
 
 
-def resident_kernel(lens, q_ref, cache_ref, m_ref, l_ref, w_ref):
+def resident_kernel(lens, q_ref, cache_hbm, k0, k1, k2, k3, state_ref, stack, cache_ref, held, sem, ins, out_sem):
+    cache_copy = pltpu.make_async_copy(cache_hbm, cache_ref, sem)
+    cache_copy.start()
+    copies = [
+        pltpu.make_async_copy(k, held.at[d], ins.at[d]) for d, k in enumerate((k0, k1, k2, k3))
+    ]
+    for copy in copies:
+        copy.start()
+    queries, _ = head_rows(q_ref)
+    for copy in copies:
+        copy.wait()
+    out = pltpu.make_async_copy(held, stack, out_sem)
+    out.start()
+    cache_copy.wait()
     count = cache_ref.shape[0]
-    queries, _ = head_rows(q_ref)
     row = lax.rem(lax.broadcasted_iota(jnp.int32, (queries.shape[0], 128), 0), count)
     column = lax.broadcasted_iota(jnp.int32, (queries.shape[0], 128), 1)
     scores = []
@@ -146,13 +169,36 @@
         p = jnp.where((row == r) & (column < lens[r]), jnp.exp(scores[r] - m), 0.0)
         total += p
         weighted += nt(p.astype(bf16), cache_ref[r, :LATENT])
-    m_ref[...] = m
-    l_ref[...] = jnp.sum(total, axis=1, keepdims=True)
-    w_ref[...] = weighted
+    state_ref[:, :LATENT] = weighted
+    state_ref[:, LATENT : LATENT + 128] = jnp.broadcast_to(m, total.shape)
+    state_ref[:, LATENT + 128 :] = jnp.broadcast_to(jnp.sum(total, axis=1, keepdims=True), total.shape)
+    out.wait()
+
+
+def resident_attention(cache_len, packet, dec_cache, pieces):
+    hbm = pl.BlockSpec(memory_space=pltpu.HBM)
+    stack = (SIDE,) + pieces[0].shape
+    return pl.pallas_call(
+        resident_kernel,
+        out_shape=[
+            jax.ShapeDtypeStruct((64, LATENT + 256), f32),
+            jax.ShapeDtypeStruct(stack, bf16),
+        ],
+        in_specs=[SMEM, VMEM] + [hbm] * 5,
+        out_specs=[VMEM, hbm],
+        scratch_shapes=[
+            pltpu.VMEM(dec_cache.shape, bf16),
+            pltpu.VMEM(stack, bf16),
+            pltpu.SemaphoreType.DMA,
+            pltpu.SemaphoreType.DMA((SIDE,)),
+            pltpu.SemaphoreType.DMA,
+        ],
+        compiler_params=pltpu.CompilerParams(vmem_limit_bytes=8 << 20),
+    )(cache_len, packet, in_hbm(dec_cache), *[in_hbm(piece) for piece in pieces])
 
 
 def span_kernel(
-    info, q0, q1, q2, q3, k0, k1, k2, k3, kp, w_uv, rm, rl, rw, out_ref, scr
+    info, q0, q1, q2, q3, k0, k1, k2, k3, kp, w_uv, state, out_ref, scr
 ):
     group = info[0].astype(f32)
     y = info[1]
@@ -170,13 +216,16 @@
     weighted = nt(jnp.where(own, p, 0.0).astype(bf16), own_keys[:LATENT]) + nt(
         jnp.where(own, 0.0, p).astype(bf16), far_keys[:LATENT]
     )
-    here = rm.shape[0]
-    newest = jnp.maximum(m[:here], rm[...])
+    here = state.shape[0]
+    rw = state[:, :LATENT]
+    rm = state[:, LATENT : LATENT + 1]
+    rl = state[:, LATENT + 128 : LATENT + 129]
+    newest = jnp.maximum(m[:here], rm)
     a = jnp.exp(m[:here] - newest)
-    b = jnp.exp(rm[...] - newest)
+    b = jnp.exp(rm - newest)
     m = jnp.concatenate([newest, m[here:]], axis=0)
-    total = jnp.concatenate([total[:here] * a + rl[...] * b, total[here:]], axis=0)
-    weighted = jnp.concatenate([weighted[:here] * a + rw[...] * b, weighted[here:]], axis=0)
+    total = jnp.concatenate([total[:here] * a + rl * b, total[here:]], axis=0)
+    weighted = jnp.concatenate([weighted[:here] * a + rw * b, weighted[here:]], axis=0)
     some = total > 0.0
     safe = jnp.where(some, total, 1.0)
     latent = (weighted / safe).reshape(SIDE, 8, 8, LATENT)
@@ -238,13 +287,23 @@
     packed_ref[:, features:] = extra.astype(bf16)
 
 
-def expert_kernel(info, near_ref, far_ref, w_ref, act_ref, place_ref, gate_ref):
+def expert_kernel(info, near_ref, far_ref, w_hbm, act_ref, place_ref, gate_ref, w_ref, sems):
+    copies = [
+        pltpu.make_async_copy(
+            w_hbm.at[:, pl.ds(i * SIDE, SIDE)], w_ref.at[:, pl.ds(i * SIDE, SIDE)], sems.at[i]
+        )
+        for i in range(SIDE)
+    ]
+    for copy in copies:
+        copy.start()
     shards, half, _ = near_ref.shape
     features, block = w_ref.shape[2], 16
     rows, slots = 2 * half, act_ref.shape[0]
     both = jnp.zeros((rows, 256), f32)
     tails = jnp.zeros((rows, 64), f32)
     for s in range(shards):
+        if s % SIDE == 0:
+            copies[s // SIDE].wait()
         x = jnp.concatenate([near_ref[s], far_ref[s]], axis=0)
         both += nn(x[:, :features], jnp.concatenate([w_ref[0, s], w_ref[1, s]], axis=1))
         tails += x[:, features:].astype(f32)
@@ -269,12 +328,64 @@
     act_ref[...] = tn(place, act).astype(bf16)
 
 
+def experts(info, near, far, w_in):
+    slots = 16 * CAP
+    return pl.pallas_call(
+        expert_kernel,
+        out_shape=[
+            jax.ShapeDtypeStruct((slots, 128), bf16),
+            jax.ShapeDtypeStruct((256, slots), bf16),
+            jax.ShapeDtypeStruct((256, 1), f32),
+        ],
+        in_specs=[SMEM, VMEM, VMEM, pl.BlockSpec(memory_space=pltpu.HBM)],
+        out_specs=[VMEM, VMEM, VMEM],
+        scratch_shapes=[pltpu.VMEM(w_in.shape, bf16), pltpu.SemaphoreType.DMA((SIDE,))],
+        compiler_params=pltpu.CompilerParams(vmem_limit_bytes=16 << 20),
+    )(info, near, far, in_hbm(w_in))
+
+
+def cut_down_kernel(info, w_hbm, o0, o1, o2, o3, w_ref, held, w_sem, sems):
+    features = o0.shape[1]
+    whole = pltpu.make_async_copy(w_hbm, w_ref, w_sem)
+    whole.start()
+    whole.wait()
+    for place in range(SIDE):
+        step = jnp.bitwise_xor(info[6], place)
+        for square in range(SIDE):
+            at = (NEIGHBOURS[place] + SQUARES[square]) * features
+            held[step, square] = w_ref[:, at : at + features].T
+    copies = [
+        pltpu.make_async_copy(held.at[d], out, sems.at[d]) for d, out in enumerate((o0, o1, o2, o3))
+    ]
+    for copy in copies:
+        copy.start()
+    for copy in copies:
+        copy.wait()
+
+
+def cut_down(info, w_down, features):
+    anywhere = pl.BlockSpec(memory_space=pltpu.HBM)
+    shape = (SIDE, features, w_down.shape[0])
+    return pl.pallas_call(
+        cut_down_kernel,
+        out_shape=[pltpu.HBM(shape, bf16)] * SIDE,
+        in_specs=[SMEM, anywhere],
+        out_specs=[anywhere] * SIDE,
+        scratch_shapes=[
+            pltpu.VMEM(w_down.shape, bf16),
+            pltpu.VMEM((SIDE,) + shape, bf16),
+            pltpu.SemaphoreType.DMA,
+            pltpu.SemaphoreType.DMA((SIDE,)),
+        ],
+        compiler_params=pltpu.CompilerParams(vmem_limit_bytes=8 << 20),
+    )(info, in_hbm(w_down))
+
+
 def down_kernel(info, a0, a1, a2, a3, w0, w1, w2, w3, place_ref, gate_ref, near_ref, far_ref):
-    y = info[1]
     place, gates = place_ref[...], gate_ref[...]
     half = near_ref.shape[1]
     for d in range(SIDE):
-        to = lax.rem(y + d, SIDE)
+        to = jnp.bitwise_xor(info[7], d)
         total = sum(nt(a[...], w[to]) for a, w in ((a0, w0), (a1, w1), (a2, w2), (a3, w3)))
         high = total.astype(bf16)
         low = (total - high.astype(f32)).astype(bf16)
@@ -343,7 +454,7 @@
             pltpu.VMEM((pieces, heads * tokens, 256), f32),
             pltpu.VMEM((heads * tokens, LATENT), f32),
         ],
-        compiler_params=pltpu.CompilerParams(vmem_limit_bytes=48 << 20),
+        compiler_params=pltpu.CompilerParams(vmem_limit_bytes=32 << 20),
         cost_estimate=pl.CostEstimate(
             flops=2 * 8 * tokens * 4096 * 1088, bytes_accessed=8 << 20, transcendentals=8 * tokens * 4096
         ),
@@ -374,61 +485,34 @@
     shards = lax.axis_size("seq")
     depth = lax.axis_size("expert")
     info = jnp.stack(
-        [group, seq // SIDE, seq % SIDE, group * depth + z, seq, prefix_len[0], z, z]
+        [
+            group,
+            seq // SIDE,
+            seq % SIDE,
+            group * depth + z,
+            seq,
+            prefix_len[0],
+            seq % 2 + seq // SIDE % 2 * 2,
+            seq // 2 % 2 + seq // (2 * SIDE) * 2,
+        ]
     ).astype(jnp.int32)
     features = x_dec.shape[1]
 
     wanted = jnp.broadcast_to(requests.astype(bf16)[:, None], (8, 128))
-    packet = jnp.concatenate([q_dec, wanted], axis=1)
+    packet = jnp.concatenate(
+        [
+            jnp.concatenate([q_dec[:, : 4 * 576], wanted], axis=1),
+            jnp.concatenate([q_dec[:, 4 * 576 :], wanted], axis=1),
+        ],
+        axis=0,
+    )
     span, packet, prefix, columns = lax.optimization_barrier(
         (span_cache[0], packet, prefix_cache[0], span_cache[0])
     )
     keys = lax.all_gather(jnp.concatenate([prefix, columns], axis=1), "seq", axis=0)
     pieces, packets = along_x(span), along_y(packet)
-    resident = call(
-        resident_kernel,
-        [
-            jax.ShapeDtypeStruct((64, 1), f32),
-            jax.ShapeDtypeStruct((64, 1), f32),
-            jax.ShapeDtypeStruct((64, LATENT), f32),
-        ],
-        [cache_len, packet, dec_cache],
-    )
-    w_back = w_down[0].T.reshape(SIDE, SIDE, features, 128).transpose(1, 0, 2, 3)
-    pieces, packets, resident, w_back = lax.optimization_barrier(
-        (pieces, packets, resident, w_back)
-    )
-    far = other_core(jnp.stack(pieces))
-    part = call(
-        span_kernel,
-        jax.ShapeDtypeStruct((32, 9 * VDIM), bf16),
-        [info, *packets, *pieces, far, w_uv, *resident],
-        [pltpu.VMEM((SIDE, 8, 9 * VDIM), f32)],
-        fetch=(5, 6, 7, 8, 9),
-    )
-
-    dec_val = call(
-        merge_kernel,
-        jax.ShapeDtypeStruct((32, 8 * VDIM), bf16),
-        [info, *along_y(part)],
-        fetch=(1, 2, 3, 4),
-    )
-    product = call(
-        project_kernel,
-        jax.ShapeDtypeStruct((128, features), bf16),
-        [info, *along_x(dec_val), w_out.T],
-        [pltpu.VMEM((SIDE, SIDE, 8, features), f32)],
-        fetch=(1, 2, 3, 4),
-    )
-    product, w_back = lax.optimization_barrier((product, w_back))
-    x_here = seq % SIDE
-    w_back = [
-        lax.dynamic_index_in_dim(w_back, (x_here + d) % SIDE, 0, keepdims=False)
-        for d in range(SIDE)
-    ]
-    w_back = [w_back[0]] + [to_x(w_back[d], d) for d in range(1, SIDE)]
-    terms = lax.all_to_all(product.reshape(depth, 16, features), "expert", 0, 0, tiled=True)
-
+    pieces, packets = lax.optimization_barrier((pieces, packets))
+    resident, stacked = resident_attention(cache_len, packets[0], dec_cache, pieces)
     g_high = lax.reduce_precision(expert_gates, 8, 7)
     g_mid = lax.reduce_precision(expert_gates - g_high, 8, 7)
     g_low = lax.reduce_precision(expert_gates - g_high - g_mid, 8, 7)
@@ -436,6 +520,33 @@
         [expert_ids.astype(f32), g_high, g_mid, g_low, jnp.zeros((16, 32), f32)], axis=1
     )
     gain = lax.dynamic_slice(norm_gain, (seq * features,), (features,))[None]
+    part = call(
+        span_kernel,
+        jax.ShapeDtypeStruct((32, 9 * VDIM), bf16),
+        [info, *packets, *pieces, other_core(stacked), w_uv, resident],
+        [pltpu.VMEM((SIDE, 8, 9 * VDIM), f32)],
+        fetch=tuple(range(1, 11)),
+        mib=16,
+    )
+    part, w_back = lax.optimization_barrier((part, w_down[0]))
+    parts = along_y(part)
+    w_back = cut_down(info, w_back, features)
+    parts, w_back = lax.optimization_barrier((parts, w_back))
+    *w_back, diagonal = [w_back[0]] + [swap(w_back[d], NEIGHBOURS[d]) for d in (1, 2)] + [w_back[3]]
+    dec_val = call(
+        merge_kernel,
+        jax.ShapeDtypeStruct((32, 8 * VDIM), bf16),
+        [info, *parts],
+    )
+    values = along_x(dec_val)
+    product = call(
+        project_kernel,
+        jax.ShapeDtypeStruct((128, features), bf16),
+        [info, *values, w_out.T],
+        [pltpu.VMEM((SIDE, SIDE, 8, features), f32)],
+    )
+    terms = lax.all_to_all(product.reshape(depth, 16, features), "expert", 0, 0, tiled=True)
+
     hidden, packed = call(
         hidden_kernel,
         [
@@ -445,27 +556,23 @@
         [info, terms, x_dec, gain, extra],
     )
     rows = everyone(packed, "expert", depth).reshape(16 * depth, features + 64)
-    rows, q_pre, keys, w_back = lax.optimization_barrier((rows, q_pre, keys, w_back))
+    rows, q_pre, w_back = lax.optimization_barrier((rows, q_pre, w_back))
     arrived = everyone(rows, "seq", shards)
     o_pre = prompt_attention(info, q_pre[0], keys)[None]
-    arrived, o_pre = lax.optimization_barrier((arrived, o_pre))
-    act, place, gate = call(
-        expert_kernel,
-        [
-            jax.ShapeDtypeStruct((16 * CAP, 128), bf16),
-            jax.ShapeDtypeStruct((256, 16 * CAP), bf16),
-            jax.ShapeDtypeStruct((256, 1), f32),
-        ],
-        [info, arrived, other_core(arrived), w_in[0].reshape(2, shards, features, 128)],
+    arrived, o_pre, diagonal = lax.optimization_barrier((arrived, o_pre, diagonal))
+    w_back.append(swap(diagonal, NEIGHBOURS[3]))
+    act, place, gate = experts(
+        info, arrived, other_core(arrived), w_in[0].reshape(2, shards, features, 128)
     )
     shape = (SIDE, 16 * depth, features)
     near, far_share = call(
         down_kernel,
         [jax.ShapeDtypeStruct(shape, f32), jax.ShapeDtypeStruct(shape, bf16)],
-        [info, *along_x(act), *w_back, place, gate],
+        [info, act, *[swap(act, mask) for mask in NEIGHBOURS[1:]], *w_back, place, gate],
+        mib=16,
     )
     share = (near + other_core(far_share).astype(f32)).astype(bf16)
-    parts = [share[0]] + [to_y(share[d], d) for d in range(1, SIDE)]
+    parts = [share[0]] + [swap(share[d], SQUARES[d]) for d in range(1, SIDE)]
     share = sum(v.astype(f32) for v in parts).astype(bf16)
     shares = lax.all_to_all(share.reshape(depth, 16, features), "expert", 0, 0, tiled=True)
     h_out = (hidden.astype(f32) + jnp.sum(shares.astype(f32), axis=0)).astype(bf16)

time: 186 us -> 176 us (0.946)
  blocking collectives: 24.9 us -> 10.1 us
  waiting for transfers between devices: 39.5 us -> 51.6 us
  local copies, waits for them, and re-layouts: 18 us -> 10.1 us
  Pallas kernels: 29.8 us -> 36.7 us
  starting transfers between devices: 51.5 us -> 48.8 us
    pallas_call x0 -> x3, Pallas kernels: none -> 12.1 us  [the longest x1 4.6 us: cut_down(): pl.pallas_call(cut_down_kernel, out_shape=[pltpu.HBM(shape, bf16)] * SIDE...]
    ppermute x0 -> x9, waiting for transfers between devices: none -> 11.6 us  [swap(): lax.ppermute(array, 'seq', [(i, i ^ mask) for i in range(SIDE * SIDE)])]
    all_to_all x1 -> x0, blocking collectives: 10.3 us -> none  [everyone(): lax.all_to_all(jnp.broadcast_to(array[None], (count,) + array.shape), axi...]
    ppermute x0 -> x9, starting transfers between devices: none -> 10.1 us  [swap(): lax.ppermute(array, 'seq', [(i, i ^ mask) for i in range(SIDE * SIDE)])]
    all_to_all x1 -> x2, waiting for transfers between devices: 5.53 us -> 13.4 us  [everyone(): lax.all_to_all(jnp.broadcast_to(array[None], (count,) + array.shape), axi...]
    unnamed x42 -> x33, local copies, waits for them, and re-layouts: 13.7 us -> 5.84 us
    ppermute x12 -> x6, starting transfers between devices: 13.2 us -> 6.04 us  [to_x(): lax.ppermute(array, 'seq', [(y * SIDE + x, y * SIDE + (x + d) % SIDE) for...]
    ppermute x9 -> x6, starting transfers between devices: 11.6 us -> 6.23 us  [to_y(): lax.ppermute(array, 'seq', [(y * SIDE + x, (y + d) % SIDE * SIDE + x) for...]
  transfers between devices with their start and end apart: 27 -> 28, of which waited for: 17 -> 18; matrix products, arithmetic and copies ran while one was open for 4% -> 2% of each run, Pallas kernels for 13% -> 19%
where the time goes in v3:
time: 176 us
  waiting for transfers between devices  51.6 us (29%)
  starting transfers between devices  48.8 us (28%)
  Pallas kernels  36.7 us (21%)
  between operations  14.9 us (8%)
  local copies, waits for them, and re-layouts  10.1 us (6%)
  blocking collectives  10.1 us (6%)
  other arithmetic  3.32 us (2%)
    pallas_call x1, Pallas kernels, prompt_attention(): pl.pallas_call(prompt_kernel, out_shape=jax.ShapeDtypeStruct((tokens, ste...  14.9 us
    all_to_all x2, waiting for transfers between devices, everyone(): lax.all_to_all(jnp.broadcast_to(array[None], (count,) + array.shape), axi...  13.4 us
    ppermute x9, waiting for transfers between devices, swap(): lax.ppermute(array, 'seq', [(i, i ^ mask) for i in range(SIDE * SIDE)])  11.6 us
    all_to_all x1, blocking collectives, on_device(): lax.all_to_all(share.reshape(depth, 16, features), 'expert', 0, 0, tiled=...  10.1 us
    ppermute x9, starting transfers between devices, swap(): lax.ppermute(array, 'seq', [(i, i ^ mask) for i in range(SIDE * SIDE)])  10.1 us
    pallas_call x5, Pallas kernels, call(): pl.pallas_call(body, out_shape=out_shape, in_specs=place, out_specs=[VMEM...  9.73 us
    all_to_all x1, starting transfers between devices, on_device(): lax.all_to_all(product.reshape(depth, 16, features), 'expert', 0, 0, tile...  9.51 us
    ppermute x3, starting transfers between devices, other_core(): return lax.ppermute(array, 'group', [(0, 1), (1, 0)])  9.28 us
  transfers between devices with their start and end apart: 28, of which 18 were waited for; matrix products, arithmetic and copies ran while one was open for 2% of the time, Pallas kernels for 19%

profile of v3, /device:TPU:1, one launch (start us, length us, event | category | flops | bytes accessed | tf_op | source)
XLA Modules:
  0.0 175.6 jit_solution(10285027912838937636)
XLA Ops:
  10.5 3.6 %collective-permute-start.5 = (bf16[16,2432]{1,0:T(8,128)(2,1)S(1)}, bf16[16,2432]{1,0:T(8,128)(2,1)S(1)}, u32[]{:S(2)}, u32[]{:S(2)}) collective-permute-start(bf16[16,2432]{1,0:T(8,128)(2,1)S(1)} %maximum_maximum_fusion.q_ref.refs_1_), channel_id=1, source_target_pairs={{0,96},{8,104},{16,112},{24,120},{32,0},{40,8},{48,16},{56,24},{64... | collective-permute-start | bytes 233480 | tf_op jit(solution)/shard_map/ppermute | solution.py:96
  14.2 2.5 %collective-permute-start.2 = (bf16[576,128]{1,0:T(8,128)(2,1)}, bf16[576,128]{1,0:T(8,128)(2,1)S(1)}, u32[]{:S(2)}, u32[]{:S(2)}) collective-permute-start(bf16[576,128]{1,0:T(8,128)(2,1)} %bitcast.37), channel_id=1, source_target_pairs={{0,24},{8,0},{16,8},{24,16},{32,56},{40,32},{48,40},{56,48},{64,88... | collective-permute-start | bytes 442376 | tf_op jit(solution)/shard_map/ppermute | solution.py:88
  18.8 3.8 %collective-permute-done.4.refs_3_ = bf16[16,2432]{1,0:T(8,128)(2,1)S(1)} collective-permute-done((bf16[16,2432]{1,0:T(8,128)(2,1)S(1)}, bf16[16,2432]{1,0:T(8,128)(2,1)S(1)}, u32[]{:S(2)}, u32[]{:S(2)}) %collective-permute-start.4) | collective-permute-done | bytes 77856 | tf_op jit(solution)/shard_map/ppermute | solution.py:96
  23.7 3.2 %collective-permute-done.k1.refs_6_ = bf16[576,128]{1,0:T(8,128)(2,1)S(1)} collective-permute-done((bf16[576,128]{1,0:T(8,128)(2,1)}, bf16[576,128]{1,0:T(8,128)(2,1)S(1)}, u32[]{:S(2)}, u32[]{:S(2)}) %collective-permute-start) | collective-permute-done | bytes 147488 | tf_op jit(solution)/shard_map/ppermute | solution.py:88
  28.3 3.1 %shard_map.167 = (f32[64,768]{1,0:T(8,128)S(1)}, bf16[4,576,128]{2,1,0:T(8,128)(2,1)S(1)}) custom-call(s32[8]{0:T(128)S(1)} %copy-done.4, bf16[16,2432]{1,0:T(8,128)(2,1)S(1)} %maximum_maximum_fusion.q_ref.refs_1_, bf16[8,576,128]{2,1,0:T(8,128)(2,1)} %cache_hbm.1, bf16[576,128]{1,0:T(8,128)(2,1)} %bitcast.40, bf16[576,128]{1,0:T(8,128)(2,1)} %copy-done.9, ...), custom_call_target="tpu_custom_call" | custom-call | tf_op jit(solution)/shard_map/pallas_call | solution.py:181
  34.8 3.9 %shard_map.168.refs_1_ = bf16[32,1152]{1,0:T(8,128)(2,1)S(1)} custom-call(s32[8]{0:T(128)S(1)} %stack.31.refs_0_.info, bf16[16,2432]{1,0:T(8,128)(2,1)} %copy-done.1, bf16[16,2432]{1,0:T(8,128)(2,1)} %copy-done.13, bf16[16,2432]{1,0:T(8,128)(2,1)} %copy-done.12, bf16[16,2432]{1,0:T(8,128)(2,1)} %copy-done.11, bf16[576,128]{1,0:T(8,128)(2,1)} %bitcast.41, ...), custom_call_target="tpu_custom_call" | custom-call | tf_op jit(solution)/shard_map/pallas_call | solution.py:54
  40.2 4.6 %shard_map.169 = (bf16[4,448,128]{2,1,0:T(8,128)(2,1)}, bf16[4,448,128]{2,1,0:T(8,128)(2,1)}, bf16[4,448,128]{2,1,0:T(8,128)(2,1)}, bf16[4,448,128]{2,1,0:T(8,128)(2,1)}) custom-call(s32[8]{0:T(128)S(1)} %stack.31.refs_0_.info, bf16[128,7168]{1,0:T(8,128)(2,1)} %bitcast.35), custom_call_target="tpu_custom_call" | custom-call | tf_op jit(solution)/shard_map/pallas_call | solution.py:369
  56.8 9.5 %all-to-all-start = ((bf16[8,16,448]{2,1,0:T(8,128)(2,1)}), bf16[8,16,448]{2,1,0:T(8,128)(2,1)S(1)}, u32[]{:S(2)}, u32[]{:S(2)}) async-start(bf16[8,16,448]{2,1,0:T(8,128)(2,1)} %bitcast.11), calls=%async_computation | async-start | bytes 262144 | tf_op jit(solution)/shard_map/all_to_all | solution.py:548
  66.4 7.9 %all-to-all-done.refs_1_ = bf16[8,16,448]{2,1,0:T(8,128)(2,1)S(1)} async-done(((bf16[8,16,448]{2,1,0:T(8,128)(2,1)}), bf16[8,16,448]{2,1,0:T(8,128)(2,1)S(1)}, u32[]{:S(2)}, u32[]{:S(2)}) %all-to-all-start) | async-done | bytes 114720 | tf_op jit(solution)/shard_map/all_to_all | solution.py:548
  75.8 3.4 %all-to-all-start.1 = ((bf16[8,16,512]{2,1,0:T(8,128)(2,1)}), bf16[8,16,512]{2,1,0:T(8,128)(2,1)S(1)}, u32[]{:S(2)}, u32[]{:S(2)}) async-start(bf16[8,16,512]{2,1,0:T(8,128)(2,1)} %broadcast_in_dim.30), calls=%async_computation.1 | async-start | bytes 262144 | tf_op jit(solution)/shard_map/all_to_all | solution.py:124
  79.2 7.9 %all-to-all-done.1 = bf16[8,16,512]{2,1,0:T(8,128)(2,1)S(1)} async-done(((bf16[8,16,512]{2,1,0:T(8,128)(2,1)}), bf16[8,16,512]{2,1,0:T(8,128)(2,1)S(1)}, u32[]{:S(2)}, u32[]{:S(2)}) %all-to-all-start.1) | async-done | bytes 131104 | tf_op jit(solution)/shard_map/all_to_all | solution.py:124
  88.6 4.2 %all-to-all-start.2 = ((bf16[16,128,512]{2,1,0:T(8,128)(2,1)}), bf16[16,128,512]{2,1,0:T(8,128)(2,1)S(1)}, u32[]{:S(2)}, u32[]{:S(2)}) async-start(bf16[16,128,512]{2,1,0:T(8,128)(2,1)} %broadcast_in_dim.31), calls=%async_computation.2 | async-start | bytes 4194304 | tf_op jit(solution)/shard_map/all_to_all | solution.py:124
  92.9 2.3 %copy-done.5 = bf16[9216,256]{1,0:T(8,128)(2,1)S(1)} copy-done((bf16[9216,256]{1,0:T(8,128)(2,1)S(1)}, bf16[9216,256]{1,0:T(8,128)(2,1)}, u32[]{:S(2)}) %copy-start.5) | copy-done | bytes 4718616
  96.5 14.9 %shard_map.173 = bf16[128,4096]{1,0:T(8,128)(2,1)} custom-call(s32[8]{0:T(128)S(1)} %stack.31.refs_0_.info, bf16[128,4608]{1,0:T(8,128)(2,1)S(1)} %bitcast.33, bf16[16,576,256]{2,1,0:T(8,128)(2,1)S(1)} %bitcast.32), custom_call_target="tpu_custom_call" | custom-call | flops 9126805504 | bytes 8388608 | tf_op jit(solution)/shard_map/pallas_call | solution.py:443
  111.4 5.5 %all-to-all-done.2.near_ref = bf16[16,128,512]{2,1,0:T(8,128)(2,1)S(1)} async-done(((bf16[16,128,512]{2,1,0:T(8,128)(2,1)}), bf16[16,128,512]{2,1,0:T(8,128)(2,1)S(1)}, u32[]{:S(2)}, u32[]{:S(2)}) %all-to-all-start.2) | async-done | bytes 2097184 | tf_op jit(solution)/shard_map/all_to_all | solution.py:124
  116.9 7.7 %collective-permute-start.15 = (bf16[16,128,512]{2,1,0:T(8,128)(2,1)S(1)}, bf16[16,128,512]{2,1,0:T(8,128)(2,1)S(1)}, u32[]{:S(2)}, u32[]{:S(2)}) collective-permute-start(bf16[16,128,512]{2,1,0:T(8,128)(2,1)S(1)} %all-to-all-done.2.near_ref), channel_id=1, source_target_pairs={{0,128},{128,0},{1,129},{129,1},{2,130},{130,2},{3,131},{131,3},{4... | collective-permute-start | bytes 6291464 | tf_op jit(solution)/shard_map/ppermute | solution.py:120
  124.7 3.8 %collective-permute-done.15.far_ref = bf16[16,128,512]{2,1,0:T(8,128)(2,1)S(1)} collective-permute-done((bf16[16,128,512]{2,1,0:T(8,128)(2,1)S(1)}, bf16[16,128,512]{2,1,0:T(8,128)(2,1)S(1)}, u32[]{:S(2)}, u32[]{:S(2)}) %collective-permute-start.15) | collective-permute-done | bytes 2097184 | tf_op jit(solution)/shard_map/ppermute | solution.py:120
  128.5 4.4 %shard_map.174 = (bf16[192,128]{1,0:T(8,128)(2,1)S(1)}, bf16[256,192]{1,0:T(8,128)(2,1)S(1)}, f32[256,1]{1,0:T(8,128)S(1)}) custom-call(s32[8]{0:T(128)S(1)} %stack.31.refs_0_.info, bf16[16,128,512]{2,1,0:T(8,128)(2,1)S(1)} %all-to-all-done.2.near_ref, bf16[16,128,512]{2,1,0:T(8,128)(2,1)S(1)} %collective-permute-done.15.far_ref, ...), custom_call_target="tpu_custom_call" | custom-call | tf_op jit(solution)/shard_map/pallas_call | solution.py:333
  135.6 2.4 %collective-permute-done.19.refs_8_ = bf16[4,448,128]{2,1,0:T(8,128)(2,1)S(1)} collective-permute-done((bf16[4,448,128]{2,1,0:T(8,128)(2,1)}, bf16[4,448,128]{2,1,0:T(8,128)(2,1)S(1)}, u32[]{:S(2)}, u32[]{:S(2)}) %collective-permute-start.19) | collective-permute-done | bytes 458784 | tf_op jit(solution)/shard_map/ppermute | solution.py:108
  140.3 2.6 %shard_map.175 = (f32[4,128,448]{2,1,0:T(8,128)S(1)}, bf16[4,128,448]{2,1,0:T(8,128)(2,1)S(1)}) custom-call(s32[8]{0:T(128)S(1)} %stack.31.refs_0_.info, bf16[192,128]{1,0:T(8,128)(2,1)S(1)} %get-tuple-element.79.refs_1_, bf16[192,128]{1,0:T(8,128)(2,1)S(1)} %collective-permute-done.16.refs_2_, bf16[192,128]{1,0:T(8,128)(2,1)S(1)} %collective-permute-done.17.refs_3_, ...), custom_call_target="tpu_custom_call" | custom-call | tf_op jit(solution)/shard_map/pallas_call | solution.py:54
  145.4 3.6 %collective-permute-start.23 = (bf16[128,448]{1,0:T(8,128)(2,1)S(1)}, bf16[128,448]{1,0:T(8,128)(2,1)S(1)}, u32[]{:S(2)}, u32[]{:S(2)}) collective-permute-start(bf16[128,448]{1,0:T(8,128)(2,1)S(1)} %get-tuple-element.89), channel_id=1, source_target_pairs={{0,80},{8,88},{16,64},{24,72},{32,112},{40,120},{48,96},{56,104},{... | collective-permute-start | bytes 344072 | tf_op jit(solution)/shard_map/ppermute | solution.py:108
  151.6 3.5 %collective-permute-done.23 = bf16[128,448]{1,0:T(8,128)(2,1)S(1)} collective-permute-done((bf16[128,448]{1,0:T(8,128)(2,1)S(1)}, bf16[128,448]{1,0:T(8,128)(2,1)S(1)}, u32[]{:S(2)}, u32[]{:S(2)}) %collective-permute-start.23) | collective-permute-done | bytes 114720 | tf_op jit(solution)/shard_map/ppermute | solution.py:108
  155.0 2.8 %collective-permute-done.22 = bf16[128,448]{1,0:T(8,128)(2,1)S(1)} collective-permute-done((bf16[128,448]{1,0:T(8,128)(2,1)S(1)}, bf16[128,448]{1,0:T(8,128)(2,1)S(1)}, u32[]{:S(2)}, u32[]{:S(2)}) %collective-permute-start.22) | collective-permute-done | bytes 114720 | tf_op jit(solution)/shard_map/ppermute | solution.py:108
  157.9 10.1 %all_to_all.20 = bf16[8,16,448]{2,1,0:T(8,128)(2,1)S(1)} all-to-all(bf16[8,16,448]{2,1,0:T(8,128)(2,1)S(1)} %bitcast.43), channel_id=1, replica_groups=mesh['group'=2,'seq'=16,'expert'=8] {'expert'}, dimensions={0} | all-to-all | bytes 229376 | tf_op jit(solution)/shard_map/all_to_all | solution.py:577
  (97 shorter events, 39.3 us)
Async XLA Ops:
  7.2 85.7 %all-gather.3.cloned.1.call-start = ((), (), s32[]{:S(2)}) async-start(), calls=%async_computation.4 | async-start | bytes 5013504 | tf_op jit(solution)/shard_map/all_gather | solution.py:512
  10.5 7.6 %collective-permute-start.5 = (bf16[16,2432]{1,0:T(8,128)(2,1)S(1)}, bf16[16,2432]{1,0:T(8,128)(2,1)S(1)}, u32[]{:S(2)}, u32[]{:S(2)}) collective-permute-start(bf16[16,2432]{1,0:T(8,128)(2,1)S(1)} %maximum_maximum_fusion.q_ref.refs_1_), channel_id=1, source_target_pairs={{0,96},{8,104},{16,112},{24,120},{32,0},{40,8},{48,16},{56,24},{64... | collective-permute-start | bytes 233480 | tf_op jit(solution)/shard_map/ppermute | solution.py:96
  14.2 9.5 %collective-permute-start.2 = (bf16[576,128]{1,0:T(8,128)(2,1)}, bf16[576,128]{1,0:T(8,128)(2,1)S(1)}, u32[]{:S(2)}, u32[]{:S(2)}) collective-permute-start(bf16[576,128]{1,0:T(8,128)(2,1)} %bitcast.37), channel_id=1, source_target_pairs={{0,24},{8,0},{16,8},{24,16},{32,56},{40,32},{48,40},{56,48},{64,88... | collective-permute-start | bytes 442376 | tf_op jit(solution)/shard_map/ppermute | solution.py:88
  16.7 7.0 %collective-permute-start.1 = (bf16[576,128]{1,0:T(8,128)(2,1)}, bf16[576,128]{1,0:T(8,128)(2,1)S(1)}, u32[]{:S(2)}, u32[]{:S(2)}) collective-permute-start(bf16[576,128]{1,0:T(8,128)(2,1)} %bitcast.38), channel_id=1, source_target_pairs={{0,16},{8,24},{16,0},{24,8},{32,48},{40,56},{48,32},{56,40},{64,80... | collective-permute-start | bytes 442376 | tf_op jit(solution)/shard_map/ppermute | solution.py:88
  17.2 9.8 %collective-permute-start = (bf16[576,128]{1,0:T(8,128)(2,1)}, bf16[576,128]{1,0:T(8,128)(2,1)S(1)}, u32[]{:S(2)}, u32[]{:S(2)}) collective-permute-start(bf16[576,128]{1,0:T(8,128)(2,1)} %bitcast.39), channel_id=1, source_target_pairs={{0,8},{8,16},{16,24},{24,0},{32,40},{40,48},{48,56},{56,32},{64,72... | collective-permute-start | bytes 442376 | tf_op jit(solution)/shard_map/ppermute | solution.py:88
  18.1 5.5 %collective-permute-start.3 = (bf16[16,2432]{1,0:T(8,128)(2,1)S(1)}, bf16[16,2432]{1,0:T(8,128)(2,1)S(1)}, u32[]{:S(2)}, u32[]{:S(2)}) collective-permute-start(bf16[16,2432]{1,0:T(8,128)(2,1)S(1)} %maximum_maximum_fusion.q_ref.refs_1_), channel_id=1, source_target_pairs={{0,32},{8,40},{16,48},{24,56},{32,64},{40,72},{48,80},{56,88},{64,... | collective-permute-start | bytes 233480 | tf_op jit(solution)/shard_map/ppermute | solution.py:96
  38.7 6.2 %collective-permute-start.9 = (bf16[32,1152]{1,0:T(8,128)(2,1)S(1)}, bf16[32,1152]{1,0:T(8,128)(2,1)S(1)}, u32[]{:S(2)}, u32[]{:S(2)}) collective-permute-start(bf16[32,1152]{1,0:T(8,128)(2,1)S(1)} %shard_map.168.refs_1_), channel_id=1, source_target_pairs={{0,96},{8,104},{16,112},{24,120},{32,0},{40,8},{48,16},{56,24},{64... | collective-permute-start | bytes 221192 | tf_op jit(solution)/shard_map/ppermute | solution.py:96
  39.3 5.5 %collective-permute-start.8 = (bf16[32,1152]{1,0:T(8,128)(2,1)S(1)}, bf16[32,1152]{1,0:T(8,128)(2,1)S(1)}, u32[]{:S(2)}, u32[]{:S(2)}) collective-permute-start(bf16[32,1152]{1,0:T(8,128)(2,1)S(1)} %shard_map.168.refs_1_), channel_id=1, source_target_pairs={{0,64},{8,72},{16,80},{24,88},{32,96},{40,104},{48,112},{56,120},{... | collective-permute-start | bytes 221192 | tf_op jit(solution)/shard_map/ppermute | solution.py:96
  39.4 7.0 %collective-permute-start.7 = (bf16[32,1152]{1,0:T(8,128)(2,1)S(1)}, bf16[32,1152]{1,0:T(8,128)(2,1)S(1)}, u32[]{:S(2)}, u32[]{:S(2)}) collective-permute-start(bf16[32,1152]{1,0:T(8,128)(2,1)S(1)} %shard_map.168.refs_1_), channel_id=1, source_target_pairs={{0,32},{8,40},{16,48},{24,56},{32,64},{40,72},{48,80},{56,88},{64,... | collective-permute-start | bytes 221192 | tf_op jit(solution)/shard_map/ppermute | solution.py:96
  47.2 5.1 %collective-permute-start.12 = (bf16[32,1024]{1,0:T(8,128)(2,1)S(1)}, bf16[32,1024]{1,0:T(8,128)(2,1)S(1)}, u32[]{:S(2)}, u32[]{:S(2)}) collective-permute-start(bf16[32,1024]{1,0:T(8,128)(2,1)S(1)} %shard_map.170.refs_1_), channel_id=1, source_target_pairs={{0,24},{8,0},{16,8},{24,16},{32,56},{40,32},{48,40},{56,48},{64,88... | collective-permute-start | bytes 196616 | tf_op jit(solution)/shard_map/ppermute | solution.py:88
  49.7 5.5 %collective-permute-start.10 = (bf16[32,1024]{1,0:T(8,128)(2,1)S(1)}, bf16[32,1024]{1,0:T(8,128)(2,1)S(1)}, u32[]{:S(2)}, u32[]{:S(2)}) collective-permute-start(bf16[32,1024]{1,0:T(8,128)(2,1)S(1)} %shard_map.170.refs_1_), channel_id=1, source_target_pairs={{0,8},{8,16},{16,24},{24,0},{32,40},{40,48},{48,56},{56,32},{64,72... | collective-permute-start | bytes 196616 | tf_op jit(solution)/shard_map/ppermute | solution.py:88
  49.7 29.5 %collective-permute-start.13 = (bf16[4,448,128]{2,1,0:T(8,128)(2,1)}, bf16[4,448,128]{2,1,0:T(8,128)(2,1)S(1)}, u32[]{:S(2)}, u32[]{:S(2)}) collective-permute-start(bf16[4,448,128]{2,1,0:T(8,128)(2,1)} %get-tuple-element.69), channel_id=1, source_target_pairs={{0,8},{8,0},{16,24},{24,16},{32,40},{40,32},{48,56},{56,48},{64,72... | collective-permute-start | bytes 1376264 | tf_op jit(solution)/shard_map/ppermute | solution.py:108
  51.0 28.1 %collective-permute-start.14 = (bf16[4,448,128]{2,1,0:T(8,128)(2,1)}, bf16[4,448,128]{2,1,0:T(8,128)(2,1)S(1)}, u32[]{:S(2)}, u32[]{:S(2)}) collective-permute-start(bf16[4,448,128]{2,1,0:T(8,128)(2,1)} %get-tuple-element.70), channel_id=1, source_target_pairs={{0,32},{8,40},{16,48},{24,56},{32,0},{40,8},{48,16},{56,24},{64,96... | collective-permute-start | bytes 1376264 | tf_op jit(solution)/shard_map/ppermute | solution.py:108
  56.8 17.5 %all-to-all-start = ((bf16[8,16,448]{2,1,0:T(8,128)(2,1)}), bf16[8,16,448]{2,1,0:T(8,128)(2,1)S(1)}, u32[]{:S(2)}, u32[]{:S(2)}) async-start(bf16[8,16,448]{2,1,0:T(8,128)(2,1)} %bitcast.11), calls=%async_computation | async-start | bytes 262144 | tf_op jit(solution)/shard_map/all_to_all | solution.py:548
  75.8 11.3 %all-to-all-start.1 = ((bf16[8,16,512]{2,1,0:T(8,128)(2,1)}), bf16[8,16,512]{2,1,0:T(8,128)(2,1)S(1)}, u32[]{:S(2)}, u32[]{:S(2)}) async-start(bf16[8,16,512]{2,1,0:T(8,128)(2,1)} %broadcast_in_dim.30), calls=%async_computation.1 | async-start | bytes 262144 | tf_op jit(solution)/shard_map/all_to_all | solution.py:124
  88.6 28.3 %all-to-all-start.2 = ((bf16[16,128,512]{2,1,0:T(8,128)(2,1)}), bf16[16,128,512]{2,1,0:T(8,128)(2,1)S(1)}, u32[]{:S(2)}, u32[]{:S(2)}) async-start(bf16[16,128,512]{2,1,0:T(8,128)(2,1)} %broadcast_in_dim.31), calls=%async_computation.2 | async-start | bytes 4194304 | tf_op jit(solution)/shard_map/all_to_all | solution.py:124
  116.9 11.5 %collective-permute-start.15 = (bf16[16,128,512]{2,1,0:T(8,128)(2,1)S(1)}, bf16[16,128,512]{2,1,0:T(8,128)(2,1)S(1)}, u32[]{:S(2)}, u32[]{:S(2)}) collective-permute-start(bf16[16,128,512]{2,1,0:T(8,128)(2,1)S(1)} %all-to-all-done.2.near_ref), channel_id=1, source_target_pairs={{0,128},{128,0},{1,129},{129,1},{2,130},{130,2},{3,131},{131,3},{4... | collective-permute-start | bytes 6291464 | tf_op jit(solution)/shard_map/ppermute | solution.py:120
  124.7 13.3 %collective-permute-start.19 = (bf16[4,448,128]{2,1,0:T(8,128)(2,1)}, bf16[4,448,128]{2,1,0:T(8,128)(2,1)S(1)}, u32[]{:S(2)}, u32[]{:S(2)}) collective-permute-start(bf16[4,448,128]{2,1,0:T(8,128)(2,1)} %get-tuple-element.83), channel_id=1, source_target_pairs={{0,40},{8,32},{16,56},{24,48},{32,8},{40,0},{48,24},{56,16},{64,10... | collective-permute-start | bytes 1376264 | tf_op jit(solution)/shard_map/ppermute | solution.py:108
  132.9 6.1 %collective-permute-start.18 = (bf16[192,128]{1,0:T(8,128)(2,1)S(1)}, bf16[192,128]{1,0:T(8,128)(2,1)S(1)}, u32[]{:S(2)}, u32[]{:S(2)}) collective-permute-start(bf16[192,128]{1,0:T(8,128)(2,1)S(1)} %get-tuple-element.79.refs_1_), channel_id=1, source_target_pairs={{0,40},{8,32},{16,56},{24,48},{32,8},{40,0},{48,24},{56,16},{64,10... | collective-permute-start | bytes 147464 | tf_op jit(solution)/shard_map/ppermute | solution.py:108
  133.0 7.3 %collective-permute-start.17 = (bf16[192,128]{1,0:T(8,128)(2,1)S(1)}, bf16[192,128]{1,0:T(8,128)(2,1)S(1)}, u32[]{:S(2)}, u32[]{:S(2)}) collective-permute-start(bf16[192,128]{1,0:T(8,128)(2,1)S(1)} %get-tuple-element.79.refs_1_), channel_id=1, source_target_pairs={{0,32},{8,40},{16,48},{24,56},{32,0},{40,8},{48,16},{56,24},{64,96... | collective-permute-start | bytes 147464 | tf_op jit(solution)/shard_map/ppermute | solution.py:108
  134.2 6.2 %collective-permute-start.16 = (bf16[192,128]{1,0:T(8,128)(2,1)S(1)}, bf16[192,128]{1,0:T(8,128)(2,1)S(1)}, u32[]{:S(2)}, u32[]{:S(2)}) collective-permute-start(bf16[192,128]{1,0:T(8,128)(2,1)S(1)} %get-tuple-element.79.refs_1_), channel_id=1, source_target_pairs={{0,8},{8,0},{16,24},{24,16},{32,40},{40,32},{48,56},{56,48},{64,72... | collective-permute-start | bytes 147464 | tf_op jit(solution)/shard_map/ppermute | solution.py:108
  145.2 6.3 %collective-permute-start.21 = (bf16[128,448]{1,0:T(8,128)(2,1)S(1)}, bf16[128,448]{1,0:T(8,128)(2,1)S(1)}, u32[]{:S(2)}, u32[]{:S(2)}) collective-permute-start(bf16[128,448]{1,0:T(8,128)(2,1)S(1)} %get-tuple-element.88), channel_id=1, source_target_pairs={{0,16},{8,24},{16,0},{24,8},{32,48},{40,56},{48,32},{56,40},{64,80... | collective-permute-start | bytes 344072 | tf_op jit(solution)/shard_map/ppermute | solution.py:108
  145.4 9.7 %collective-permute-start.23 = (bf16[128,448]{1,0:T(8,128)(2,1)S(1)}, bf16[128,448]{1,0:T(8,128)(2,1)S(1)}, u32[]{:S(2)}, u32[]{:S(2)}) collective-permute-start(bf16[128,448]{1,0:T(8,128)(2,1)S(1)} %get-tuple-element.89), channel_id=1, source_target_pairs={{0,80},{8,88},{16,64},{24,72},{32,112},{40,120},{48,96},{56,104},{... | collective-permute-start | bytes 344072 | tf_op jit(solution)/shard_map/ppermute | solution.py:108
  149.0 8.9 %collective-permute-start.22 = (bf16[128,448]{1,0:T(8,128)(2,1)S(1)}, bf16[128,448]{1,0:T(8,128)(2,1)S(1)}, u32[]{:S(2)}, u32[]{:S(2)}) collective-permute-start(bf16[128,448]{1,0:T(8,128)(2,1)S(1)} %get-tuple-element.90), channel_id=1, source_target_pairs={{0,64},{8,72},{16,80},{24,88},{32,96},{40,104},{48,112},{56,120},{... | collective-permute-start | bytes 344072 | tf_op jit(solution)/shard_map/ppermute | solution.py:108
  (20 other events, 190.2 us)
Sparse Core Ops, SparseCore 0:
  10.7 71.4 all-gather.2

commit v4 on v3

--- a/solution.py
+++ b/solution.py
@@ -65,6 +65,10 @@
     return pltpu.with_memory_space_constraint(array, pltpu.HBM)
 
 
+def in_vmem(array):
+    return pltpu.with_memory_space_constraint(array, pltpu.VMEM)
+
+
 def nn(a, b):
     return jnp.dot(a, b, preferred_element_type=f32)
 
@@ -138,19 +142,25 @@
     return jnp.concatenate(heads, axis=0).astype(bf16), jnp.concatenate([wanted] * 8, axis=0)
 
 
-def resident_kernel(lens, q_ref, cache_hbm, k0, k1, k2, k3, state_ref, stack, cache_ref, held, sem, ins, out_sem):
+def stack_kernel(k0, k1, k2, k3, out_ref):
+    for d, k in enumerate((k0, k1, k2, k3)):
+        out_ref[d] = k[...]
+
+
+def stack_of(pieces):
+    return pl.pallas_call(
+        stack_kernel,
+        out_shape=jax.ShapeDtypeStruct((SIDE,) + pieces[0].shape, bf16),
+        in_specs=[VMEM] * SIDE,
+        out_specs=VMEM,
+        compiler_params=pltpu.CompilerParams(vmem_limit_bytes=4 << 20),
+    )(*pieces)
+
+
+def resident_kernel(lens, q_ref, cache_hbm, state_ref, cache_ref, sem):
     cache_copy = pltpu.make_async_copy(cache_hbm, cache_ref, sem)
     cache_copy.start()
-    copies = [
-        pltpu.make_async_copy(k, held.at[d], ins.at[d]) for d, k in enumerate((k0, k1, k2, k3))
-    ]
-    for copy in copies:
-        copy.start()
     queries, _ = head_rows(q_ref)
-    for copy in copies:
-        copy.wait()
-    out = pltpu.make_async_copy(held, stack, out_sem)
-    out.start()
     cache_copy.wait()
     count = cache_ref.shape[0]
     row = lax.rem(lax.broadcasted_iota(jnp.int32, (queries.shape[0], 128), 0), count)
@@ -172,29 +182,17 @@
     state_ref[:, :LATENT] = weighted
     state_ref[:, LATENT : LATENT + 128] = jnp.broadcast_to(m, total.shape)
     state_ref[:, LATENT + 128 :] = jnp.broadcast_to(jnp.sum(total, axis=1, keepdims=True), total.shape)
-    out.wait()
-
-
-def resident_attention(cache_len, packet, dec_cache, pieces):
-    hbm = pl.BlockSpec(memory_space=pltpu.HBM)
-    stack = (SIDE,) + pieces[0].shape
+
+
+def resident_attention(cache_len, packet, dec_cache):
     return pl.pallas_call(
         resident_kernel,
-        out_shape=[
-            jax.ShapeDtypeStruct((64, LATENT + 256), f32),
-            jax.ShapeDtypeStruct(stack, bf16),
-        ],
-        in_specs=[SMEM, VMEM] + [hbm] * 5,
-        out_specs=[VMEM, hbm],
-        scratch_shapes=[
-            pltpu.VMEM(dec_cache.shape, bf16),
-            pltpu.VMEM(stack, bf16),
-            pltpu.SemaphoreType.DMA,
-            pltpu.SemaphoreType.DMA((SIDE,)),
-            pltpu.SemaphoreType.DMA,
-        ],
+        out_shape=pltpu.VMEM((64, LATENT + 256), f32),
+        in_specs=[SMEM, VMEM, pl.BlockSpec(memory_space=pltpu.HBM)],
+        out_specs=VMEM,
+        scratch_shapes=[pltpu.VMEM(dec_cache.shape, bf16), pltpu.SemaphoreType.DMA],
         compiler_params=pltpu.CompilerParams(vmem_limit_bytes=8 << 20),
-    )(cache_len, packet, in_hbm(dec_cache), *[in_hbm(piece) for piece in pieces])
+    )(cache_len, packet, in_hbm(dec_cache))
 
 
 def span_kernel(
@@ -279,34 +277,39 @@
     hidden_ref[...] = rounded
     hidden = rounded.astype(f32)
     features = hidden.shape[1]
-    packed_ref[:, :features] = (hidden * gain_ref[...]).astype(bf16)
+    gained = (hidden * gain_ref[...]).astype(bf16)
     extra = extra_ref[...]
     lane = lax.broadcasted_iota(jnp.int32, extra.shape, 1)
     for part, v in enumerate(split3(jnp.sum(hidden * hidden, axis=1, keepdims=True))):
         extra = jnp.where(lane == 32 + part, v, extra)
-    packed_ref[:, features:] = extra.astype(bf16)
-
-
-def expert_kernel(info, near_ref, far_ref, w_hbm, act_ref, place_ref, gate_ref, w_ref, sems):
-    copies = [
-        pltpu.make_async_copy(
-            w_hbm.at[:, pl.ds(i * SIDE, SIDE)], w_ref.at[:, pl.ds(i * SIDE, SIDE)], sems.at[i]
-        )
-        for i in range(SIDE)
-    ]
-    for copy in copies:
-        copy.start()
-    shards, half, _ = near_ref.shape
-    features, block = w_ref.shape[2], 16
-    rows, slots = 2 * half, act_ref.shape[0]
+    extra = extra.astype(bf16)
+    for i in range(packed_ref.shape[0]):
+        packed_ref[i, :, :features] = gained
+        packed_ref[i, :, features:] = extra
+
+
+def products(x_ref, w_ref):
+    shards, rows, _ = x_ref.shape
+    features = w_ref.shape[2]
     both = jnp.zeros((rows, 256), f32)
     tails = jnp.zeros((rows, 64), f32)
     for s in range(shards):
-        if s % SIDE == 0:
-            copies[s // SIDE].wait()
-        x = jnp.concatenate([near_ref[s], far_ref[s]], axis=0)
+        x = x_ref[s]
         both += nn(x[:, :features], jnp.concatenate([w_ref[0, s], w_ref[1, s]], axis=1))
         tails += x[:, features:].astype(f32)
+    return both, tails
+
+
+def near_kernel(info, near_ref, w_ref, both_ref, tails_ref):
+    both_ref[...], tails_ref[...] = products(near_ref, w_ref)
+
+
+def expert_kernel(info, near_ref, far_ref, w_ref, both_ref, tails_ref, act_ref, place_ref, gate_ref):
+    shards, features, block = w_ref.shape[1], w_ref.shape[2], 16
+    both, tails = products(far_ref, w_ref)
+    both = jnp.concatenate([both_ref[...], both], axis=0)
+    tails = jnp.concatenate([tails_ref[...], tails], axis=0)
+    rows, slots = both.shape[0], act_ref.shape[0]
     squares = tails[:, 32:33] + tails[:, 33:34] + tails[:, 34:35]
     factor = lax.rsqrt(squares * (1.0 / (shards * features)) + epsilon)
     gate = both[:, :128] * factor
@@ -329,26 +332,27 @@
 
 
 def experts(info, near, far, w_in):
-    slots = 16 * CAP
-    return pl.pallas_call(
+    slots, rows = 16 * CAP, near.shape[1]
+    both, tails = call(
+        near_kernel,
+        [jax.ShapeDtypeStruct((rows, 256), f32), jax.ShapeDtypeStruct((rows, 64), f32)],
+        [info, near, w_in],
+        mib=16,
+    )
+    return call(
         expert_kernel,
-        out_shape=[
+        [
             jax.ShapeDtypeStruct((slots, 128), bf16),
-            jax.ShapeDtypeStruct((256, slots), bf16),
-            jax.ShapeDtypeStruct((256, 1), f32),
+            jax.ShapeDtypeStruct((2 * rows, slots), bf16),
+            jax.ShapeDtypeStruct((2 * rows, 1), f32),
         ],
-        in_specs=[SMEM, VMEM, VMEM, pl.BlockSpec(memory_space=pltpu.HBM)],
-        out_specs=[VMEM, VMEM, VMEM],
-        scratch_shapes=[pltpu.VMEM(w_in.shape, bf16), pltpu.SemaphoreType.DMA((SIDE,))],
-        compiler_params=pltpu.CompilerParams(vmem_limit_bytes=16 << 20),
-    )(info, near, far, in_hbm(w_in))
-
-
-def cut_down_kernel(info, w_hbm, o0, o1, o2, o3, w_ref, held, w_sem, sems):
+        [info, near, far, w_in, both, tails],
+        mib=16,
+    )
+
+
+def cut_down_kernel(info, w_ref, o0, o1, o2, o3, held, sems):
     features = o0.shape[1]
-    whole = pltpu.make_async_copy(w_hbm, w_ref, w_sem)
-    whole.start()
-    whole.wait()
     for place in range(SIDE):
         step = jnp.bitwise_xor(info[6], place)
         for square in range(SIDE):
@@ -369,42 +373,53 @@
     return pl.pallas_call(
         cut_down_kernel,
         out_shape=[pltpu.HBM(shape, bf16)] * SIDE,
-        in_specs=[SMEM, anywhere],
+        in_specs=[SMEM, VMEM],
         out_specs=[anywhere] * SIDE,
         scratch_shapes=[
-            pltpu.VMEM(w_down.shape, bf16),
             pltpu.VMEM((SIDE,) + shape, bf16),
-            pltpu.SemaphoreType.DMA,
             pltpu.SemaphoreType.DMA((SIDE,)),
         ],
         compiler_params=pltpu.CompilerParams(vmem_limit_bytes=8 << 20),
-    )(info, in_hbm(w_down))
+    )(info, w_down)
 
 
 def down_kernel(info, a0, a1, a2, a3, w0, w1, w2, w3, place_ref, gate_ref, near_ref, far_ref):
     place, gates = place_ref[...], gate_ref[...]
     half = near_ref.shape[1]
-    for d in range(SIDE):
-        to = jnp.bitwise_xor(info[7], d)
-        total = sum(nt(a[...], w[to]) for a, w in ((a0, w0), (a1, w1), (a2, w2), (a3, w3)))
+    for square in range(SIDE):
+        total = sum(nt(a[...], w[square]) for a, w in ((a0, w0), (a1, w1), (a2, w2), (a3, w3)))
         high = total.astype(bf16)
         low = (total - high.astype(f32)).astype(bf16)
         share = (nn(place, high) + nn(place, low)) * gates
-        near_ref[d] = share[:half]
-        far_ref[d] = share[half:].astype(bf16)
-
-
-def prompt_kernel(info, q_ref, keys_ref, out_ref, scores, weighted):
+        near_ref[square] = share[:half]
+        far_ref[square] = share[half:].astype(bf16)
+
+
+def prompt_kernel(info, q_ref, keys_hbm, out_ref, keys_ref, scores, weighted, sems):
     pieces, tokens = keys_ref.shape[0], q_ref.shape[0]
+    step, unroll = pl.program_id(0), 8
+
+    def fetch(i):
+        part = pl.ds(i * unroll, unroll)
+        return pltpu.make_async_copy(keys_hbm.at[part], keys_ref.at[part], sems.at[i])
+
+    @pl.when(step == 0)
+    def _():
+        for i in range(pieces // unroll):
+            fetch(i).start()
+
     heads = q_ref.shape[1] // 576
     me, prefix_len = info[4], info[5]
     queries = jnp.concatenate([q_ref[:, h * 576 : (h + 1) * 576] for h in range(heads)], axis=0)
     rows = queries.shape[0]
     lane = lax.broadcasted_iota(jnp.int32, (tokens, 128), 1)
     ahead = lane - lax.broadcasted_iota(jnp.int32, (tokens, 128), 0)
-    unroll = 8
 
     def score(i, top):
+        @pl.when(step == 0)
+        def _():
+            fetch(i).wait()
+
         for u in range(unroll):
             j = i * unroll + u
             early = jnp.where(lane < prefix_len - j * 128, 0.0, LOW)
@@ -435,30 +450,28 @@
     for h in range(heads):
         out_ref[:, h * LATENT : (h + 1) * LATENT] = result[h * tokens : (h + 1) * tokens]
 
-
 def prompt_attention(info, queries, keys, heads=4):
     tokens, width = queries.shape
     steps = width // (576 * heads)
     pieces = keys.shape[0]
+    hbm = pl.BlockSpec(memory_space=pltpu.HBM)
     return pl.pallas_call(
         prompt_kernel,
         out_shape=jax.ShapeDtypeStruct((tokens, steps * heads * LATENT), bf16),
         grid=(steps,),
-        in_specs=[
-            SMEM,
-            pl.BlockSpec((tokens, heads * 576), lambda i: (0, i)),
-            pl.BlockSpec(keys.shape, lambda i: (0, 0, 0)),
-        ],
+        in_specs=[SMEM, pl.BlockSpec((tokens, heads * 576), lambda i: (0, i)), hbm],
         out_specs=pl.BlockSpec((tokens, heads * LATENT), lambda i: (0, i)),
         scratch_shapes=[
+            pltpu.VMEM(keys.shape, bf16),
             pltpu.VMEM((pieces, heads * tokens, 256), f32),
             pltpu.VMEM((heads * tokens, LATENT), f32),
+            pltpu.SemaphoreType.DMA((pieces // 8,)),
         ],
         compiler_params=pltpu.CompilerParams(vmem_limit_bytes=32 << 20),
         cost_estimate=pl.CostEstimate(
             flops=2 * 8 * tokens * 4096 * 1088, bytes_accessed=8 << 20, transcendentals=8 * tokens * 4096
         ),
-    )(info, queries, keys)
+    )(info, in_hbm(queries), in_hbm(keys))
 
 
 def on_device(
@@ -512,7 +525,7 @@
     keys = lax.all_gather(jnp.concatenate([prefix, columns], axis=1), "seq", axis=0)
     pieces, packets = along_x(span), along_y(packet)
     pieces, packets = lax.optimization_barrier((pieces, packets))
-    resident, stacked = resident_attention(cache_len, packets[0], dec_cache, pieces)
+    resident = resident_attention(cache_len, packets[0], dec_cache)
     g_high = lax.reduce_precision(expert_gates, 8, 7)
     g_mid = lax.reduce_precision(expert_gates - g_high, 8, 7)
     g_low = lax.reduce_precision(expert_gates - g_high - g_mid, 8, 7)
@@ -523,7 +536,7 @@
     part = call(
         span_kernel,
         jax.ShapeDtypeStruct((32, 9 * VDIM), bf16),
-        [info, *packets, *pieces, other_core(stacked), w_uv, resident],
+        [info, *packets, *pieces, other_core(stack_of(pieces)), w_uv, in_vmem(resident)],
         [pltpu.VMEM((SIDE, 8, 9 * VDIM), f32)],
         fetch=tuple(range(1, 11)),
         mib=16,
@@ -551,14 +564,14 @@
         hidden_kernel,
         [
             jax.ShapeDtypeStruct((16, features), bf16),
-            jax.ShapeDtypeStruct((16, features + 64), bf16),
+            jax.ShapeDtypeStruct((depth, 16, features + 64), bf16),
         ],
         [info, terms, x_dec, gain, extra],
     )
-    rows = everyone(packed, "expert", depth).reshape(16 * depth, features + 64)
+    rows = lax.all_to_all(packed, "expert", 0, 0, tiled=True).reshape(16 * depth, features + 64)
     rows, q_pre, w_back = lax.optimization_barrier((rows, q_pre, w_back))
     arrived = everyone(rows, "seq", shards)
-    o_pre = prompt_attention(info, q_pre[0], keys)[None]
+    o_pre = prompt_attention(info, q_pre[0], keys)
     arrived, o_pre, diagonal = lax.optimization_barrier((arrived, o_pre, diagonal))
     w_back.append(swap(diagonal, NEIGHBOURS[3]))
     act, place, gate = experts(
@@ -572,12 +585,13 @@
         mib=16,
     )
     share = (near + other_core(far_share).astype(f32)).astype(bf16)
-    parts = [share[0]] + [swap(share[d], SQUARES[d]) for d in range(1, SIDE)]
-    share = sum(v.astype(f32) for v in parts).astype(bf16)
+    same_place = [[place + square for square in SQUARES] for place in NEIGHBOURS]
+    parts = lax.all_to_all(share, "seq", 0, 0, tiled=True, axis_index_groups=same_place)
+    share = jnp.sum(parts.astype(f32), axis=0).astype(bf16)
     shares = lax.all_to_all(share.reshape(depth, 16, features), "expert", 0, 0, tiled=True)
     h_out = (hidden.astype(f32) + jnp.sum(shares.astype(f32), axis=0)).astype(bf16)
 
-    return (o_pre, h_out)
+    return (o_pre[None], h_out)
 
 
 def solution(mesh):

time: 176 us -> 173 us (0.983)
  blocking collectives: 10.1 us -> 23.4 us
  starting transfers between devices: 48.8 us -> 40.1 us
  waiting for transfers between devices: 51.6 us -> 46 us
  local copies, waits for them, and re-layouts: 10.1 us -> 7.78 us
    all_to_all x0 -> x1, blocking collectives: none -> 13 us  [on_device(): lax.all_to_all(share, 'seq', 0, 0, tiled=True, axis_index_groups=same_place)]
    all_to_all x0 -> x1, waiting for transfers between devices: none -> 7.91 us  [on_device(): lax.all_to_all(packed, 'expert', 0, 0, tiled=True)]
    all_to_all x2 -> x1, waiting for transfers between devices: 13.4 us -> 7.02 us  [everyone(): lax.all_to_all(jnp.broadcast_to(array[None], (count,) + array.shape), axi...]
    ppermute x9 -> x6, starting transfers between devices: 10.1 us -> 4.27 us  [swap(): lax.ppermute(array, 'seq', [(i, i ^ mask) for i in range(SIDE * SIDE)])]
    pallas_call x2, Pallas kernels: 7.5 us -> 2.78 us  [the longest x1 2.74 us: resident_attention(): pl.pallas_call(resident_kernel, out_shape=pltpu.VMEM((64, LATENT + 256),...]
    ppermute x3, waiting for transfers between devices: 6.2 us -> 1.95 us  [other_core(): return lax.ppermute(array, 'group', [(0, 1), (1, 0)])]
    ppermute x9 -> x6, waiting for transfers between devices: 11.6 us -> 7.42 us  [swap(): lax.ppermute(array, 'seq', [(i, i ^ mask) for i in range(SIDE * SIDE)])]
    all_to_all x2 -> x1, starting transfers between devices: 7.61 us -> 3.72 us  [everyone(): lax.all_to_all(jnp.broadcast_to(array[None], (count,) + array.shape), axi...]
  transfers between devices with their start and end apart: 28 -> 25, of which waited for: 18 -> 15; matrix products, arithmetic and copies ran while one was open for 2% -> 2% of each run, Pallas kernels for 19% -> 20%
where the time goes in v4:
time: 173 us; the launch traced here: 172 us
  waiting for transfers between devices  46 us (27%)
  starting transfers between devices  40.1 us (23%)
  Pallas kernels  36.7 us (21%)
  blocking collectives  23.4 us (14%)
  between operations  15 us (9%)
  local copies, waits for them, and re-layouts  7.78 us (4%)
  other arithmetic  3.36 us (2%)
    pallas_call x1, Pallas kernels, prompt_attention(): pl.pallas_call(prompt_kernel, out_shape=jax.ShapeDtypeStruct((tokens, ste...  17.4 us
    pallas_call x7, Pallas kernels, call(): pl.pallas_call(body, out_shape=out_shape, in_specs=place, out_specs=[VMEM...  13.4 us
    all_to_all x1, blocking collectives, on_device(): lax.all_to_all(share, 'seq', 0, 0, tiled=True, axis_index_groups=same_place)  13 us
    all_to_all x1, blocking collectives, on_device(): lax.all_to_all(share.reshape(depth, 16, features), 'expert', 0, 0, tiled=...  10.4 us
    ppermute x3, starting transfers between devices, other_core(): return lax.ppermute(array, 'group', [(0, 1), (1, 0)])  8.78 us
    all_to_all x1, starting transfers between devices, on_device(): lax.all_to_all(product.reshape(depth, 16, features), 'expert', 0, 0, tile...  8.13 us
    ppermute x6, waiting for transfers between devices, to_y(): lax.ppermute(array, 'seq', [(y * SIDE + x, (y + d) % SIDE * SIDE + x) for...  8.07 us
    all_to_all x1, waiting for transfers between devices, on_device(): lax.all_to_all(product.reshape(depth, 16, features), 'expert', 0, 0, tile...  7.94 us
  transfers between devices with their start and end apart: 25, of which 15 were waited for; matrix products, arithmetic and copies ran while one was open for 2% of the time, Pallas kernels for 20%

profile of v4, /device:TPU:1, one launch (start us, length us, event | category | flops | bytes accessed | tf_op | source)
XLA Modules:
  0.0 172.3 jit_solution(8226221305908592253)
XLA Ops:
  8.8 1.8 %pad_maximum_fusion = bf16[576,256]{1,0:T(8,128)(2,1)} fusion(bf16[576,128]{1,0:T(8,128)(2,1)} %bitcast.22, bf16[576,128]{1,0:T(8,128)(2,1)} %bitcast.32), kind=kLoop, calls=%fused_computation.1 | loop fusion | flops 589824 | bytes 589824 | tf_op jit(solution)/shard_map/concatenate | solution.py:525
  10.6 3.6 %collective-permute-start.5 = (bf16[16,2432]{1,0:T(8,128)(2,1)S(1)}, bf16[16,2432]{1,0:T(8,128)(2,1)S(1)}, u32[]{:S(2)}, u32[]{:S(2)}) collective-permute-start(bf16[16,2432]{1,0:T(8,128)(2,1)S(1)} %maximum_maximum_fusion.q_ref.refs_1_), channel_id=1, source_target_pairs={{0,96},{8,104},{16,112},{24,120},{32,0},{40,8},{48,16},{56,24},{64... | collective-permute-start | bytes 233480 | tf_op jit(solution)/shard_map/ppermute | solution.py:100
  14.2 2.5 %collective-permute-start.2 = (bf16[576,128]{1,0:T(8,128)(2,1)}, bf16[576,128]{1,0:T(8,128)(2,1)S(1)}, u32[]{:S(2)}, u32[]{:S(2)}) collective-permute-start(bf16[576,128]{1,0:T(8,128)(2,1)} %bitcast.23), channel_id=1, source_target_pairs={{0,24},{8,0},{16,8},{24,16},{32,56},{40,32},{48,40},{56,48},{64,88... | collective-permute-start | bytes 442376 | tf_op jit(solution)/shard_map/ppermute | solution.py:92
  18.9 3.8 %collective-permute-done.4.refs_3_ = bf16[16,2432]{1,0:T(8,128)(2,1)S(1)} collective-permute-done((bf16[16,2432]{1,0:T(8,128)(2,1)S(1)}, bf16[16,2432]{1,0:T(8,128)(2,1)S(1)}, u32[]{:S(2)}, u32[]{:S(2)}) %collective-permute-start.4) | collective-permute-done | bytes 77856 | tf_op jit(solution)/shard_map/ppermute | solution.py:100
  23.7 3.2 %collective-permute-done.k1.refs_6_ = bf16[576,128]{1,0:T(8,128)(2,1)S(1)} collective-permute-done((bf16[576,128]{1,0:T(8,128)(2,1)}, bf16[576,128]{1,0:T(8,128)(2,1)S(1)}, u32[]{:S(2)}, u32[]{:S(2)}) %collective-permute-start) | collective-permute-done | bytes 147488 | tf_op jit(solution)/shard_map/ppermute | solution.py:92
  29.6 2.7 %shard_map.168.refs_11_ = f32[64,768]{1,0:T(8,128)S(1)} custom-call(s32[8]{0:T(128)S(1)} %copy-done.10, bf16[16,2432]{1,0:T(8,128)(2,1)S(1)} %maximum_maximum_fusion.q_ref.refs_1_, bf16[8,576,128]{2,1,0:T(8,128)(2,1)} %cache_hbm.1), custom_call_target="tpu_custom_call" | custom-call | tf_op jit(solution)/shard_map/pallas_call | solution.py:188
  33.3 3.9 %shard_map.169.refs_1_ = bf16[32,1152]{1,0:T(8,128)(2,1)S(1)} custom-call(s32[8]{0:T(128)S(1)} %stack.31.refs_0_.info, bf16[16,2432]{1,0:T(8,128)(2,1)} %copy-done.4, bf16[16,2432]{1,0:T(8,128)(2,1)} %copy-done.14, bf16[16,2432]{1,0:T(8,128)(2,1)} %copy-done.13, bf16[16,2432]{1,0:T(8,128)(2,1)} %copy-done.12, bf16[576,128]{1,0:T(8,128)(2,1)} %bitcast.26, ...), custom_call_target="tpu_custom_call" | custom-call | tf_op jit(solution)/shard_map/pallas_call | solution.py:54
  38.8 3.1 %shard_map.170 = (bf16[4,448,128]{2,1,0:T(8,128)(2,1)}, bf16[4,448,128]{2,1,0:T(8,128)(2,1)}, bf16[4,448,128]{2,1,0:T(8,128)(2,1)}, bf16[4,448,128]{2,1,0:T(8,128)(2,1)}) custom-call(s32[8]{0:T(128)S(1)} %stack.31.refs_0_.info, bf16[128,7168]{1,0:T(8,128)(2,1)S(1)} %bitcast.21), custom_call_target="tpu_custom_call" | custom-call | tf_op jit(solution)/shard_map/pallas_call | solution.py:373
  42.6 2.5 %collective-permute-done.7.refs_2_ = bf16[32,1152]{1,0:T(8,128)(2,1)S(1)} collective-permute-done((bf16[32,1152]{1,0:T(8,128)(2,1)S(1)}, bf16[32,1152]{1,0:T(8,128)(2,1)S(1)}, u32[]{:S(2)}, u32[]{:S(2)}) %collective-permute-start.7) | collective-permute-done | bytes 73760 | tf_op jit(solution)/shard_map/ppermute | solution.py:100
  54.6 8.1 %all-to-all-start = ((bf16[8,16,448]{2,1,0:T(8,128)(2,1)}), bf16[8,16,448]{2,1,0:T(8,128)(2,1)S(1)}, u32[]{:S(2)}, u32[]{:S(2)}) async-start(bf16[8,16,448]{2,1,0:T(8,128)(2,1)} %bitcast.11), calls=%async_computation | async-start | bytes 262144 | tf_op jit(solution)/shard_map/all_to_all | solution.py:561
  62.8 7.9 %all-to-all-done.refs_1_ = bf16[8,16,448]{2,1,0:T(8,128)(2,1)S(1)} async-done(((bf16[8,16,448]{2,1,0:T(8,128)(2,1)}), bf16[8,16,448]{2,1,0:T(8,128)(2,1)S(1)}, u32[]{:S(2)}, u32[]{:S(2)}) %all-to-all-start) | async-done | bytes 114720 | tf_op jit(solution)/shard_map/all_to_all | solution.py:561
  72.1 3.4 %all-to-all-start.1 = ((bf16[8,16,512]{2,1,0:T(8,128)(2,1)}), bf16[8,16,512]{2,1,0:T(8,128)(2,1)S(1)}, u32[]{:S(2)}, u32[]{:S(2)}) async-start(bf16[8,16,512]{2,1,0:T(8,128)(2,1)} %get-tuple-element.65), calls=%async_computation.1 | async-start | bytes 262144 | tf_op jit(solution)/shard_map/all_to_all | solution.py:571
  75.5 7.9 %all-to-all-done.1 = bf16[8,16,512]{2,1,0:T(8,128)(2,1)S(1)} async-done(((bf16[8,16,512]{2,1,0:T(8,128)(2,1)}), bf16[8,16,512]{2,1,0:T(8,128)(2,1)S(1)}, u32[]{:S(2)}, u32[]{:S(2)}) %all-to-all-start.1) | async-done | bytes 131104 | tf_op jit(solution)/shard_map/all_to_all | solution.py:571
  85.0 3.7 %all-to-all-start.2 = ((bf16[16,128,512]{2,1,0:T(8,128)(2,1)}), bf16[16,128,512]{2,1,0:T(8,128)(2,1)S(1)}, u32[]{:S(2)}, u32[]{:S(2)}) async-start(bf16[16,128,512]{2,1,0:T(8,128)(2,1)} %broadcast_in_dim.24), calls=%async_computation.2 | async-start | bytes 4194304 | tf_op jit(solution)/shard_map/all_to_all | solution.py:128
  88.7 17.4 %shard_map.174 = bf16[128,4096]{1,0:T(8,128)(2,1)} custom-call(s32[8]{0:T(128)S(1)} %stack.31.refs_0_.info, bf16[128,4608]{1,0:T(8,128)(2,1)} %bitcast.34, bf16[16,576,256]{2,1,0:T(8,128)(2,1)} %bitcast.33), custom_call_target="tpu_custom_call" | custom-call | flops 9126805504 | bytes 8388608 | tf_op jit(solution)/shard_map/pallas_call | solution.py:458
  106.2 7.0 %all-to-all-done.2.refs_1_ = bf16[16,128,512]{2,1,0:T(8,128)(2,1)S(1)} async-done(((bf16[16,128,512]{2,1,0:T(8,128)(2,1)}), bf16[16,128,512]{2,1,0:T(8,128)(2,1)S(1)}, u32[]{:S(2)}, u32[]{:S(2)}) %all-to-all-start.2) | async-done | bytes 2097184 | tf_op jit(solution)/shard_map/all_to_all | solution.py:128
  113.2 7.3 %collective-permute-start.15 = (bf16[16,128,512]{2,1,0:T(8,128)(2,1)S(1)}, bf16[16,128,512]{2,1,0:T(8,128)(2,1)S(1)}, u32[]{:S(2)}, u32[]{:S(2)}) collective-permute-start(bf16[16,128,512]{2,1,0:T(8,128)(2,1)S(1)} %all-to-all-done.2.refs_1_), channel_id=1, source_target_pairs={{0,128},{128,0},{1,129},{129,1},{2,130},{130,2},{3,131},{131,3},{4... | collective-permute-start | bytes 6291464 | tf_op jit(solution)/shard_map/ppermute | solution.py:124
  120.4 2.0 %copy-done = bf16[1,2,7168,128]{3,2,1,0:T(8,128)(2,1)S(1)} copy-done((bf16[1,2,7168,128]{3,2,1,0:T(8,128)(2,1)S(1)}, bf16[1,2,7168,128]{3,2,1,0:T(8,128)(2,1)}, u32[]{:S(2)}) %copy-start) | copy-done | bytes 3670040
  124.2 1.7 shard_map.176
  125.9 2.1 %collective-permute-start.18 = (bf16[192,128]{1,0:T(8,128)(2,1)S(1)}, bf16[192,128]{1,0:T(8,128)(2,1)S(1)}, u32[]{:S(2)}, u32[]{:S(2)}) collective-permute-start(bf16[192,128]{1,0:T(8,128)(2,1)S(1)} %get-tuple-element.79.refs_1_), channel_id=1, source_target_pairs={{0,40},{8,32},{16,56},{24,48},{32,8},{40,0},{48,24},{56,16},{64,10... | collective-permute-start | bytes 147464 | tf_op jit(solution)/shard_map/ppermute | solution.py:112
  128.7 5.1 %collective-permute-done.19.refs_8_ = bf16[4,448,128]{2,1,0:T(8,128)(2,1)S(1)} collective-permute-done((bf16[4,448,128]{2,1,0:T(8,128)(2,1)}, bf16[4,448,128]{2,1,0:T(8,128)(2,1)S(1)}, u32[]{:S(2)}, u32[]{:S(2)}) %collective-permute-start.19) | collective-permute-done | bytes 458784 | tf_op jit(solution)/shard_map/ppermute | solution.py:112
  136.1 2.6 %shard_map.177 = (f32[4,128,448]{2,1,0:T(8,128)S(1)}, bf16[4,128,448]{2,1,0:T(8,128)(2,1)S(1)}) custom-call(s32[8]{0:T(128)S(1)} %stack.31.refs_0_.info, bf16[192,128]{1,0:T(8,128)(2,1)S(1)} %get-tuple-element.79.refs_1_, bf16[192,128]{1,0:T(8,128)(2,1)S(1)} %collective-permute-done.16.refs_2_, bf16[192,128]{1,0:T(8,128)(2,1)S(1)} %collective-permute-done.17.refs_3_, ...), custom_call_target="tpu_custom_call" | custom-call | tf_op jit(solution)/shard_map/pallas_call | solution.py:54
  141.2 13.0 %all_to_all.25 = bf16[4,128,448]{1,2,0:T(8,128)(2,1)S(1)} all-to-all(bf16[4,128,448]{1,2,0:T(8,128)(2,1)S(1)} %copy.38), channel_id=1, replica_groups={{0,16,64,80},{8,24,72,88},{32,48,96,112},{40,56,104,120},{1,17,65,81},{..., dimensions={0} | all-to-all | bytes 917504 | tf_op jit(solution)/shard_map/all_to_all | solution.py:589
  154.4 10.4 %all_to_all.26 = bf16[8,16,448]{2,1,0:T(8,128)(2,1)S(1)} all-to-all(bf16[8,16,448]{2,1,0:T(8,128)(2,1)S(1)} %bitcast.31), channel_id=1, replica_groups=mesh['group'=2,'seq'=16,'expert'=8] {'expert'}, dimensions={0} | all-to-all | bytes 229376 | tf_op jit(solution)/shard_map/all_to_all | solution.py:591
  (96 shorter events, 30.5 us)
Async XLA Ops:
  7.2 81.6 %all-gather.3.cloned.1.call-start = ((), (), s32[]{:S(2)}) async-start(), calls=%async_computation.5 | async-start | bytes 5013504 | tf_op jit(solution)/shard_map/all_gather | solution.py:525
  10.6 7.6 %collective-permute-start.5 = (bf16[16,2432]{1,0:T(8,128)(2,1)S(1)}, bf16[16,2432]{1,0:T(8,128)(2,1)S(1)}, u32[]{:S(2)}, u32[]{:S(2)}) collective-permute-start(bf16[16,2432]{1,0:T(8,128)(2,1)S(1)} %maximum_maximum_fusion.q_ref.refs_1_), channel_id=1, source_target_pairs={{0,96},{8,104},{16,112},{24,120},{32,0},{40,8},{48,16},{56,24},{64... | collective-permute-start | bytes 233480 | tf_op jit(solution)/shard_map/ppermute | solution.py:100
  14.2 9.5 %collective-permute-start.2 = (bf16[576,128]{1,0:T(8,128)(2,1)}, bf16[576,128]{1,0:T(8,128)(2,1)S(1)}, u32[]{:S(2)}, u32[]{:S(2)}) collective-permute-start(bf16[576,128]{1,0:T(8,128)(2,1)} %bitcast.23), channel_id=1, source_target_pairs={{0,24},{8,0},{16,8},{24,16},{32,56},{40,32},{48,40},{56,48},{64,88... | collective-permute-start | bytes 442376 | tf_op jit(solution)/shard_map/ppermute | solution.py:92
  16.7 7.0 %collective-permute-start.1 = (bf16[576,128]{1,0:T(8,128)(2,1)}, bf16[576,128]{1,0:T(8,128)(2,1)S(1)}, u32[]{:S(2)}, u32[]{:S(2)}) collective-permute-start(bf16[576,128]{1,0:T(8,128)(2,1)} %bitcast.24), channel_id=1, source_target_pairs={{0,16},{8,24},{16,0},{24,8},{32,48},{40,56},{48,32},{56,40},{64,80... | collective-permute-start | bytes 442376 | tf_op jit(solution)/shard_map/ppermute | solution.py:92
  17.2 9.8 %collective-permute-start = (bf16[576,128]{1,0:T(8,128)(2,1)}, bf16[576,128]{1,0:T(8,128)(2,1)S(1)}, u32[]{:S(2)}, u32[]{:S(2)}) collective-permute-start(bf16[576,128]{1,0:T(8,128)(2,1)} %bitcast.25), channel_id=1, source_target_pairs={{0,8},{8,16},{16,24},{24,0},{32,40},{40,48},{48,56},{56,32},{64,72... | collective-permute-start | bytes 442376 | tf_op jit(solution)/shard_map/ppermute | solution.py:92
  17.8 4.8 %collective-permute-start.4 = (bf16[16,2432]{1,0:T(8,128)(2,1)S(1)}, bf16[16,2432]{1,0:T(8,128)(2,1)S(1)}, u32[]{:S(2)}, u32[]{:S(2)}) collective-permute-start(bf16[16,2432]{1,0:T(8,128)(2,1)S(1)} %maximum_maximum_fusion.q_ref.refs_1_), channel_id=1, source_target_pairs={{0,64},{8,72},{16,80},{24,88},{32,96},{40,104},{48,112},{56,120},{... | collective-permute-start | bytes 233480 | tf_op jit(solution)/shard_map/ppermute | solution.py:100
  18.2 5.5 %collective-permute-start.3 = (bf16[16,2432]{1,0:T(8,128)(2,1)S(1)}, bf16[16,2432]{1,0:T(8,128)(2,1)S(1)}, u32[]{:S(2)}, u32[]{:S(2)}) collective-permute-start(bf16[16,2432]{1,0:T(8,128)(2,1)S(1)} %maximum_maximum_fusion.q_ref.refs_1_), channel_id=1, source_target_pairs={{0,32},{8,40},{16,48},{24,56},{32,64},{40,72},{48,80},{56,88},{64,... | collective-permute-start | bytes 233480 | tf_op jit(solution)/shard_map/ppermute | solution.py:100
  27.9 4.5 %collective-permute-start.6 = (bf16[4,576,128]{2,1,0:T(8,128)(2,1)S(1)}, bf16[4,576,128]{2,1,0:T(8,128)(2,1)S(1)}, u32[]{:S(2)}, u32[]{:S(2)}) collective-permute-start(bf16[4,576,128]{2,1,0:T(8,128)(2,1)S(1)} %shard_map.167), channel_id=1, source_target_pairs={{0,128},{128,0},{1,129},{129,1},{2,130},{130,2},{3,131},{131,3},{4... | collective-permute-start | bytes 1769480 | tf_op jit(solution)/shard_map/ppermute | solution.py:124
  37.2 4.7 %collective-permute-start.9 = (bf16[32,1152]{1,0:T(8,128)(2,1)S(1)}, bf16[32,1152]{1,0:T(8,128)(2,1)S(1)}, u32[]{:S(2)}, u32[]{:S(2)}) collective-permute-start(bf16[32,1152]{1,0:T(8,128)(2,1)S(1)} %shard_map.169.refs_1_), channel_id=1, source_target_pairs={{0,96},{8,104},{16,112},{24,120},{32,0},{40,8},{48,16},{56,24},{64... | collective-permute-start | bytes 221192 | tf_op jit(solution)/shard_map/ppermute | solution.py:100
  37.9 4.8 %collective-permute-start.8 = (bf16[32,1152]{1,0:T(8,128)(2,1)S(1)}, bf16[32,1152]{1,0:T(8,128)(2,1)S(1)}, u32[]{:S(2)}, u32[]{:S(2)}) collective-permute-start(bf16[32,1152]{1,0:T(8,128)(2,1)S(1)} %shard_map.169.refs_1_), channel_id=1, source_target_pairs={{0,64},{8,72},{16,80},{24,88},{32,96},{40,104},{48,112},{56,120},{... | collective-permute-start | bytes 221192 | tf_op jit(solution)/shard_map/ppermute | solution.py:100
  38.0 7.2 %collective-permute-start.7 = (bf16[32,1152]{1,0:T(8,128)(2,1)S(1)}, bf16[32,1152]{1,0:T(8,128)(2,1)S(1)}, u32[]{:S(2)}, u32[]{:S(2)}) collective-permute-start(bf16[32,1152]{1,0:T(8,128)(2,1)S(1)} %shard_map.169.refs_1_), channel_id=1, source_target_pairs={{0,32},{8,40},{16,48},{24,56},{32,64},{40,72},{48,80},{56,88},{64,... | collective-permute-start | bytes 221192 | tf_op jit(solution)/shard_map/ppermute | solution.py:100
  46.0 4.5 %collective-permute-start.12 = (bf16[32,1024]{1,0:T(8,128)(2,1)S(1)}, bf16[32,1024]{1,0:T(8,128)(2,1)S(1)}, u32[]{:S(2)}, u32[]{:S(2)}) collective-permute-start(bf16[32,1024]{1,0:T(8,128)(2,1)S(1)} %shard_map.171.refs_1_), channel_id=1, source_target_pairs={{0,24},{8,0},{16,8},{24,16},{32,56},{40,32},{48,40},{56,48},{64,88... | collective-permute-start | bytes 196616 | tf_op jit(solution)/shard_map/ppermute | solution.py:92
  46.9 4.6 %collective-permute-start.11 = (bf16[32,1024]{1,0:T(8,128)(2,1)S(1)}, bf16[32,1024]{1,0:T(8,128)(2,1)S(1)}, u32[]{:S(2)}, u32[]{:S(2)}) collective-permute-start(bf16[32,1024]{1,0:T(8,128)(2,1)S(1)} %shard_map.171.refs_1_), channel_id=1, source_target_pairs={{0,16},{8,24},{16,0},{24,8},{32,48},{40,56},{48,32},{56,40},{64,80... | collective-permute-start | bytes 196616 | tf_op jit(solution)/shard_map/ppermute | solution.py:92
  48.0 5.0 %collective-permute-start.10 = (bf16[32,1024]{1,0:T(8,128)(2,1)S(1)}, bf16[32,1024]{1,0:T(8,128)(2,1)S(1)}, u32[]{:S(2)}, u32[]{:S(2)}) collective-permute-start(bf16[32,1024]{1,0:T(8,128)(2,1)S(1)} %shard_map.171.refs_1_), channel_id=1, source_target_pairs={{0,8},{8,16},{16,24},{24,0},{32,40},{40,48},{48,56},{56,32},{64,72... | collective-permute-start | bytes 196616 | tf_op jit(solution)/shard_map/ppermute | solution.py:92
  48.0 27.5 %collective-permute-start.13 = (bf16[4,448,128]{2,1,0:T(8,128)(2,1)}, bf16[4,448,128]{2,1,0:T(8,128)(2,1)S(1)}, u32[]{:S(2)}, u32[]{:S(2)}) collective-permute-start(bf16[4,448,128]{2,1,0:T(8,128)(2,1)} %get-tuple-element.67), channel_id=1, source_target_pairs={{0,8},{8,0},{16,24},{24,16},{32,40},{40,32},{48,56},{56,48},{64,72... | collective-permute-start | bytes 1376264 | tf_op jit(solution)/shard_map/ppermute | solution.py:112
  49.5 26.0 %collective-permute-start.14 = (bf16[4,448,128]{2,1,0:T(8,128)(2,1)}, bf16[4,448,128]{2,1,0:T(8,128)(2,1)S(1)}, u32[]{:S(2)}, u32[]{:S(2)}) collective-permute-start(bf16[4,448,128]{2,1,0:T(8,128)(2,1)} %get-tuple-element.68), channel_id=1, source_target_pairs={{0,32},{8,40},{16,48},{24,56},{32,0},{40,8},{48,16},{56,24},{64,96... | collective-permute-start | bytes 1376264 | tf_op jit(solution)/shard_map/ppermute | solution.py:112
  54.6 16.2 %all-to-all-start = ((bf16[8,16,448]{2,1,0:T(8,128)(2,1)}), bf16[8,16,448]{2,1,0:T(8,128)(2,1)S(1)}, u32[]{:S(2)}, u32[]{:S(2)}) async-start(bf16[8,16,448]{2,1,0:T(8,128)(2,1)} %bitcast.11), calls=%async_computation | async-start | bytes 262144 | tf_op jit(solution)/shard_map/all_to_all | solution.py:561
  72.1 11.3 %all-to-all-start.1 = ((bf16[8,16,512]{2,1,0:T(8,128)(2,1)}), bf16[8,16,512]{2,1,0:T(8,128)(2,1)S(1)}, u32[]{:S(2)}, u32[]{:S(2)}) async-start(bf16[8,16,512]{2,1,0:T(8,128)(2,1)} %get-tuple-element.65), calls=%async_computation.1 | async-start | bytes 262144 | tf_op jit(solution)/shard_map/all_to_all | solution.py:571
  85.0 28.2 %all-to-all-start.2 = ((bf16[16,128,512]{2,1,0:T(8,128)(2,1)}), bf16[16,128,512]{2,1,0:T(8,128)(2,1)S(1)}, u32[]{:S(2)}, u32[]{:S(2)}) async-start(bf16[16,128,512]{2,1,0:T(8,128)(2,1)} %broadcast_in_dim.24), calls=%async_computation.2 | async-start | bytes 4194304 | tf_op jit(solution)/shard_map/all_to_all | solution.py:128
  113.2 11.0 %collective-permute-start.15 = (bf16[16,128,512]{2,1,0:T(8,128)(2,1)S(1)}, bf16[16,128,512]{2,1,0:T(8,128)(2,1)S(1)}, u32[]{:S(2)}, u32[]{:S(2)}) collective-permute-start(bf16[16,128,512]{2,1,0:T(8,128)(2,1)S(1)} %all-to-all-done.2.refs_1_), channel_id=1, source_target_pairs={{0,128},{128,0},{1,129},{129,1},{2,130},{130,2},{3,131},{131,3},{4... | collective-permute-start | bytes 6291464 | tf_op jit(solution)/shard_map/ppermute | solution.py:124
  120.4 13.3 %collective-permute-start.19 = (bf16[4,448,128]{2,1,0:T(8,128)(2,1)}, bf16[4,448,128]{2,1,0:T(8,128)(2,1)S(1)}, u32[]{:S(2)}, u32[]{:S(2)}) collective-permute-start(bf16[4,448,128]{2,1,0:T(8,128)(2,1)} %get-tuple-element.83), channel_id=1, source_target_pairs={{0,40},{8,32},{16,56},{24,48},{32,8},{40,0},{48,24},{56,16},{64,10... | collective-permute-start | bytes 1376264 | tf_op jit(solution)/shard_map/ppermute | solution.py:112
  125.9 8.9 %collective-permute-start.18 = (bf16[192,128]{1,0:T(8,128)(2,1)S(1)}, bf16[192,128]{1,0:T(8,128)(2,1)S(1)}, u32[]{:S(2)}, u32[]{:S(2)}) collective-permute-start(bf16[192,128]{1,0:T(8,128)(2,1)S(1)} %get-tuple-element.79.refs_1_), channel_id=1, source_target_pairs={{0,40},{8,32},{16,56},{24,48},{32,8},{40,0},{48,24},{56,16},{64,10... | collective-permute-start | bytes 147464 | tf_op jit(solution)/shard_map/ppermute | solution.py:112
  128.0 8.1 %collective-permute-start.17 = (bf16[192,128]{1,0:T(8,128)(2,1)S(1)}, bf16[192,128]{1,0:T(8,128)(2,1)S(1)}, u32[]{:S(2)}, u32[]{:S(2)}) collective-permute-start(bf16[192,128]{1,0:T(8,128)(2,1)S(1)} %get-tuple-element.79.refs_1_), channel_id=1, source_target_pairs={{0,32},{8,40},{16,48},{24,56},{32,0},{40,8},{48,16},{56,24},{64,96... | collective-permute-start | bytes 147464 | tf_op jit(solution)/shard_map/ppermute | solution.py:112
  128.0 8.1 %collective-permute-start.16 = (bf16[192,128]{1,0:T(8,128)(2,1)S(1)}, bf16[192,128]{1,0:T(8,128)(2,1)S(1)}, u32[]{:S(2)}, u32[]{:S(2)}) collective-permute-start(bf16[192,128]{1,0:T(8,128)(2,1)S(1)} %get-tuple-element.79.refs_1_), channel_id=1, source_target_pairs={{0,8},{8,0},{16,24},{24,16},{32,40},{40,32},{48,56},{56,48},{64,72... | collective-permute-start | bytes 147464 | tf_op jit(solution)/shard_map/ppermute | solution.py:112
  (18 other events, 216.4 us)
Sparse Core Ops, SparseCore 0:
  10.7 70.9 all-gather.2

commit v5 on v4

--- a/solution.py
+++ b/solution.py
@@ -142,19 +142,23 @@
     return jnp.concatenate(heads, axis=0).astype(bf16), jnp.concatenate([wanted] * 8, axis=0)
 
 
-def stack_kernel(k0, k1, k2, k3, out_ref):
-    for d, k in enumerate((k0, k1, k2, k3)):
-        out_ref[d] = k[...]
+def stack_kernel(k0, k1, k2, k3, out_ref, sem):
+    own = pltpu.make_async_copy(k0, out_ref.at[0], sem)
+    own.start()
+    for d, k in enumerate((k1, k2, k3)):
+        out_ref[d + 1] = k[...]
+    own.wait()
 
 
 def stack_of(pieces):
     return pl.pallas_call(
         stack_kernel,
-        out_shape=jax.ShapeDtypeStruct((SIDE,) + pieces[0].shape, bf16),
-        in_specs=[VMEM] * SIDE,
+        out_shape=pltpu.VMEM((SIDE,) + pieces[0].shape, bf16),
+        in_specs=[pl.BlockSpec(memory_space=pltpu.HBM)] + [VMEM] * 3,
         out_specs=VMEM,
+        scratch_shapes=[pltpu.SemaphoreType.DMA],
         compiler_params=pltpu.CompilerParams(vmem_limit_bytes=4 << 20),
-    )(*pieces)
+    )(in_hbm(pieces[0]), *[in_vmem(piece) for piece in pieces[1:]])
 
 
 def resident_kernel(lens, q_ref, cache_hbm, state_ref, cache_ref, sem):
@@ -196,14 +200,14 @@
 
 
 def span_kernel(
-    info, q0, q1, q2, q3, k0, k1, k2, k3, kp, w_uv, state, out_ref, scr
+    info, q0, q1, q2, q3, ko, kp, w_uv, state, out_ref, scr
 ):
     group = info[0].astype(f32)
     y = info[1]
     parts = [head_rows(q) for q in (q0, q1, q2, q3)]
     queries = jnp.concatenate([p[0] for p in parts], axis=0)
     wanted = jnp.concatenate([p[1] for p in parts], axis=0)
-    own_keys = jnp.concatenate([k0[...], k1[...], k2[...], k3[...]], axis=1)
+    own_keys = jnp.concatenate([ko[0], ko[1], ko[2], ko[3]], axis=1)
     far_keys = jnp.concatenate([kp[0], kp[1], kp[2], kp[3]], axis=1)
     own = wanted == group
     valid = wanted < 1.5
@@ -271,17 +275,16 @@
     out_ref[...] = scr[...].reshape(out_ref.shape).astype(bf16)
 
 
-def hidden_kernel(info, terms_ref, x_ref, gain_ref, extra_ref, hidden_ref, packed_ref):
+def hidden_kernel(info, terms_ref, x_ref, gain_ref, ids_ref, gates_ref, hidden_ref, packed_ref):
     attention = jnp.sum(terms_ref[...].astype(f32), axis=0)
     rounded = (x_ref[...].astype(f32) + attention).astype(bf16)
     hidden_ref[...] = rounded
     hidden = rounded.astype(f32)
     features = hidden.shape[1]
     gained = (hidden * gain_ref[...]).astype(bf16)
-    extra = extra_ref[...]
-    lane = lax.broadcasted_iota(jnp.int32, extra.shape, 1)
-    for part, v in enumerate(split3(jnp.sum(hidden * hidden, axis=1, keepdims=True))):
-        extra = jnp.where(lane == 32 + part, v, extra)
+    columns = [ids_ref[...].astype(f32), *split3(gates_ref[...])]
+    columns += split3(jnp.sum(hidden * hidden, axis=1, keepdims=True))
+    extra = jnp.concatenate([*columns, jnp.zeros((hidden.shape[0], 29), f32)], axis=1)
     extra = extra.astype(bf16)
     for i in range(packed_ref.shape[0]):
         packed_ref[i, :, :features] = gained
@@ -526,19 +529,13 @@
     pieces, packets = along_x(span), along_y(packet)
     pieces, packets = lax.optimization_barrier((pieces, packets))
     resident = resident_attention(cache_len, packets[0], dec_cache)
-    g_high = lax.reduce_precision(expert_gates, 8, 7)
-    g_mid = lax.reduce_precision(expert_gates - g_high, 8, 7)
-    g_low = lax.reduce_precision(expert_gates - g_high - g_mid, 8, 7)
-    extra = jnp.concatenate(
-        [expert_ids.astype(f32), g_high, g_mid, g_low, jnp.zeros((16, 32), f32)], axis=1
-    )
-    gain = lax.dynamic_slice(norm_gain, (seq * features,), (features,))[None]
+    stacked = stack_of(pieces)
     part = call(
         span_kernel,
         jax.ShapeDtypeStruct((32, 9 * VDIM), bf16),
-        [info, *packets, *pieces, other_core(stack_of(pieces)), w_uv, in_vmem(resident)],
+        [info, *[in_vmem(v) for v in (*packets, stacked, other_core(stacked))], w_uv, in_vmem(resident)],
         [pltpu.VMEM((SIDE, 8, 9 * VDIM), f32)],
-        fetch=tuple(range(1, 11)),
+        fetch=(7,),
         mib=16,
     )
     part, w_back = lax.optimization_barrier((part, w_down[0]))
@@ -558,15 +555,19 @@
         [info, *values, w_out.T],
         [pltpu.VMEM((SIDE, SIDE, 8, features), f32)],
     )
+    product, expert_ids, expert_gates, norm_gain, x_dec = lax.optimization_barrier(
+        (product, expert_ids, expert_gates, norm_gain, x_dec)
+    )
     terms = lax.all_to_all(product.reshape(depth, 16, features), "expert", 0, 0, tiled=True)
 
+    gain = lax.dynamic_slice(norm_gain, (seq * features,), (features,))[None]
     hidden, packed = call(
         hidden_kernel,
         [
             jax.ShapeDtypeStruct((16, features), bf16),
             jax.ShapeDtypeStruct((depth, 16, features + 64), bf16),
         ],
-        [info, terms, x_dec, gain, extra],
+        [info, terms, x_dec, gain, expert_ids, expert_gates],
     )
     rows = lax.all_to_all(packed, "expert", 0, 0, tiled=True).reshape(16 * depth, features + 64)
     rows, q_pre, w_back = lax.optimization_barrier((rows, q_pre, w_back))

time: 173 us -> 171 us (0.988)
  local copies, waits for them, and re-layouts: 7.78 us -> 5.87 us
    unnamed x35 -> x18, local copies, waits for them, and re-layouts: 3.9 us -> 2.08 us
  transfers between devices with their start and end apart: 25 -> 25, of which waited for: 15 -> 16; matrix products, arithmetic and copies ran while one was open for 2% -> 2% of each run, Pallas kernels for 20% -> 20%
where the time goes in v5:
time: 171 us; the launch traced here: 170 us
  waiting for transfers between devices  46.9 us (27%)
  starting transfers between devices  39.4 us (23%)
  Pallas kernels  36.6 us (21%)
  blocking collectives  23.4 us (14%)
  between operations  14.9 us (9%)
  local copies, waits for them, and re-layouts  5.87 us (3%)
  other arithmetic  3.33 us (2%)
    pallas_call x1, Pallas kernels, prompt_attention(): pl.pallas_call(prompt_kernel, out_shape=jax.ShapeDtypeStruct((tokens, ste...  17 us
    all_to_all x1, blocking collectives, on_device(): lax.all_to_all(share, 'seq', 0, 0, tiled=True, axis_index_groups=same_place)  13 us
    pallas_call x7, Pallas kernels, call(): pl.pallas_call(body, out_shape=out_shape, in_specs=place, out_specs=[VMEM...  12.8 us
    all_to_all x1, blocking collectives, on_device(): lax.all_to_all(share.reshape(depth, 16, features), 'expert', 0, 0, tiled=...  10.4 us
    ppermute x6, waiting for transfers between devices, to_y(): lax.ppermute(array, 'seq', [(y * SIDE + x, (y + d) % SIDE * SIDE + x) for...  8.4 us
    ppermute x3, starting transfers between devices, other_core(): return lax.ppermute(array, 'group', [(0, 1), (1, 0)])  8.4 us
    all_to_all x1, waiting for transfers between devices, on_device(): lax.all_to_all(packed, 'expert', 0, 0, tiled=True)  7.92 us
    all_to_all x1, waiting for transfers between devices, everyone(): lax.all_to_all(jnp.broadcast_to(array[None], (count,) + array.shape), axi...  7.7 us
  transfers between devices with their start and end apart: 25, of which 16 were waited for; matrix products, arithmetic and copies ran while one was open for 2% of the time, Pallas kernels for 20%

profile of v5, /device:TPU:1, one launch (start us, length us, event | category | flops | bytes accessed | tf_op | source)
XLA Modules:
  0.0 170.3 jit_solution(3177352103587907561)
XLA Ops:
  8.8 1.8 %pad_maximum_fusion = bf16[576,256]{1,0:T(8,128)(2,1)} fusion(bf16[576,128]{1,0:T(8,128)(2,1)} %bitcast.24, bf16[576,128]{1,0:T(8,128)(2,1)} %bitcast.31), kind=kLoop, calls=%fused_computation.1 | loop fusion | flops 589824 | bytes 589824 | tf_op jit(solution)/shard_map/concatenate | solution.py:528
  10.5 3.6 %collective-permute-start.5 = (bf16[16,2432]{1,0:T(8,128)(2,1)S(1)}, bf16[16,2432]{1,0:T(8,128)(2,1)S(1)}, u32[]{:S(2)}, u32[]{:S(2)}) collective-permute-start(bf16[16,2432]{1,0:T(8,128)(2,1)S(1)} %maximum_maximum_fusion.q_ref.refs_1_), channel_id=1, source_target_pairs={{0,96},{8,104},{16,112},{24,120},{32,0},{40,8},{48,16},{56,24},{64... | collective-permute-start | bytes 233480 | tf_op jit(solution)/shard_map/ppermute | solution.py:100
  14.2 2.5 %collective-permute-start.2 = (bf16[576,128]{1,0:T(8,128)(2,1)}, bf16[576,128]{1,0:T(8,128)(2,1)S(1)}, u32[]{:S(2)}, u32[]{:S(2)}) collective-permute-start(bf16[576,128]{1,0:T(8,128)(2,1)} %bitcast.25), channel_id=1, source_target_pairs={{0,24},{8,0},{16,8},{24,16},{32,56},{40,32},{48,40},{56,48},{64,88... | collective-permute-start | bytes 442376 | tf_op jit(solution)/shard_map/ppermute | solution.py:92
  18.8 3.8 %collective-permute-done.4.refs_3_ = bf16[16,2432]{1,0:T(8,128)(2,1)S(1)} collective-permute-done((bf16[16,2432]{1,0:T(8,128)(2,1)S(1)}, bf16[16,2432]{1,0:T(8,128)(2,1)S(1)}, u32[]{:S(2)}, u32[]{:S(2)}) %collective-permute-start.4) | collective-permute-done | bytes 77856 | tf_op jit(solution)/shard_map/ppermute | solution.py:100
  23.7 3.3 %collective-permute-done.k1 = bf16[576,128]{1,0:T(8,128)(2,1)S(1)} collective-permute-done((bf16[576,128]{1,0:T(8,128)(2,1)}, bf16[576,128]{1,0:T(8,128)(2,1)S(1)}, u32[]{:S(2)}, u32[]{:S(2)}) %collective-permute-start) | collective-permute-done | bytes 147488 | tf_op jit(solution)/shard_map/ppermute | solution.py:92
  29.6 2.7 %shard_map.168.refs_8_ = f32[64,768]{1,0:T(8,128)S(1)} custom-call(s32[8]{0:T(128)S(1)} %copy-done.5, bf16[16,2432]{1,0:T(8,128)(2,1)S(1)} %maximum_maximum_fusion.q_ref.refs_1_, bf16[8,576,128]{2,1,0:T(8,128)(2,1)} %cache_hbm.1), custom_call_target="tpu_custom_call" | custom-call | tf_op jit(solution)/shard_map/pallas_call | solution.py:192
  32.3 3.2 %shard_map.169.refs_1_ = bf16[32,1152]{1,0:T(8,128)(2,1)S(1)} custom-call(s32[8]{0:T(128)S(1)} %stack.31.refs_0_.info, bf16[16,2432]{1,0:T(8,128)(2,1)S(1)} %maximum_maximum_fusion.q_ref.refs_1_, bf16[16,2432]{1,0:T(8,128)(2,1)S(1)} %collective-permute-done.3.refs_2_, bf16[16,2432]{1,0:T(8,128)(2,1)S(1)} %collective-permute-done.4.refs_3_, ...), custom_call_target="tpu_custom_call" | custom-call | tf_op jit(solution)/shard_map/pallas_call | solution.py:54
  37.2 3.1 %shard_map.170 = (bf16[4,448,128]{2,1,0:T(8,128)(2,1)}, bf16[4,448,128]{2,1,0:T(8,128)(2,1)}, bf16[4,448,128]{2,1,0:T(8,128)(2,1)}, bf16[4,448,128]{2,1,0:T(8,128)(2,1)}) custom-call(s32[8]{0:T(128)S(1)} %stack.31.refs_0_.info, bf16[128,7168]{1,0:T(8,128)(2,1)S(1)} %bitcast.21), custom_call_target="tpu_custom_call" | custom-call | tf_op jit(solution)/shard_map/pallas_call | solution.py:376
  47.0 1.9 %collective-permute-start.13 = (bf16[4,448,128]{2,1,0:T(8,128)(2,1)}, bf16[4,448,128]{2,1,0:T(8,128)(2,1)S(1)}, u32[]{:S(2)}, u32[]{:S(2)}) collective-permute-start(bf16[4,448,128]{2,1,0:T(8,128)(2,1)} %get-tuple-element.77), channel_id=1, source_target_pairs={{0,8},{8,0},{16,24},{24,16},{32,40},{40,32},{48,56},{56,48},{64,72... | collective-permute-start | bytes 1376264 | tf_op jit(solution)/shard_map/ppermute | solution.py:112
  48.9 2.0 %collective-permute-done.11.refs_3_ = bf16[32,1024]{1,0:T(8,128)(2,1)S(1)} collective-permute-done((bf16[32,1024]{1,0:T(8,128)(2,1)S(1)}, bf16[32,1024]{1,0:T(8,128)(2,1)S(1)}, u32[]{:S(2)}, u32[]{:S(2)}) %collective-permute-start.11) | collective-permute-done | bytes 65568 | tf_op jit(solution)/shard_map/ppermute | solution.py:92
  53.9 7.1 %all-to-all-start = ((bf16[8,16,448]{2,1,0:T(8,128)(2,1)}), bf16[8,16,448]{2,1,0:T(8,128)(2,1)S(1)}, u32[]{:S(2)}, u32[]{:S(2)}) async-start(bf16[8,16,448]{2,1,0:T(8,128)(2,1)} %bitcast.11), calls=%async_computation | async-start | bytes 262144 | tf_op jit(solution)/shard_map/all_to_all | solution.py:561
  61.9 7.1 %all-to-all-done.refs_1_ = bf16[8,16,448]{2,1,0:T(8,128)(2,1)S(1)} async-done(((bf16[8,16,448]{2,1,0:T(8,128)(2,1)}), bf16[8,16,448]{2,1,0:T(8,128)(2,1)S(1)}, u32[]{:S(2)}, u32[]{:S(2)}) %all-to-all-start) | async-done | bytes 114720 | tf_op jit(solution)/shard_map/all_to_all | solution.py:561
  70.4 3.4 %all-to-all-start.1 = ((bf16[8,16,512]{2,1,0:T(8,128)(2,1)}), bf16[8,16,512]{2,1,0:T(8,128)(2,1)S(1)}, u32[]{:S(2)}, u32[]{:S(2)}) async-start(bf16[8,16,512]{2,1,0:T(8,128)(2,1)} %get-tuple-element.75), calls=%async_computation.1 | async-start | bytes 262144 | tf_op jit(solution)/shard_map/all_to_all | solution.py:572
  73.8 7.9 %all-to-all-done.1 = bf16[8,16,512]{2,1,0:T(8,128)(2,1)S(1)} async-done(((bf16[8,16,512]{2,1,0:T(8,128)(2,1)}), bf16[8,16,512]{2,1,0:T(8,128)(2,1)S(1)}, u32[]{:S(2)}, u32[]{:S(2)}) %all-to-all-start.1) | async-done | bytes 131104 | tf_op jit(solution)/shard_map/all_to_all | solution.py:572
  83.3 3.7 %all-to-all-start.2 = ((bf16[16,128,512]{2,1,0:T(8,128)(2,1)}), bf16[16,128,512]{2,1,0:T(8,128)(2,1)S(1)}, u32[]{:S(2)}, u32[]{:S(2)}) async-start(bf16[16,128,512]{2,1,0:T(8,128)(2,1)} %broadcast_in_dim.20), calls=%async_computation.2 | async-start | bytes 4194304 | tf_op jit(solution)/shard_map/all_to_all | solution.py:128
  87.0 17.0 %shard_map.174 = bf16[128,4096]{1,0:T(8,128)(2,1)} custom-call(s32[8]{0:T(128)S(1)} %stack.31.refs_0_.info, bf16[128,4608]{1,0:T(8,128)(2,1)} %bitcast.33, bf16[16,576,256]{2,1,0:T(8,128)(2,1)} %bitcast.32), custom_call_target="tpu_custom_call" | custom-call | flops 9126805504 | bytes 8388608 | tf_op jit(solution)/shard_map/pallas_call | solution.py:461
  104.1 7.7 %all-to-all-done.2.refs_1_ = bf16[16,128,512]{2,1,0:T(8,128)(2,1)S(1)} async-done(((bf16[16,128,512]{2,1,0:T(8,128)(2,1)}), bf16[16,128,512]{2,1,0:T(8,128)(2,1)S(1)}, u32[]{:S(2)}, u32[]{:S(2)}) %all-to-all-start.2) | async-done | bytes 2097184 | tf_op jit(solution)/shard_map/all_to_all | solution.py:128
  111.8 6.9 %collective-permute-start.15 = (bf16[16,128,512]{2,1,0:T(8,128)(2,1)S(1)}, bf16[16,128,512]{2,1,0:T(8,128)(2,1)S(1)}, u32[]{:S(2)}, u32[]{:S(2)}) collective-permute-start(bf16[16,128,512]{2,1,0:T(8,128)(2,1)S(1)} %all-to-all-done.2.refs_1_), channel_id=1, source_target_pairs={{0,128},{128,0},{1,129},{129,1},{2,130},{130,2},{3,131},{131,3},{4... | collective-permute-start | bytes 6291464 | tf_op jit(solution)/shard_map/ppermute | solution.py:124
  118.7 2.0 %copy-done = bf16[1,2,7168,128]{3,2,1,0:T(8,128)(2,1)S(1)} copy-done((bf16[1,2,7168,128]{3,2,1,0:T(8,128)(2,1)S(1)}, bf16[1,2,7168,128]{3,2,1,0:T(8,128)(2,1)}, u32[]{:S(2)}) %copy-start) | copy-done | bytes 3670040
  124.2 2.1 %collective-permute-start.18 = (bf16[192,128]{1,0:T(8,128)(2,1)S(1)}, bf16[192,128]{1,0:T(8,128)(2,1)S(1)}, u32[]{:S(2)}, u32[]{:S(2)}) collective-permute-start(bf16[192,128]{1,0:T(8,128)(2,1)S(1)} %get-tuple-element.89.refs_1_), channel_id=1, source_target_pairs={{0,40},{8,32},{16,56},{24,48},{32,8},{40,0},{48,24},{56,16},{64,10... | collective-permute-start | bytes 147464 | tf_op jit(solution)/shard_map/ppermute | solution.py:112
  126.9 4.8 %collective-permute-done.19.refs_8_ = bf16[4,448,128]{2,1,0:T(8,128)(2,1)S(1)} collective-permute-done((bf16[4,448,128]{2,1,0:T(8,128)(2,1)S(1)}, bf16[4,448,128]{2,1,0:T(8,128)(2,1)S(1)}, u32[]{:S(2)}, u32[]{:S(2)}) %collective-permute-start.19) | collective-permute-done | bytes 458784 | tf_op jit(solution)/shard_map/ppermute | solution.py:112
  134.1 2.6 %shard_map.177 = (f32[4,128,448]{2,1,0:T(8,128)S(1)}, bf16[4,128,448]{2,1,0:T(8,128)(2,1)S(1)}) custom-call(s32[8]{0:T(128)S(1)} %stack.31.refs_0_.info, bf16[192,128]{1,0:T(8,128)(2,1)S(1)} %get-tuple-element.89.refs_1_, bf16[192,128]{1,0:T(8,128)(2,1)S(1)} %collective-permute-done.16.refs_2_, bf16[192,128]{1,0:T(8,128)(2,1)S(1)} %collective-permute-done.17.refs_3_, ...), custom_call_target="tpu_custom_call" | custom-call | tf_op jit(solution)/shard_map/pallas_call | solution.py:54
  139.3 13.0 %all_to_all.25 = bf16[4,128,448]{1,2,0:T(8,128)(2,1)S(1)} all-to-all(bf16[4,128,448]{1,2,0:T(8,128)(2,1)S(1)} %copy.28), channel_id=1, replica_groups={{0,16,64,80},{8,24,72,88},{32,48,96,112},{40,56,104,120},{1,17,65,81},{..., dimensions={0} | all-to-all | bytes 917504 | tf_op jit(solution)/shard_map/all_to_all | solution.py:590
  152.4 10.4 %all_to_all.26 = bf16[8,16,448]{2,1,0:T(8,128)(2,1)S(1)} all-to-all(bf16[8,16,448]{2,1,0:T(8,128)(2,1)S(1)} %bitcast.30), channel_id=1, replica_groups=mesh['group'=2,'seq'=16,'expert'=8] {'expert'}, dimensions={0} | all-to-all | bytes 229376 | tf_op jit(solution)/shard_map/all_to_all | solution.py:592
  (74 shorter events, 31.8 us)
Async XLA Ops:
  7.2 79.8 %all-gather.3.cloned.1.call-start = ((), (), s32[]{:S(2)}) async-start(), calls=%async_computation.5 | async-start | bytes 5013504 | tf_op jit(solution)/shard_map/all_gather | solution.py:528
  10.5 7.6 %collective-permute-start.5 = (bf16[16,2432]{1,0:T(8,128)(2,1)S(1)}, bf16[16,2432]{1,0:T(8,128)(2,1)S(1)}, u32[]{:S(2)}, u32[]{:S(2)}) collective-permute-start(bf16[16,2432]{1,0:T(8,128)(2,1)S(1)} %maximum_maximum_fusion.q_ref.refs_1_), channel_id=1, source_target_pairs={{0,96},{8,104},{16,112},{24,120},{32,0},{40,8},{48,16},{56,24},{64... | collective-permute-start | bytes 233480 | tf_op jit(solution)/shard_map/ppermute | solution.py:100
  14.2 9.5 %collective-permute-start.2 = (bf16[576,128]{1,0:T(8,128)(2,1)}, bf16[576,128]{1,0:T(8,128)(2,1)S(1)}, u32[]{:S(2)}, u32[]{:S(2)}) collective-permute-start(bf16[576,128]{1,0:T(8,128)(2,1)} %bitcast.25), channel_id=1, source_target_pairs={{0,24},{8,0},{16,8},{24,16},{32,56},{40,32},{48,40},{56,48},{64,88... | collective-permute-start | bytes 442376 | tf_op jit(solution)/shard_map/ppermute | solution.py:92
  16.6 7.0 %collective-permute-start.1 = (bf16[576,128]{1,0:T(8,128)(2,1)}, bf16[576,128]{1,0:T(8,128)(2,1)S(1)}, u32[]{:S(2)}, u32[]{:S(2)}) collective-permute-start(bf16[576,128]{1,0:T(8,128)(2,1)} %bitcast.26), channel_id=1, source_target_pairs={{0,16},{8,24},{16,0},{24,8},{32,48},{40,56},{48,32},{56,40},{64,80... | collective-permute-start | bytes 442376 | tf_op jit(solution)/shard_map/ppermute | solution.py:92
  17.2 9.8 %collective-permute-start = (bf16[576,128]{1,0:T(8,128)(2,1)}, bf16[576,128]{1,0:T(8,128)(2,1)S(1)}, u32[]{:S(2)}, u32[]{:S(2)}) collective-permute-start(bf16[576,128]{1,0:T(8,128)(2,1)} %bitcast.27), channel_id=1, source_target_pairs={{0,8},{8,16},{16,24},{24,0},{32,40},{40,48},{48,56},{56,32},{64,72... | collective-permute-start | bytes 442376 | tf_op jit(solution)/shard_map/ppermute | solution.py:92
  17.8 4.8 %collective-permute-start.4 = (bf16[16,2432]{1,0:T(8,128)(2,1)S(1)}, bf16[16,2432]{1,0:T(8,128)(2,1)S(1)}, u32[]{:S(2)}, u32[]{:S(2)}) collective-permute-start(bf16[16,2432]{1,0:T(8,128)(2,1)S(1)} %maximum_maximum_fusion.q_ref.refs_1_), channel_id=1, source_target_pairs={{0,64},{8,72},{16,80},{24,88},{32,96},{40,104},{48,112},{56,120},{... | collective-permute-start | bytes 233480 | tf_op jit(solution)/shard_map/ppermute | solution.py:100
  18.1 5.5 %collective-permute-start.3 = (bf16[16,2432]{1,0:T(8,128)(2,1)S(1)}, bf16[16,2432]{1,0:T(8,128)(2,1)S(1)}, u32[]{:S(2)}, u32[]{:S(2)}) collective-permute-start(bf16[16,2432]{1,0:T(8,128)(2,1)S(1)} %maximum_maximum_fusion.q_ref.refs_1_), channel_id=1, source_target_pairs={{0,32},{8,40},{16,48},{24,56},{32,64},{40,72},{48,80},{56,88},{64,... | collective-permute-start | bytes 233480 | tf_op jit(solution)/shard_map/ppermute | solution.py:100
  27.9 4.5 %collective-permute-start.6 = (bf16[4,576,128]{2,1,0:T(8,128)(2,1)S(1)}, bf16[4,576,128]{2,1,0:T(8,128)(2,1)S(1)}, u32[]{:S(2)}, u32[]{:S(2)}) collective-permute-start(bf16[4,576,128]{2,1,0:T(8,128)(2,1)S(1)} %shard_map.167.refs_5_), channel_id=1, source_target_pairs={{0,128},{128,0},{1,129},{129,1},{2,130},{130,2},{3,131},{131,3},{4... | collective-permute-start | bytes 1769480 | tf_op jit(solution)/shard_map/ppermute | solution.py:124
  35.6 5.4 %collective-permute-start.9 = (bf16[32,1152]{1,0:T(8,128)(2,1)S(1)}, bf16[32,1152]{1,0:T(8,128)(2,1)S(1)}, u32[]{:S(2)}, u32[]{:S(2)}) collective-permute-start(bf16[32,1152]{1,0:T(8,128)(2,1)S(1)} %shard_map.169.refs_1_), channel_id=1, source_target_pairs={{0,96},{8,104},{16,112},{24,120},{32,0},{40,8},{48,16},{56,24},{64... | collective-permute-start | bytes 221192 | tf_op jit(solution)/shard_map/ppermute | solution.py:100
  36.2 5.9 %collective-permute-start.8 = (bf16[32,1152]{1,0:T(8,128)(2,1)S(1)}, bf16[32,1152]{1,0:T(8,128)(2,1)S(1)}, u32[]{:S(2)}, u32[]{:S(2)}) collective-permute-start(bf16[32,1152]{1,0:T(8,128)(2,1)S(1)} %shard_map.169.refs_1_), channel_id=1, source_target_pairs={{0,64},{8,72},{16,80},{24,88},{32,96},{40,104},{48,112},{56,120},{... | collective-permute-start | bytes 221192 | tf_op jit(solution)/shard_map/ppermute | solution.py:100
  36.3 7.5 %collective-permute-start.7 = (bf16[32,1152]{1,0:T(8,128)(2,1)S(1)}, bf16[32,1152]{1,0:T(8,128)(2,1)S(1)}, u32[]{:S(2)}, u32[]{:S(2)}) collective-permute-start(bf16[32,1152]{1,0:T(8,128)(2,1)S(1)} %shard_map.169.refs_1_), channel_id=1, source_target_pairs={{0,32},{8,40},{16,48},{24,56},{32,64},{40,72},{48,80},{56,88},{64,... | collective-permute-start | bytes 221192 | tf_op jit(solution)/shard_map/ppermute | solution.py:100
  44.7 4.2 %collective-permute-start.12 = (bf16[32,1024]{1,0:T(8,128)(2,1)S(1)}, bf16[32,1024]{1,0:T(8,128)(2,1)S(1)}, u32[]{:S(2)}, u32[]{:S(2)}) collective-permute-start(bf16[32,1024]{1,0:T(8,128)(2,1)S(1)} %shard_map.171.refs_1_), channel_id=1, source_target_pairs={{0,24},{8,0},{16,8},{24,16},{32,56},{40,32},{48,40},{56,48},{64,88... | collective-permute-start | bytes 196616 | tf_op jit(solution)/shard_map/ppermute | solution.py:92
  46.2 4.6 %collective-permute-start.11 = (bf16[32,1024]{1,0:T(8,128)(2,1)S(1)}, bf16[32,1024]{1,0:T(8,128)(2,1)S(1)}, u32[]{:S(2)}, u32[]{:S(2)}) collective-permute-start(bf16[32,1024]{1,0:T(8,128)(2,1)S(1)} %shard_map.171.refs_1_), channel_id=1, source_target_pairs={{0,16},{8,24},{16,0},{24,8},{32,48},{40,56},{48,32},{56,40},{64,80... | collective-permute-start | bytes 196616 | tf_op jit(solution)/shard_map/ppermute | solution.py:92
  47.0 5.2 %collective-permute-start.10 = (bf16[32,1024]{1,0:T(8,128)(2,1)S(1)}, bf16[32,1024]{1,0:T(8,128)(2,1)S(1)}, u32[]{:S(2)}, u32[]{:S(2)}) collective-permute-start(bf16[32,1024]{1,0:T(8,128)(2,1)S(1)} %shard_map.171.refs_1_), channel_id=1, source_target_pairs={{0,8},{8,16},{16,24},{24,0},{32,40},{40,48},{48,56},{56,32},{64,72... | collective-permute-start | bytes 196616 | tf_op jit(solution)/shard_map/ppermute | solution.py:92
  47.0 26.8 %collective-permute-start.13 = (bf16[4,448,128]{2,1,0:T(8,128)(2,1)}, bf16[4,448,128]{2,1,0:T(8,128)(2,1)S(1)}, u32[]{:S(2)}, u32[]{:S(2)}) collective-permute-start(bf16[4,448,128]{2,1,0:T(8,128)(2,1)} %get-tuple-element.77), channel_id=1, source_target_pairs={{0,8},{8,0},{16,24},{24,16},{32,40},{40,32},{48,56},{56,48},{64,72... | collective-permute-start | bytes 1376264 | tf_op jit(solution)/shard_map/ppermute | solution.py:112
  48.9 24.9 %collective-permute-start.14 = (bf16[4,448,128]{2,1,0:T(8,128)(2,1)}, bf16[4,448,128]{2,1,0:T(8,128)(2,1)S(1)}, u32[]{:S(2)}, u32[]{:S(2)}) collective-permute-start(bf16[4,448,128]{2,1,0:T(8,128)(2,1)} %get-tuple-element.78), channel_id=1, source_target_pairs={{0,32},{8,40},{16,48},{24,56},{32,0},{40,8},{48,16},{56,24},{64,96... | collective-permute-start | bytes 1376264 | tf_op jit(solution)/shard_map/ppermute | solution.py:112
  53.9 15.1 %all-to-all-start = ((bf16[8,16,448]{2,1,0:T(8,128)(2,1)}), bf16[8,16,448]{2,1,0:T(8,128)(2,1)S(1)}, u32[]{:S(2)}, u32[]{:S(2)}) async-start(bf16[8,16,448]{2,1,0:T(8,128)(2,1)} %bitcast.11), calls=%async_computation | async-start | bytes 262144 | tf_op jit(solution)/shard_map/all_to_all | solution.py:561
  70.4 11.3 %all-to-all-start.1 = ((bf16[8,16,512]{2,1,0:T(8,128)(2,1)}), bf16[8,16,512]{2,1,0:T(8,128)(2,1)S(1)}, u32[]{:S(2)}, u32[]{:S(2)}) async-start(bf16[8,16,512]{2,1,0:T(8,128)(2,1)} %get-tuple-element.75), calls=%async_computation.1 | async-start | bytes 262144 | tf_op jit(solution)/shard_map/all_to_all | solution.py:572
  83.3 28.5 %all-to-all-start.2 = ((bf16[16,128,512]{2,1,0:T(8,128)(2,1)}), bf16[16,128,512]{2,1,0:T(8,128)(2,1)S(1)}, u32[]{:S(2)}, u32[]{:S(2)}) async-start(bf16[16,128,512]{2,1,0:T(8,128)(2,1)} %broadcast_in_dim.20), calls=%async_computation.2 | async-start | bytes 4194304 | tf_op jit(solution)/shard_map/all_to_all | solution.py:128
  111.8 10.6 %collective-permute-start.15 = (bf16[16,128,512]{2,1,0:T(8,128)(2,1)S(1)}, bf16[16,128,512]{2,1,0:T(8,128)(2,1)S(1)}, u32[]{:S(2)}, u32[]{:S(2)}) collective-permute-start(bf16[16,128,512]{2,1,0:T(8,128)(2,1)S(1)} %all-to-all-done.2.refs_1_), channel_id=1, source_target_pairs={{0,128},{128,0},{1,129},{129,1},{2,130},{130,2},{3,131},{131,3},{4... | collective-permute-start | bytes 6291464 | tf_op jit(solution)/shard_map/ppermute | solution.py:124
  118.6 13.1 %collective-permute-start.19 = (bf16[4,448,128]{2,1,0:T(8,128)(2,1)S(1)}, bf16[4,448,128]{2,1,0:T(8,128)(2,1)S(1)}, u32[]{:S(2)}, u32[]{:S(2)}) collective-permute-start(bf16[4,448,128]{2,1,0:T(8,128)(2,1)S(1)} %copy-done.8), channel_id=1, source_target_pairs={{0,40},{8,32},{16,56},{24,48},{32,8},{40,0},{48,24},{56,16},{64,10... | collective-permute-start | bytes 1376264 | tf_op jit(solution)/shard_map/ppermute | solution.py:112
  124.2 8.6 %collective-permute-start.18 = (bf16[192,128]{1,0:T(8,128)(2,1)S(1)}, bf16[192,128]{1,0:T(8,128)(2,1)S(1)}, u32[]{:S(2)}, u32[]{:S(2)}) collective-permute-start(bf16[192,128]{1,0:T(8,128)(2,1)S(1)} %get-tuple-element.89.refs_1_), channel_id=1, source_target_pairs={{0,40},{8,32},{16,56},{24,48},{32,8},{40,0},{48,24},{56,16},{64,10... | collective-permute-start | bytes 147464 | tf_op jit(solution)/shard_map/ppermute | solution.py:112
  126.3 7.8 %collective-permute-start.17 = (bf16[192,128]{1,0:T(8,128)(2,1)S(1)}, bf16[192,128]{1,0:T(8,128)(2,1)S(1)}, u32[]{:S(2)}, u32[]{:S(2)}) collective-permute-start(bf16[192,128]{1,0:T(8,128)(2,1)S(1)} %get-tuple-element.89.refs_1_), channel_id=1, source_target_pairs={{0,32},{8,40},{16,48},{24,56},{32,0},{40,8},{48,16},{56,24},{64,96... | collective-permute-start | bytes 147464 | tf_op jit(solution)/shard_map/ppermute | solution.py:112
  126.3 7.8 %collective-permute-start.16 = (bf16[192,128]{1,0:T(8,128)(2,1)S(1)}, bf16[192,128]{1,0:T(8,128)(2,1)S(1)}, u32[]{:S(2)}, u32[]{:S(2)}) collective-permute-start(bf16[192,128]{1,0:T(8,128)(2,1)S(1)} %get-tuple-element.89.refs_1_), channel_id=1, source_target_pairs={{0,8},{8,0},{16,24},{24,16},{32,40},{40,32},{48,56},{56,48},{64,72... | collective-permute-start | bytes 147464 | tf_op jit(solution)/shard_map/ppermute | solution.py:112
  (10 other events, 181.6 us)
Sparse Core Ops, SparseCore 0:
  10.6 70.3 all-gather.2

commit v6 on v5

--- a/solution.py
+++ b/solution.py
@@ -161,11 +161,8 @@
     )(in_hbm(pieces[0]), *[in_vmem(piece) for piece in pieces[1:]])
 
 
-def resident_kernel(lens, q_ref, cache_hbm, state_ref, cache_ref, sem):
-    cache_copy = pltpu.make_async_copy(cache_hbm, cache_ref, sem)
-    cache_copy.start()
+def resident_kernel(lens, q_ref, cache_ref, state_ref):
     queries, _ = head_rows(q_ref)
-    cache_copy.wait()
     count = cache_ref.shape[0]
     row = lax.rem(lax.broadcasted_iota(jnp.int32, (queries.shape[0], 128), 0), count)
     column = lax.broadcasted_iota(jnp.int32, (queries.shape[0], 128), 1)
@@ -192,11 +189,10 @@
     return pl.pallas_call(
         resident_kernel,
         out_shape=pltpu.VMEM((64, LATENT + 256), f32),
-        in_specs=[SMEM, VMEM, pl.BlockSpec(memory_space=pltpu.HBM)],
+        in_specs=[SMEM, VMEM, VMEM],
         out_specs=VMEM,
-        scratch_shapes=[pltpu.VMEM(dec_cache.shape, bf16), pltpu.SemaphoreType.DMA],
         compiler_params=pltpu.CompilerParams(vmem_limit_bytes=8 << 20),
-    )(cache_len, packet, in_hbm(dec_cache))
+    )(cache_len, packet, in_vmem(dec_cache))
 
 
 def span_kernel(

time: 171 us -> 170 us (level)
  transfers between devices with their start and end apart: 25 -> 25, of which waited for: 16 -> 15; matrix products, arithmetic and copies ran while one was open for 2% -> 2% of each run, Pallas kernels for 20% -> 19%
where the time goes in v6:
time: 170 us
  waiting for transfers between devices  47.8 us (28%)
  starting transfers between devices  39.1 us (23%)
  Pallas kernels  35.3 us (21%)
  blocking collectives  23.4 us (14%)
  between operations  14.9 us (9%)
  local copies, waits for them, and re-layouts  5.88 us (3%)
  other arithmetic  3.41 us (2%)
    pallas_call x1, Pallas kernels, prompt_attention(): pl.pallas_call(prompt_kernel, out_shape=jax.ShapeDtypeStruct((tokens, ste...  17 us
    all_to_all x1, blocking collectives, on_device(): lax.all_to_all(share, 'seq', 0, 0, tiled=True, axis_index_groups=same_place)  13 us
    pallas_call x7, Pallas kernels, call(): pl.pallas_call(body, out_shape=out_shape, in_specs=place, out_specs=[VMEM...  12.8 us
    all_to_all x1, blocking collectives, on_device(): lax.all_to_all(share.reshape(depth, 16, features), 'expert', 0, 0, tiled=...  10.4 us
    ppermute x6, waiting for transfers between devices, to_y(): lax.ppermute(array, 'seq', [(y * SIDE + x, (y + d) % SIDE * SIDE + x) for...  9.26 us
    ppermute x3, starting transfers between devices, other_core(): return lax.ppermute(array, 'group', [(0, 1), (1, 0)])  8.3 us
    all_to_all x1, waiting for transfers between devices, on_device(): lax.all_to_all(packed, 'expert', 0, 0, tiled=True)  7.92 us
    all_to_all x1, waiting for transfers between devices, everyone(): lax.all_to_all(jnp.broadcast_to(array[None], (count,) + array.shape), axi...  7.72 us
  transfers between devices with their start and end apart: 25, of which 15 were waited for; matrix products, arithmetic and copies ran while one was open for 2% of the time, Pallas kernels for 19%

profile of v6, /device:TPU:1, one launch (start us, length us, event | category | flops | bytes accessed | tf_op | source)
XLA Modules:
  0.0 169.9 jit_solution(5453132665670571727)
XLA Ops:
  8.9 1.7 %pad_maximum_fusion = bf16[576,256]{1,0:T(8,128)(2,1)} fusion(bf16[576,128]{1,0:T(8,128)(2,1)} %bitcast.24, bf16[576,128]{1,0:T(8,128)(2,1)} %bitcast.31), kind=kLoop, calls=%fused_computation.1 | loop fusion | flops 589824 | bytes 589824 | tf_op jit(solution)/shard_map/concatenate | solution.py:524
  10.6 3.6 %collective-permute-start.5 = (bf16[16,2432]{1,0:T(8,128)(2,1)S(1)}, bf16[16,2432]{1,0:T(8,128)(2,1)S(1)}, u32[]{:S(2)}, u32[]{:S(2)}) collective-permute-start(bf16[16,2432]{1,0:T(8,128)(2,1)S(1)} %maximum_maximum_fusion.q_ref.refs_1_), channel_id=1, source_target_pairs={{0,96},{8,104},{16,112},{24,120},{32,0},{40,8},{48,16},{56,24},{64... | collective-permute-start | bytes 233480 | tf_op jit(solution)/shard_map/ppermute | solution.py:100
  14.3 2.5 %collective-permute-start.2 = (bf16[576,128]{1,0:T(8,128)(2,1)}, bf16[576,128]{1,0:T(8,128)(2,1)S(1)}, u32[]{:S(2)}, u32[]{:S(2)}) collective-permute-start(bf16[576,128]{1,0:T(8,128)(2,1)} %bitcast.25), channel_id=1, source_target_pairs={{0,24},{8,0},{16,8},{24,16},{32,56},{40,32},{48,40},{56,48},{64,88... | collective-permute-start | bytes 442376 | tf_op jit(solution)/shard_map/ppermute | solution.py:92
  18.9 3.8 %collective-permute-done.4.refs_3_ = bf16[16,2432]{1,0:T(8,128)(2,1)S(1)} collective-permute-done((bf16[16,2432]{1,0:T(8,128)(2,1)S(1)}, bf16[16,2432]{1,0:T(8,128)(2,1)S(1)}, u32[]{:S(2)}, u32[]{:S(2)}) %collective-permute-start.4) | collective-permute-done | bytes 77856 | tf_op jit(solution)/shard_map/ppermute | solution.py:100
  23.8 3.3 %collective-permute-done.k1 = bf16[576,128]{1,0:T(8,128)(2,1)S(1)} collective-permute-done((bf16[576,128]{1,0:T(8,128)(2,1)}, bf16[576,128]{1,0:T(8,128)(2,1)S(1)}, u32[]{:S(2)}, u32[]{:S(2)}) %collective-permute-start) | collective-permute-done | bytes 147488 | tf_op jit(solution)/shard_map/ppermute | solution.py:92
  31.2 3.2 %shard_map.169.refs_1_ = bf16[32,1152]{1,0:T(8,128)(2,1)S(1)} custom-call(s32[8]{0:T(128)S(1)} %stack.31.refs_0_.info, bf16[16,2432]{1,0:T(8,128)(2,1)S(1)} %maximum_maximum_fusion.q_ref.refs_1_, bf16[16,2432]{1,0:T(8,128)(2,1)S(1)} %collective-permute-done.3.refs_2_, bf16[16,2432]{1,0:T(8,128)(2,1)S(1)} %collective-permute-done.4.refs_3_, ...), custom_call_target="tpu_custom_call" | custom-call | tf_op jit(solution)/shard_map/pallas_call | solution.py:54
  36.0 3.1 %shard_map.170 = (bf16[4,448,128]{2,1,0:T(8,128)(2,1)}, bf16[4,448,128]{2,1,0:T(8,128)(2,1)}, bf16[4,448,128]{2,1,0:T(8,128)(2,1)}, bf16[4,448,128]{2,1,0:T(8,128)(2,1)}) custom-call(s32[8]{0:T(128)S(1)} %stack.31.refs_0_.info, bf16[128,7168]{1,0:T(8,128)(2,1)S(1)} %bitcast.21), custom_call_target="tpu_custom_call" | custom-call | tf_op jit(solution)/shard_map/pallas_call | solution.py:372
  39.1 1.9 %collective-permute-done.8.refs_3_ = bf16[32,1152]{1,0:T(8,128)(2,1)S(1)} collective-permute-done((bf16[32,1152]{1,0:T(8,128)(2,1)S(1)}, bf16[32,1152]{1,0:T(8,128)(2,1)S(1)}, u32[]{:S(2)}, u32[]{:S(2)}) %collective-permute-start.8) | collective-permute-done | bytes 73760 | tf_op jit(solution)/shard_map/ppermute | solution.py:100
  41.0 2.5 %collective-permute-done.7.refs_2_ = bf16[32,1152]{1,0:T(8,128)(2,1)S(1)} collective-permute-done((bf16[32,1152]{1,0:T(8,128)(2,1)S(1)}, bf16[32,1152]{1,0:T(8,128)(2,1)S(1)}, u32[]{:S(2)}, u32[]{:S(2)}) %collective-permute-start.7) | collective-permute-done | bytes 73760 | tf_op jit(solution)/shard_map/ppermute | solution.py:100
  48.0 2.0 %collective-permute-done.11.refs_3_ = bf16[32,1024]{1,0:T(8,128)(2,1)S(1)} collective-permute-done((bf16[32,1024]{1,0:T(8,128)(2,1)S(1)}, bf16[32,1024]{1,0:T(8,128)(2,1)S(1)}, u32[]{:S(2)}, u32[]{:S(2)}) %collective-permute-start.11) | collective-permute-done | bytes 65568 | tf_op jit(solution)/shard_map/ppermute | solution.py:92
  53.2 7.5 %all-to-all-start = ((bf16[8,16,448]{2,1,0:T(8,128)(2,1)}), bf16[8,16,448]{2,1,0:T(8,128)(2,1)S(1)}, u32[]{:S(2)}, u32[]{:S(2)}) async-start(bf16[8,16,448]{2,1,0:T(8,128)(2,1)} %bitcast.11), calls=%async_computation | async-start | bytes 262144 | tf_op jit(solution)/shard_map/all_to_all | solution.py:557
  61.6 7.0 %all-to-all-done.refs_1_ = bf16[8,16,448]{2,1,0:T(8,128)(2,1)S(1)} async-done(((bf16[8,16,448]{2,1,0:T(8,128)(2,1)}), bf16[8,16,448]{2,1,0:T(8,128)(2,1)S(1)}, u32[]{:S(2)}, u32[]{:S(2)}) %all-to-all-start) | async-done | bytes 114720 | tf_op jit(solution)/shard_map/all_to_all | solution.py:557
  70.0 3.4 %all-to-all-start.1 = ((bf16[8,16,512]{2,1,0:T(8,128)(2,1)}), bf16[8,16,512]{2,1,0:T(8,128)(2,1)S(1)}, u32[]{:S(2)}, u32[]{:S(2)}) async-start(bf16[8,16,512]{2,1,0:T(8,128)(2,1)} %get-tuple-element.75), calls=%async_computation.1 | async-start | bytes 262144 | tf_op jit(solution)/shard_map/all_to_all | solution.py:568
  73.4 7.9 %all-to-all-done.1 = bf16[8,16,512]{2,1,0:T(8,128)(2,1)S(1)} async-done(((bf16[8,16,512]{2,1,0:T(8,128)(2,1)}), bf16[8,16,512]{2,1,0:T(8,128)(2,1)S(1)}, u32[]{:S(2)}, u32[]{:S(2)}) %all-to-all-start.1) | async-done | bytes 131104 | tf_op jit(solution)/shard_map/all_to_all | solution.py:568
  82.9 3.7 %all-to-all-start.2 = ((bf16[16,128,512]{2,1,0:T(8,128)(2,1)}), bf16[16,128,512]{2,1,0:T(8,128)(2,1)S(1)}, u32[]{:S(2)}, u32[]{:S(2)}) async-start(bf16[16,128,512]{2,1,0:T(8,128)(2,1)} %broadcast_in_dim.20), calls=%async_computation.2 | async-start | bytes 4194304 | tf_op jit(solution)/shard_map/all_to_all | solution.py:128
  86.7 17.0 %shard_map.174 = bf16[128,4096]{1,0:T(8,128)(2,1)} custom-call(s32[8]{0:T(128)S(1)} %stack.31.refs_0_.info, bf16[128,4608]{1,0:T(8,128)(2,1)} %bitcast.33, bf16[16,576,256]{2,1,0:T(8,128)(2,1)} %bitcast.32), custom_call_target="tpu_custom_call" | custom-call | flops 9126805504 | bytes 8388608 | tf_op jit(solution)/shard_map/pallas_call | solution.py:457
  103.7 7.7 %all-to-all-done.2.refs_1_ = bf16[16,128,512]{2,1,0:T(8,128)(2,1)S(1)} async-done(((bf16[16,128,512]{2,1,0:T(8,128)(2,1)}), bf16[16,128,512]{2,1,0:T(8,128)(2,1)S(1)}, u32[]{:S(2)}, u32[]{:S(2)}) %all-to-all-start.2) | async-done | bytes 2097184 | tf_op jit(solution)/shard_map/all_to_all | solution.py:128
  111.5 6.8 %collective-permute-start.15 = (bf16[16,128,512]{2,1,0:T(8,128)(2,1)S(1)}, bf16[16,128,512]{2,1,0:T(8,128)(2,1)S(1)}, u32[]{:S(2)}, u32[]{:S(2)}) collective-permute-start(bf16[16,128,512]{2,1,0:T(8,128)(2,1)S(1)} %all-to-all-done.2.refs_1_), channel_id=1, source_target_pairs={{0,128},{128,0},{1,129},{129,1},{2,130},{130,2},{3,131},{131,3},{4... | collective-permute-start | bytes 6291464 | tf_op jit(solution)/shard_map/ppermute | solution.py:124
  118.2 2.0 %copy-done = bf16[1,2,7168,128]{3,2,1,0:T(8,128)(2,1)S(1)} copy-done((bf16[1,2,7168,128]{3,2,1,0:T(8,128)(2,1)S(1)}, bf16[1,2,7168,128]{3,2,1,0:T(8,128)(2,1)}, u32[]{:S(2)}) %copy-start) | copy-done | bytes 3670040
  123.7 2.1 %collective-permute-start.18 = (bf16[192,128]{1,0:T(8,128)(2,1)S(1)}, bf16[192,128]{1,0:T(8,128)(2,1)S(1)}, u32[]{:S(2)}, u32[]{:S(2)}) collective-permute-start(bf16[192,128]{1,0:T(8,128)(2,1)S(1)} %get-tuple-element.89.refs_1_), channel_id=1, source_target_pairs={{0,40},{8,32},{16,56},{24,48},{32,8},{40,0},{48,24},{56,16},{64,10... | collective-permute-start | bytes 147464 | tf_op jit(solution)/shard_map/ppermute | solution.py:112
  126.5 4.8 %collective-permute-done.19.refs_8_ = bf16[4,448,128]{2,1,0:T(8,128)(2,1)S(1)} collective-permute-done((bf16[4,448,128]{2,1,0:T(8,128)(2,1)S(1)}, bf16[4,448,128]{2,1,0:T(8,128)(2,1)S(1)}, u32[]{:S(2)}, u32[]{:S(2)}) %collective-permute-start.19) | collective-permute-done | bytes 458784 | tf_op jit(solution)/shard_map/ppermute | solution.py:112
  133.7 2.6 %shard_map.177 = (f32[4,128,448]{2,1,0:T(8,128)S(1)}, bf16[4,128,448]{2,1,0:T(8,128)(2,1)S(1)}) custom-call(s32[8]{0:T(128)S(1)} %stack.31.refs_0_.info, bf16[192,128]{1,0:T(8,128)(2,1)S(1)} %get-tuple-element.89.refs_1_, bf16[192,128]{1,0:T(8,128)(2,1)S(1)} %collective-permute-done.16.refs_2_, bf16[192,128]{1,0:T(8,128)(2,1)S(1)} %collective-permute-done.17.refs_3_, ...), custom_call_target="tpu_custom_call" | custom-call | tf_op jit(solution)/shard_map/pallas_call | solution.py:54
  138.8 13.0 %all_to_all.25 = bf16[4,128,448]{1,2,0:T(8,128)(2,1)S(1)} all-to-all(bf16[4,128,448]{1,2,0:T(8,128)(2,1)S(1)} %copy.28), channel_id=1, replica_groups={{0,16,64,80},{8,24,72,88},{32,48,96,112},{40,56,104,120},{1,17,65,81},{..., dimensions={0} | all-to-all | bytes 917504 | tf_op jit(solution)/shard_map/all_to_all | solution.py:586
  152.0 10.4 %all_to_all.26 = bf16[8,16,448]{2,1,0:T(8,128)(2,1)S(1)} all-to-all(bf16[8,16,448]{2,1,0:T(8,128)(2,1)S(1)} %bitcast.30), channel_id=1, replica_groups=mesh['group'=2,'seq'=16,'expert'=8] {'expert'}, dimensions={0} | all-to-all | bytes 229376 | tf_op jit(solution)/shard_map/all_to_all | solution.py:588
  (76 shorter events, 31.3 us)
Async XLA Ops:
  7.2 79.5 %all-gather.3.cloned.1.call-start = ((), (), s32[]{:S(2)}) async-start(), calls=%async_computation.5 | async-start | bytes 5013504 | tf_op jit(solution)/shard_map/all_gather | solution.py:524
  10.6 7.6 %collective-permute-start.5 = (bf16[16,2432]{1,0:T(8,128)(2,1)S(1)}, bf16[16,2432]{1,0:T(8,128)(2,1)S(1)}, u32[]{:S(2)}, u32[]{:S(2)}) collective-permute-start(bf16[16,2432]{1,0:T(8,128)(2,1)S(1)} %maximum_maximum_fusion.q_ref.refs_1_), channel_id=1, source_target_pairs={{0,96},{8,104},{16,112},{24,120},{32,0},{40,8},{48,16},{56,24},{64... | collective-permute-start | bytes 233480 | tf_op jit(solution)/shard_map/ppermute | solution.py:100
  14.3 9.5 %collective-permute-start.2 = (bf16[576,128]{1,0:T(8,128)(2,1)}, bf16[576,128]{1,0:T(8,128)(2,1)S(1)}, u32[]{:S(2)}, u32[]{:S(2)}) collective-permute-start(bf16[576,128]{1,0:T(8,128)(2,1)} %bitcast.25), channel_id=1, source_target_pairs={{0,24},{8,0},{16,8},{24,16},{32,56},{40,32},{48,40},{56,48},{64,88... | collective-permute-start | bytes 442376 | tf_op jit(solution)/shard_map/ppermute | solution.py:92
  16.7 7.0 %collective-permute-start.1 = (bf16[576,128]{1,0:T(8,128)(2,1)}, bf16[576,128]{1,0:T(8,128)(2,1)S(1)}, u32[]{:S(2)}, u32[]{:S(2)}) collective-permute-start(bf16[576,128]{1,0:T(8,128)(2,1)} %bitcast.26), channel_id=1, source_target_pairs={{0,16},{8,24},{16,0},{24,8},{32,48},{40,56},{48,32},{56,40},{64,80... | collective-permute-start | bytes 442376 | tf_op jit(solution)/shard_map/ppermute | solution.py:92
  17.3 9.8 %collective-permute-start = (bf16[576,128]{1,0:T(8,128)(2,1)}, bf16[576,128]{1,0:T(8,128)(2,1)S(1)}, u32[]{:S(2)}, u32[]{:S(2)}) collective-permute-start(bf16[576,128]{1,0:T(8,128)(2,1)} %bitcast.27), channel_id=1, source_target_pairs={{0,8},{8,16},{16,24},{24,0},{32,40},{40,48},{48,56},{56,32},{64,72... | collective-permute-start | bytes 442376 | tf_op jit(solution)/shard_map/ppermute | solution.py:92
  17.9 4.8 %collective-permute-start.4 = (bf16[16,2432]{1,0:T(8,128)(2,1)S(1)}, bf16[16,2432]{1,0:T(8,128)(2,1)S(1)}, u32[]{:S(2)}, u32[]{:S(2)}) collective-permute-start(bf16[16,2432]{1,0:T(8,128)(2,1)S(1)} %maximum_maximum_fusion.q_ref.refs_1_), channel_id=1, source_target_pairs={{0,64},{8,72},{16,80},{24,88},{32,96},{40,104},{48,112},{56,120},{... | collective-permute-start | bytes 233480 | tf_op jit(solution)/shard_map/ppermute | solution.py:100
  18.2 5.5 %collective-permute-start.3 = (bf16[16,2432]{1,0:T(8,128)(2,1)S(1)}, bf16[16,2432]{1,0:T(8,128)(2,1)S(1)}, u32[]{:S(2)}, u32[]{:S(2)}) collective-permute-start(bf16[16,2432]{1,0:T(8,128)(2,1)S(1)} %maximum_maximum_fusion.q_ref.refs_1_), channel_id=1, source_target_pairs={{0,32},{8,40},{16,48},{24,56},{32,64},{40,72},{48,80},{56,88},{64,... | collective-permute-start | bytes 233480 | tf_op jit(solution)/shard_map/ppermute | solution.py:100
  28.0 3.2 %collective-permute-start.6 = (bf16[4,576,128]{2,1,0:T(8,128)(2,1)S(1)}, bf16[4,576,128]{2,1,0:T(8,128)(2,1)S(1)}, u32[]{:S(2)}, u32[]{:S(2)}) collective-permute-start(bf16[4,576,128]{2,1,0:T(8,128)(2,1)S(1)} %shard_map.167.refs_5_), channel_id=1, source_target_pairs={{0,128},{128,0},{1,129},{129,1},{2,130},{130,2},{3,131},{131,3},{4... | collective-permute-start | bytes 1769480 | tf_op jit(solution)/shard_map/ppermute | solution.py:124
  34.5 4.7 %collective-permute-start.9 = (bf16[32,1152]{1,0:T(8,128)(2,1)S(1)}, bf16[32,1152]{1,0:T(8,128)(2,1)S(1)}, u32[]{:S(2)}, u32[]{:S(2)}) collective-permute-start(bf16[32,1152]{1,0:T(8,128)(2,1)S(1)} %shard_map.169.refs_1_), channel_id=1, source_target_pairs={{0,96},{8,104},{16,112},{24,120},{32,0},{40,8},{48,16},{56,24},{64... | collective-permute-start | bytes 221192 | tf_op jit(solution)/shard_map/ppermute | solution.py:100
  35.0 6.0 %collective-permute-start.8 = (bf16[32,1152]{1,0:T(8,128)(2,1)S(1)}, bf16[32,1152]{1,0:T(8,128)(2,1)S(1)}, u32[]{:S(2)}, u32[]{:S(2)}) collective-permute-start(bf16[32,1152]{1,0:T(8,128)(2,1)S(1)} %shard_map.169.refs_1_), channel_id=1, source_target_pairs={{0,64},{8,72},{16,80},{24,88},{32,96},{40,104},{48,112},{56,120},{... | collective-permute-start | bytes 221192 | tf_op jit(solution)/shard_map/ppermute | solution.py:100
  35.0 8.5 %collective-permute-start.7 = (bf16[32,1152]{1,0:T(8,128)(2,1)S(1)}, bf16[32,1152]{1,0:T(8,128)(2,1)S(1)}, u32[]{:S(2)}, u32[]{:S(2)}) collective-permute-start(bf16[32,1152]{1,0:T(8,128)(2,1)S(1)} %shard_map.169.refs_1_), channel_id=1, source_target_pairs={{0,32},{8,40},{16,48},{24,56},{32,64},{40,72},{48,80},{56,88},{64,... | collective-permute-start | bytes 221192 | tf_op jit(solution)/shard_map/ppermute | solution.py:100
  44.4 3.6 %collective-permute-start.12 = (bf16[32,1024]{1,0:T(8,128)(2,1)S(1)}, bf16[32,1024]{1,0:T(8,128)(2,1)S(1)}, u32[]{:S(2)}, u32[]{:S(2)}) collective-permute-start(bf16[32,1024]{1,0:T(8,128)(2,1)S(1)} %shard_map.171.refs_1_), channel_id=1, source_target_pairs={{0,24},{8,0},{16,8},{24,16},{32,56},{40,32},{48,40},{56,48},{64,88... | collective-permute-start | bytes 196616 | tf_op jit(solution)/shard_map/ppermute | solution.py:92
  45.4 4.6 %collective-permute-start.11 = (bf16[32,1024]{1,0:T(8,128)(2,1)S(1)}, bf16[32,1024]{1,0:T(8,128)(2,1)S(1)}, u32[]{:S(2)}, u32[]{:S(2)}) collective-permute-start(bf16[32,1024]{1,0:T(8,128)(2,1)S(1)} %shard_map.171.refs_1_), channel_id=1, source_target_pairs={{0,16},{8,24},{16,0},{24,8},{32,48},{40,56},{48,32},{56,40},{64,80... | collective-permute-start | bytes 196616 | tf_op jit(solution)/shard_map/ppermute | solution.py:92
  46.3 5.2 %collective-permute-start.10 = (bf16[32,1024]{1,0:T(8,128)(2,1)S(1)}, bf16[32,1024]{1,0:T(8,128)(2,1)S(1)}, u32[]{:S(2)}, u32[]{:S(2)}) collective-permute-start(bf16[32,1024]{1,0:T(8,128)(2,1)S(1)} %shard_map.171.refs_1_), channel_id=1, source_target_pairs={{0,8},{8,16},{16,24},{24,0},{32,40},{40,48},{48,56},{56,32},{64,72... | collective-permute-start | bytes 196616 | tf_op jit(solution)/shard_map/ppermute | solution.py:92
  46.3 27.1 %collective-permute-start.13 = (bf16[4,448,128]{2,1,0:T(8,128)(2,1)}, bf16[4,448,128]{2,1,0:T(8,128)(2,1)S(1)}, u32[]{:S(2)}, u32[]{:S(2)}) collective-permute-start(bf16[4,448,128]{2,1,0:T(8,128)(2,1)} %get-tuple-element.77), channel_id=1, source_target_pairs={{0,8},{8,0},{16,24},{24,16},{32,40},{40,32},{48,56},{56,48},{64,72... | collective-permute-start | bytes 1376264 | tf_op jit(solution)/shard_map/ppermute | solution.py:112
  48.0 25.4 %collective-permute-start.14 = (bf16[4,448,128]{2,1,0:T(8,128)(2,1)}, bf16[4,448,128]{2,1,0:T(8,128)(2,1)S(1)}, u32[]{:S(2)}, u32[]{:S(2)}) collective-permute-start(bf16[4,448,128]{2,1,0:T(8,128)(2,1)} %get-tuple-element.78), channel_id=1, source_target_pairs={{0,32},{8,40},{16,48},{24,56},{32,0},{40,8},{48,16},{56,24},{64,96... | collective-permute-start | bytes 1376264 | tf_op jit(solution)/shard_map/ppermute | solution.py:112
  53.2 15.5 %all-to-all-start = ((bf16[8,16,448]{2,1,0:T(8,128)(2,1)}), bf16[8,16,448]{2,1,0:T(8,128)(2,1)S(1)}, u32[]{:S(2)}, u32[]{:S(2)}) async-start(bf16[8,16,448]{2,1,0:T(8,128)(2,1)} %bitcast.11), calls=%async_computation | async-start | bytes 262144 | tf_op jit(solution)/shard_map/all_to_all | solution.py:557
  70.0 11.3 %all-to-all-start.1 = ((bf16[8,16,512]{2,1,0:T(8,128)(2,1)}), bf16[8,16,512]{2,1,0:T(8,128)(2,1)S(1)}, u32[]{:S(2)}, u32[]{:S(2)}) async-start(bf16[8,16,512]{2,1,0:T(8,128)(2,1)} %get-tuple-element.75), calls=%async_computation.1 | async-start | bytes 262144 | tf_op jit(solution)/shard_map/all_to_all | solution.py:568
  82.9 28.5 %all-to-all-start.2 = ((bf16[16,128,512]{2,1,0:T(8,128)(2,1)}), bf16[16,128,512]{2,1,0:T(8,128)(2,1)S(1)}, u32[]{:S(2)}, u32[]{:S(2)}) async-start(bf16[16,128,512]{2,1,0:T(8,128)(2,1)} %broadcast_in_dim.20), calls=%async_computation.2 | async-start | bytes 4194304 | tf_op jit(solution)/shard_map/all_to_all | solution.py:128
  111.5 10.6 %collective-permute-start.15 = (bf16[16,128,512]{2,1,0:T(8,128)(2,1)S(1)}, bf16[16,128,512]{2,1,0:T(8,128)(2,1)S(1)}, u32[]{:S(2)}, u32[]{:S(2)}) collective-permute-start(bf16[16,128,512]{2,1,0:T(8,128)(2,1)S(1)} %all-to-all-done.2.refs_1_), channel_id=1, source_target_pairs={{0,128},{128,0},{1,129},{129,1},{2,130},{130,2},{3,131},{131,3},{4... | collective-permute-start | bytes 6291464 | tf_op jit(solution)/shard_map/ppermute | solution.py:124
  118.2 13.1 %collective-permute-start.19 = (bf16[4,448,128]{2,1,0:T(8,128)(2,1)S(1)}, bf16[4,448,128]{2,1,0:T(8,128)(2,1)S(1)}, u32[]{:S(2)}, u32[]{:S(2)}) collective-permute-start(bf16[4,448,128]{2,1,0:T(8,128)(2,1)S(1)} %copy-done.9), channel_id=1, source_target_pairs={{0,40},{8,32},{16,56},{24,48},{32,8},{40,0},{48,24},{56,16},{64,10... | collective-permute-start | bytes 1376264 | tf_op jit(solution)/shard_map/ppermute | solution.py:112
  123.7 8.6 %collective-permute-start.18 = (bf16[192,128]{1,0:T(8,128)(2,1)S(1)}, bf16[192,128]{1,0:T(8,128)(2,1)S(1)}, u32[]{:S(2)}, u32[]{:S(2)}) collective-permute-start(bf16[192,128]{1,0:T(8,128)(2,1)S(1)} %get-tuple-element.89.refs_1_), channel_id=1, source_target_pairs={{0,40},{8,32},{16,56},{24,48},{32,8},{40,0},{48,24},{56,16},{64,10... | collective-permute-start | bytes 147464 | tf_op jit(solution)/shard_map/ppermute | solution.py:112
  125.8 7.8 %collective-permute-start.17 = (bf16[192,128]{1,0:T(8,128)(2,1)S(1)}, bf16[192,128]{1,0:T(8,128)(2,1)S(1)}, u32[]{:S(2)}, u32[]{:S(2)}) collective-permute-start(bf16[192,128]{1,0:T(8,128)(2,1)S(1)} %get-tuple-element.89.refs_1_), channel_id=1, source_target_pairs={{0,32},{8,40},{16,48},{24,56},{32,0},{40,8},{48,16},{56,24},{64,96... | collective-permute-start | bytes 147464 | tf_op jit(solution)/shard_map/ppermute | solution.py:112
  125.8 7.8 %collective-permute-start.16 = (bf16[192,128]{1,0:T(8,128)(2,1)S(1)}, bf16[192,128]{1,0:T(8,128)(2,1)S(1)}, u32[]{:S(2)}, u32[]{:S(2)}) collective-permute-start(bf16[192,128]{1,0:T(8,128)(2,1)S(1)} %get-tuple-element.89.refs_1_), channel_id=1, source_target_pairs={{0,8},{8,0},{16,24},{24,16},{32,40},{40,32},{48,56},{56,48},{64,72... | collective-permute-start | bytes 147464 | tf_op jit(solution)/shard_map/ppermute | solution.py:112
  (11 other events, 205.9 us)
Sparse Core Ops, SparseCore 0:
  10.7 69.3 all-gather.2
